TPU v7x, 128 devices: a whole 4x4x4 slice. The times are simulated.
128 devices in a mesh: section: 2 (over core), seq: 2 (over x_lo), fsdp: 32 (over x_hi, y, z).
Axes of the slice: x: 4 (x_hi: 2, x_lo: 2; x = x_hi * 2 + x_lo), y: 4, z: 4, core: 2. Of those that a mesh axis runs over, the one named last changes fastest.
Arguments:
- inputs: bfloat16 [2, 4096, 1536], P(None, ('seq', 'fsdp')), may hold values from -6 to 6
- cotangent: bfloat16 [2, 4096, 1536], P(None, ('seq', 'fsdp')), may hold values from -6 to 6
- w_in: bfloat16 [2, 1536, 4608], P('section', 'fsdp'), may hold values from -0.15625 to 0.15625
- w_out: bfloat16 [2, 1536, 1536], P('section', 'fsdp'), may hold values from -0.15625 to 0.15625
- w_gate: bfloat16 [2, 1536, 6912], P('section', 'fsdp'), may hold values from -0.15625 to 0.15625
- w_up: bfloat16 [2, 1536, 6912], P('section', 'fsdp'), may hold values from -0.15625 to 0.15625
- w_down: bfloat16 [2, 6912, 1536], P('section', 'fsdp'), may hold values from -0.078125 to 0.078125
- kernel: bfloat16 [2, 3, 1536], P('section', None, 'fsdp'), may hold values from -3.5 to 3.5
- gain_mix: bfloat16 [2, 1536], P('section', 'fsdp'), may hold values from 0.5 to 1.5
- gain_ffn: bfloat16 [2, 1536], P('section', 'fsdp'), may hold values from 0.5 to 1.5
Outputs:
- layer_outputs: bfloat16 [2, 2, 4096, 1536], P('section', None, ('seq', 'fsdp'))
- input_grads: float32 [2, 2, 4096, 1536], P('section', None, ('seq', 'fsdp'))
- grad_w_in: float32 [2, 1536, 4608], P('section', 'fsdp')
- grad_w_out: float32 [2, 1536, 1536], P('section', 'fsdp')
- grad_w_gate: float32 [2, 1536, 6912], P('section', 'fsdp')
- grad_w_up: float32 [2, 1536, 6912], P('section', 'fsdp')
- grad_w_down: float32 [2, 6912, 1536], P('section', 'fsdp')
- grad_kernel: float32 [2, 3, 1536], P('section', None, 'fsdp')
- grad_gain_mix: float32 [2, 1536], P('section', 'fsdp')
- grad_gain_ffn: float32 [2, 1536], P('section', 'fsdp')
All inputs are finite; a program needn't handle non-finite values.
Results may differ from a plain program's by a relative error of at most 0.03.
Values may be sent and summed in bfloat16 or wider, within the bound.
A program may use at most 320 MiB of HBM per device.

v0:
```python
import jax
import jax.numpy as jnp
from jax import lax
from jax.sharding import PartitionSpec as P

epsilon = 1e-06


def from_behind(value, axis, steps):
    count = lax.axis_size(axis)
    first, last = (max(0, -steps), min(count, count - steps))
    return lax.ppermute(value, axis, [(source, source + steps) for source in range(first, last)])


def guarded(active, compute, operands):

    def silent(values):
        return jax.tree.map(jnp.zeros_like, compute(values))

    return lax.cond(active, compute, silent, operands)


def contract_last(left_side, right_side):
    return lax.dot_general(
        left_side, right_side, (((1,), (1,)), ((), ())), preferred_element_type=jnp.float32
    )


def contract_rows(left_side, right_side):
    return lax.dot_general(
        left_side, right_side, (((0,), (0,)), ((), ())), preferred_element_type=jnp.float32
    )


def norm_forward(values, gain_vector):
    inverse = lax.rsqrt(jnp.mean(values * values, axis=-1, keepdims=True) + epsilon)
    return (inverse, values * inverse * gain_vector)


def norm_backward(values, inverse, gain_vector, grad_normed):
    weighted = grad_normed * gain_vector
    mean_term = jnp.mean(weighted * values, axis=-1, keepdims=True)
    grad_values = inverse * weighted - values * (inverse * inverse * inverse) * mean_term
    grad_gain = jnp.sum(grad_normed * values * inverse, axis=0)
    return (grad_values, grad_gain)


def mixer_front(operands):
    block_in, weights = operands
    feature_count = block_in.shape[1]
    inverse_mix, normed = norm_forward(block_in, weights[6].astype(jnp.float32))
    normed_low = normed.astype(jnp.bfloat16)
    projected = jnp.dot(normed_low, weights[0], preferred_element_type=jnp.float32)
    gated_in = projected[:, :feature_count] * projected[:, 2 * feature_count :]
    return (inverse_mix, normed_low, projected, gated_in)


def mixer_rest(operands):
    block_in, weights, projected, gated_in, border = operands
    token_rows, feature_count = block_in.shape
    kernel_full = weights[5].astype(jnp.float32)
    taps_count = kernel_full.shape[0]
    extended = jnp.concatenate([border, gated_in], axis=0)
    convolved = jnp.zeros_like(gated_in)
    for offset in range(taps_count):
        first_row = taps_count - 1 - offset
        convolved = convolved + kernel_full[offset] * extended[first_row : first_row + token_rows]
    c_part = projected[:, feature_count : 2 * feature_count]
    mixed_low = (c_part * convolved).astype(jnp.bfloat16)
    middle = block_in + jnp.dot(mixed_low, weights[1], preferred_element_type=jnp.float32)
    inverse_ffn, normed_ffn = norm_forward(middle, weights[7].astype(jnp.float32))
    normed_ffn_low = normed_ffn.astype(jnp.bfloat16)
    gating = jnp.dot(normed_ffn_low, weights[2], preferred_element_type=jnp.float32)
    up_proj = jnp.dot(normed_ffn_low, weights[3], preferred_element_type=jnp.float32)
    hidden = (jax.nn.silu(gating) * up_proj).astype(jnp.bfloat16)
    result = middle + jnp.dot(hidden, weights[4], preferred_element_type=jnp.float32)
    return (
        extended,
        convolved,
        mixed_low,
        middle,
        inverse_ffn,
        normed_ffn_low,
        gating,
        up_proj,
        hidden,
        result,
    )


def back_front(operands):
    grad_out, weights, block_in, front_part, rest_part = operands
    (
        extended,
        convolved,
        mixed_low,
        middle,
        inverse_ffn,
        normed_ffn_low,
        gating,
        up_proj,
        hidden,
        result,
    ) = rest_part
    projected = front_part[2]
    feature_count = block_in.shape[1]
    grad_low = grad_out.astype(jnp.bfloat16)
    grad_hidden = contract_last(grad_low, weights[4])
    sigmoid_gate = jax.nn.sigmoid(gating)
    grad_gating = (
        grad_hidden * up_proj * sigmoid_gate * (1.0 + gating * (1.0 - sigmoid_gate))
    ).astype(jnp.bfloat16)
    grad_up = (grad_hidden * gating * sigmoid_gate).astype(jnp.bfloat16)
    grad_normed_ffn = contract_last(grad_gating, weights[2]) + contract_last(grad_up, weights[3])
    grad_middle_part, grad_gain_ffn = norm_backward(
        middle, inverse_ffn, weights[7].astype(jnp.float32), grad_normed_ffn
    )
    grad_middle = grad_out + grad_middle_part
    grad_branch = grad_middle.astype(jnp.bfloat16)
    grad_mixed = contract_last(grad_branch, weights[1])
    grad_c = grad_mixed * convolved
    grad_conv = grad_mixed * projected[:, feature_count : 2 * feature_count]
    factors = (hidden, grad_low, grad_gating, grad_up, normed_ffn_low, mixed_low, grad_branch)
    return (grad_middle, grad_c, grad_conv, grad_gain_ffn, factors)


def back_rest(operands):
    head_part, weights, block_in, front_part, rest_part, border_back = operands
    grad_middle, grad_c, grad_conv, grad_gain_ffn, factors = head_part
    inverse_mix, normed_low, projected, gated_in = front_part
    extended = rest_part[0]
    token_rows, feature_count = block_in.shape
    kernel_full = weights[5].astype(jnp.float32)
    taps_count = kernel_full.shape[0]
    extended_grad = jnp.concatenate([grad_conv, border_back], axis=0)
    grad_gated = jnp.zeros_like(grad_conv)
    kernel_rows = []
    for offset in range(taps_count):
        grad_gated = grad_gated + kernel_full[offset] * extended_grad[offset : offset + token_rows]
        first_row = taps_count - 1 - offset
        kernel_rows.append(
            jnp.sum(grad_conv * extended[first_row : first_row + token_rows], axis=0)
        )
    grad_kernel = jnp.stack(kernel_rows)
    grad_proj = jnp.concatenate(
        [
            grad_gated * projected[:, 2 * feature_count :],
            grad_c,
            grad_gated * projected[:, :feature_count],
        ],
        axis=1,
    ).astype(jnp.bfloat16)
    grad_normed = contract_last(grad_proj, weights[0])
    grad_input_part, grad_gain_mix = norm_backward(
        block_in, inverse_mix, weights[6].astype(jnp.float32), grad_normed
    )
    grad_input = grad_middle + grad_input_part
    return (grad_input, grad_proj, grad_kernel, grad_gain_mix)


def weight_terms(factors):
    (
        hidden,
        grad_low,
        grad_gating,
        grad_up,
        normed_ffn_low,
        mixed_low,
        grad_branch,
        normed_low,
        grad_proj,
    ) = factors
    return (
        contract_rows(normed_low, grad_proj),
        contract_rows(mixed_low, grad_branch),
        contract_rows(normed_ffn_low, grad_gating),
        contract_rows(normed_ffn_low, grad_up),
        contract_rows(hidden, grad_low),
    )


def local(inputs, cotangent, w_in, w_out, w_gate, w_up, w_down, kernel, gain_mix, gain_ffn):
    section_index = lax.axis_index("section")
    batches = inputs.shape[0]
    token_rows = inputs.shape[1]
    taps_count = kernel.shape[1]
    weights = (
        lax.all_gather(w_in[0], "fsdp", axis=0, tiled=True),
        lax.all_gather(w_out[0], "fsdp", axis=0, tiled=True),
        lax.all_gather(w_gate[0], "fsdp", axis=0, tiled=True),
        lax.all_gather(w_up[0], "fsdp", axis=0, tiled=True),
        lax.all_gather(w_down[0], "fsdp", axis=0, tiled=True),
        lax.all_gather(kernel[0], "fsdp", axis=1, tiled=True),
        lax.all_gather(gain_mix[0], "fsdp", axis=0, tiled=True),
        lax.all_gather(gain_ffn[0], "fsdp", axis=0, tiled=True),
    )
    arriving = jnp.zeros(inputs.shape[1:], jnp.bfloat16)
    kept_acts = []
    produced = []
    for moment in range(batches + 1):
        own_input = inputs[min(moment, batches - 1)]
        block_in = jnp.where(section_index == 0, own_input, arriving).astype(jnp.float32)
        active = jnp.logical_or(
            jnp.logical_and(section_index == 0, moment < batches),
            jnp.logical_and(section_index == 1, moment >= 1),
        )
        front_part = guarded(active, mixer_front, (block_in, weights))
        border = from_behind(front_part[3][token_rows - taps_count + 1 :], ("seq", "fsdp"), 1)
        rest_part = guarded(
            active, mixer_rest, (block_in, weights, front_part[2], front_part[3], border)
        )
        result_low = rest_part[9].astype(jnp.bfloat16)
        arriving = from_behind(result_low, "section", 1)
        kept_acts.append((block_in, front_part, rest_part))
        produced.append(result_low)
    returning = jnp.zeros(inputs.shape[1:], jnp.bfloat16)
    shares = ()
    small_sums = ()
    factor_list = []
    input_list = []
    for moment in range(batches + 1):
        late_index = min(moment + 1, batches)
        early_index = max(moment - 1, 0)
        chosen = jax.tree.map(
            lambda later_value, earlier_value: jnp.where(
                section_index == 1, later_value, earlier_value
            ),
            kept_acts[late_index],
            kept_acts[early_index],
        )
        block_in, front_part, rest_part = chosen
        own_cotangent = cotangent[min(moment, batches - 1)]
        grad_out = jnp.where(section_index == 1, own_cotangent, returning).astype(jnp.float32)
        active = jnp.logical_or(
            jnp.logical_and(section_index == 1, moment < batches),
            jnp.logical_and(section_index == 0, moment >= 1),
        )
        head_part = guarded(
            active, back_front, (grad_out, weights, block_in, front_part, rest_part)
        )
        border_back = from_behind(head_part[2][: taps_count - 1], ("seq", "fsdp"), -1)
        grad_input, grad_proj, grad_kernel, grad_gain_mix = guarded(
            active, back_rest, (head_part, weights, block_in, front_part, rest_part, border_back)
        )
        returning = from_behind(grad_input.astype(jnp.bfloat16), "section", -1)
        input_list.append(grad_input)
        factors = tuple(head_part[4]) + (front_part[1], grad_proj)
        small = (grad_kernel, grad_gain_mix, head_part[3])
        factor_list.append(factors)
        if moment == 0:
            small_sums = small
        else:
            small_sums = tuple((total + piece for total, piece in zip(small_sums, small)))
    picked = [
        jax.tree.map(
            lambda first_value, second_value: jnp.where(
                section_index == 1, first_value, second_value
            ),
            factor_list[position],
            factor_list[position + 1],
        )
        for position in range(batches)
    ]
    joined = tuple(
        (
            jnp.concatenate([entry[slot] for entry in picked], axis=0)
            for slot in range(len(picked[0]))
        )
    )
    big = weight_terms(joined)
    shares = (
        lax.psum_scatter(
            big[0].astype(jnp.bfloat16), "fsdp", scatter_dimension=0, tiled=True
        ).astype(jnp.float32),
        lax.psum_scatter(
            big[1].astype(jnp.bfloat16), "fsdp", scatter_dimension=0, tiled=True
        ).astype(jnp.float32),
        lax.psum_scatter(
            big[2].astype(jnp.bfloat16), "fsdp", scatter_dimension=0, tiled=True
        ).astype(jnp.float32),
        lax.psum_scatter(
            big[3].astype(jnp.bfloat16), "fsdp", scatter_dimension=0, tiled=True
        ).astype(jnp.float32),
        lax.psum_scatter(
            big[4].astype(jnp.bfloat16), "fsdp", scatter_dimension=0, tiled=True
        ).astype(jnp.float32),
        lax.psum_scatter(
            small_sums[0].astype(jnp.bfloat16), "fsdp", scatter_dimension=1, tiled=True
        ).astype(jnp.float32),
        lax.psum_scatter(
            small_sums[1].astype(jnp.bfloat16), "fsdp", scatter_dimension=0, tiled=True
        ).astype(jnp.float32),
        lax.psum_scatter(
            small_sums[2].astype(jnp.bfloat16), "fsdp", scatter_dimension=0, tiled=True
        ).astype(jnp.float32),
    )
    totals = (
        lax.psum(shares[0].astype(jnp.bfloat16), "seq").astype(jnp.float32),
        lax.psum(shares[1].astype(jnp.bfloat16), "seq").astype(jnp.float32),
        lax.psum(shares[2].astype(jnp.bfloat16), "seq").astype(jnp.float32),
        lax.psum(shares[3].astype(jnp.bfloat16), "seq").astype(jnp.float32),
        lax.psum(shares[4].astype(jnp.bfloat16), "seq").astype(jnp.float32),
        lax.psum(shares[5].astype(jnp.bfloat16), "seq").astype(jnp.float32),
        lax.psum(shares[6].astype(jnp.bfloat16), "seq").astype(jnp.float32),
        lax.psum(shares[7].astype(jnp.bfloat16), "seq").astype(jnp.float32),
    )
    layer_outputs = jnp.stack(
        [
            jnp.where(section_index == 0, produced[position], produced[position + 1])
            for position in range(batches)
        ]
    )[None]
    input_grads = jnp.stack(
        [
            jnp.where(section_index == 1, input_list[position], input_list[position + 1])
            for position in range(batches)
        ]
    )[None]
    return (
        layer_outputs,
        input_grads,
        totals[0][None],
        totals[1][None],
        totals[2][None],
        totals[3][None],
        totals[4][None],
        totals[5][None],
        totals[6][None],
        totals[7][None],
    )


def solution(mesh):
    placed = (
        P(None, ("seq", "fsdp"), None),
        P(None, ("seq", "fsdp"), None),
        P("section", "fsdp", None),
        P("section", "fsdp", None),
        P("section", "fsdp", None),
        P("section", "fsdp", None),
        P("section", "fsdp", None),
        P("section", None, "fsdp"),
        P("section", "fsdp"),
        P("section", "fsdp"),
    )
    return jax.shard_map(
        local,
        mesh=mesh,
        in_specs=placed,
        out_specs=(
            P("section", None, ("seq", "fsdp"), None),
            P("section", None, ("seq", "fsdp"), None),
            P("section", "fsdp", None),
            P("section", "fsdp", None),
            P("section", "fsdp", None),
            P("section", "fsdp", None),
            P("section", "fsdp", None),
            P("section", None, "fsdp"),
            P("section", "fsdp"),
            P("section", "fsdp"),
        ),
        check_vma=False,
    )
```

profile of v0, /device:TPU:2, one launch (start us, length us, event | category | flops | bytes accessed | tf_op | source)
XLA Modules:
  0.0 2859.6 jit_solution(15636956946458673056)
XLA Ops:
  12.4 100.0 %all-reduce.5 = (bf16[1536]{0:T(1024)(128)(2,1)S(1)}, bf16[1536]{0:T(1024)(128)(2,1)}) all-reduce(bf16[1536]{0:T(1024)(128)(2,1)S(1)} %dynamic-update-slice, bf16[1536]{0:T(1024)(128)(2,1)S(1)} %dynamic-update-slice.1), channel_id=2, replica_groups=mesh['section'=2,'seq'=2,'fsdp'=32] {'fsdp'}, use_global_device_ids=true, to_apply=%add | all-reduce | flops 3072 | bytes 12288 | tf_op jit(solution)/shard_map/all_gather | solution.py:194
  112.4 40.8 %all-gather.14.cloned.1.call-done = bf16[1,1536,4608]{2,1,0:T(8,128)(2,1)} async-done(((bf16[1,48,4608]{2,1,0:T(8,128)(2,1)}), bf16[1,1536,4608]{2,1,0:T(8,128)(2,1)}) %all-gather.14.cloned.1.call-update) | async-done | bytes 14155792 | tf_op jit(solution)/shard_map/all_gather | solution.py:188
  153.2 10.8 conditional.12
  154.1 8.7 fusion.95
  164.0 3.5 collective-permute-start
  167.6 95.6 %all-gather.2 = bf16[1,3,1536]{1,0,2:T(2,128)(2,1)S(1)} all-gather(bf16[1,3,48]{1,0,2:T(2,128)(2,1)S(1)} %copy.28), channel_id=4, replica_groups=mesh['section'=2,'seq'=2,'fsdp'=32] {'fsdp'}, dimensions={2}, use_global_device_ids=true | all-gather | bytes 9504 | tf_op jit(solution)/shard_map/all_gather | solution.py:193
  263.6 162.6 %all-gather.18.cloned.1.call-done = bf16[1,1536,6912]{2,1,0:T(8,128)(2,1)} async-done(((bf16[1,48,6912]{2,1,0:T(8,128)(2,1)}), bf16[1,1536,6912]{2,1,0:T(8,128)(2,1)}) %all-gather.18.cloned.1.call-update) | async-done | bytes 21233680 | tf_op jit(solution)/shard_map/all_gather | solution.py:190
  426.2 185.7 %all-gather.20.cloned.1.call-done = bf16[1,1536,6912]{2,1,0:T(8,128)(2,1)} async-done(((bf16[1,48,6912]{2,1,0:T(8,128)(2,1)}), bf16[1,1536,6912]{2,1,0:T(8,128)(2,1)}) %all-gather.20.cloned.1.call-update) | async-done | bytes 21233680 | tf_op jit(solution)/shard_map/all_gather | solution.py:191
  611.9 185.7 %all-gather.22.cloned.1.call-done = bf16[1,6912,1536]{2,1,0:T(8,128)(2,1)} async-done(((bf16[1,216,1536]{2,1,0:T(8,128)(2,1)}), bf16[1,6912,1536]{2,1,0:T(8,128)(2,1)}) %all-gather.22.cloned.1.call-update) | async-done | bytes 21233680 | tf_op jit(solution)/shard_map/all_gather | solution.py:192
  797.6 41.0 %conditional.13 = (f32[66,1536]{1,0:T(8,128)}, f32[64,1536]{1,0:T(8,128)}, bf16[64,1536]{1,0:T(8,128)(2,1)}, f32[64,1536]{1,0:T(8,128)}, f32[64,1]{0,1:T(1,128)}...) conditional(s32[]{:T(128)} %convert_element_type.258, ...), branch_computations={%region_3.4_spmd, %region_4.6_spmd} | conditional | flops 4383286272 | bytes 179443120 | solution.py:20
  800.4 4.2 multiply_reduce_fusion.9
  807.8 9.2 fusion.101
  817.0 3.9 copy-done
  820.9 5.9 multiply_convert_fusion.9
  826.8 11.9 fusion.7
  843.1 11.0 conditional.14
  844.2 8.7 fusion.96
  854.1 3.5 collective-permute-start.2
  857.6 6.3 collective-permute-done.2
  863.9 41.7 %conditional.15 = (f32[66,1536]{1,0:T(8,128)}, f32[64,1536]{1,0:T(8,128)}, bf16[64,1536]{1,0:T(8,128)(2,1)}, f32[64,1536]{1,0:T(8,128)}, f32[64,1]{0,1:T(1,128)}...) conditional(s32[]{:T(128)} %convert_element_type.261, ...), branch_computations={%region_9.10_spmd, %region_10.12_spmd} | conditional | flops 4383286272 | bytes 181016000 | solution.py:20
  866.7 4.3 multiply_reduce_fusion.10
  874.2 9.2 fusion.102
  883.4 3.9 copy-done.1
  887.3 6.5 multiply_convert_fusion.12
  893.8 11.9 fusion.15
  912.1 4.1 broadcast_select_fusion.20
  917.2 8.8 conditional.18
  928.7 3.7 collective-permute-done.5
  939.8 7.9 collective-permute-done.4
  947.7 6.8 conditional.17
  954.4 47.9 %collective-permute-done.6 = bf16[64,1536]{1,0:T(8,128)(2,1)} collective-permute-done((bf16[64,1536]{1,0:T(8,128)(2,1)}, bf16[64,1536]{1,0:T(8,128)(2,1)}, u32[]{:S(2)}, u32[]{:S(2)}) %collective-permute-start.6) | collective-permute-done | bytes 196640 | tf_op jit(solution)/shard_map/ppermute | solution.py:12
  1003.4 46.6 %conditional.20 = (f32[64,1536]{1,0:T(8,128)S(1)}, f32[64,1536]{1,0:T(8,128)S(1)}, f32[64,1536]{1,0:T(8,128)S(1)}, f32[1536]{0:T(1024)S(1)}, bf16[64,6912]{1,0:T...) conditional(s32[]{:T(128)} %convert_element_type.261, ...), branch_computations={%region_29.30_spmd, %region_30.33_spmd} | conditional | flops 4387995648 | bytes 108216432 | solution.py:20
  1006.9 13.1 multiply_convert_fusion.5
  1021.8 10.9 fusion.99
  1032.8 11.7 multiply_reduce_fusion.5
  1047.2 2.8 slice_multiply_fusion.4
  1050.0 6.4 collective-permute-start.7
  1057.8 13.4 conditional.21
  1061.5 9.6 multiply_reduce_fusion.14
  1072.6 47.7 %collective-permute-done.8 = bf16[64,1536]{1,0:T(8,128)(2,1)S(1)} collective-permute-done((bf16[64,1536]{1,0:T(8,128)(2,1)S(1)}, bf16[64,1536]{1,0:T(8,128)(2,1)S(1)}, u32[]{:S(2)}, u32[]{:S(2)}) %collective-permute-start.8) | collective-permute-done | bytes 196640 | tf_op jit(solution)/shard_map/ppermute | solution.py:12
  1121.4 46.2 %conditional.22 = (f32[64,1536]{1,0:T(8,128)}, f32[64,1536]{1,0:T(8,128)}, f32[64,1536]{1,0:T(8,128)}, f32[1536]{0:T(1024)S(1)}, bf16[64,6912]{1,0:T(8,128)(2,1)...) conditional(s32[]{:T(128)} %convert_element_type.258, ...), branch_computations={%region_40.41_spmd, %region_41.44_spmd} | conditional | flops 4387995648 | bytes 115243072 | solution.py:20
  1123.1 12.8 multiply_convert_fusion.7
  1135.9 3.0 select_n.331
  1138.9 10.9 fusion.100
  1149.9 11.1 multiply_reduce_fusion.7
  1163.8 3.8 slice_multiply_fusion.5
  1171.6 3.6 convolution_convert_fusion.4
  1176.2 6.4 collective-permute-start.9
  1184.5 16.6 conditional.23
  1190.1 9.6 multiply_reduce_fusion.16
  1203.2 7.1 convolution_convert_fusion.3
  1211.6 2.7 broadcast_select_fusion.13
  1214.3 10.2 convolution_convert_fusion
  1226.2 10.2 convolution_convert_fusion.2
  1237.7 10.2 convolution_convert_fusion.1
  1249.7 155.4 %reduce-scatter.11.cloned.1.call-done = bf16[48,1536]{1,0:T(8,128)(2,1)} async-done(((bf16[1536,1536]{1,0:T(8,128)(2,1)}), bf16[48,1536]{1,0:T(8,128)(2,1)}) %reduce-scatter.11.cloned.1.call-update) | async-done | bytes 147472 | tf_op jit(solution)/shard_map/reduce_scatter | solution.py:275
  1405.1 260.7 %reduce-scatter.9.cloned.1.call-done = bf16[48,4608]{1,0:T(8,128)(2,1)} async-done(((bf16[1536,4608]{1,0:T(8,128)(2,1)}), bf16[48,4608]{1,0:T(8,128)(2,1)}) %reduce-scatter.9.cloned.1.call-update) | async-done | bytes 442384 | tf_op jit(solution)/shard_map/reduce_scatter | solution.py:272
  1665.8 291.6 %reduce-scatter.17.cloned.1.call-done = bf16[216,1536]{1,0:T(8,128)(2,1)} async-done(((bf16[6912,1536]{1,0:T(8,128)(2,1)}), bf16[216,1536]{1,0:T(8,128)(2,1)}) %reduce-scatter.17.cloned.1.call-update) | async-done | bytes 663568 | tf_op jit(solution)/shard_map/reduce_scatter | solution.py:284
  1957.4 291.6 %reduce-scatter.13.cloned.1.call-done = bf16[48,6912]{1,0:T(8,128)(2,1)} async-done(((bf16[1536,6912]{1,0:T(8,128)(2,1)}), bf16[48,6912]{1,0:T(8,128)(2,1)}) %reduce-scatter.13.cloned.1.call-update) | async-done | bytes 663568 | tf_op jit(solution)/shard_map/reduce_scatter | solution.py:278
  2249.0 291.6 %reduce-scatter.15.cloned.1.call-done = bf16[48,6912]{1,0:T(8,128)(2,1)} async-done(((bf16[1536,6912]{1,0:T(8,128)(2,1)}), bf16[48,6912]{1,0:T(8,128)(2,1)}) %reduce-scatter.15.cloned.1.call-update) | async-done | bytes 663568 | tf_op jit(solution)/shard_map/reduce_scatter | solution.py:281
  2544.0 93.6 %all-reduce.4 = (bf16[1536]{0:T(1024)(128)(2,1)S(1)}, bf16[1536]{0:T(1024)(128)(2,1)S(1)}) all-reduce(bf16[1536]{0:T(1024)(128)(2,1)S(1)} %add_convert_fusion.2, bf16[1536]{0:T(1024)(128)(2,1)S(1)} %add_convert_fusion.1), channel_id=16, replica_groups=mesh['section'=2,'seq'=2,'fsdp'=32] {'fsdp'}, use_global_device_ids=true, to_apply=%region_63.64.clone | all-reduce | flops 3072 | bytes 12288
  2638.7 125.9 %reduce-scatter.19.cloned.1.call-done = bf16[48,3]{1,0:T(8,128)(2,1)} async-done(((bf16[1536,3]{1,0:T(8,128)(2,1)}), bf16[48,3]{1,0:T(8,128)(2,1)}) %reduce-scatter.19.cloned.1.call-update) | async-done | bytes 304
  2765.4 4.9 all-reduce.6
  2771.9 73.1 %all-reduce.10.cloned.1.call-done = (bf16[1,48,4608]{2,1,0:T(8,128)(2,1)}, bf16[1,48,1536]{2,1,0:T(8,128)(2,1)}, bf16[1,48,6912]{2,1,0:T(8,128)(2,1)}, bf16[1,48,6912]{2,1,0:T(8,128)(2,1)}, bf16[1,216,1536]{2,1,0:T(8,128)(2,1)}) async-done(((bf16[1,48,4608]{2,1,0:T(8,128)(2,1)}, bf16[1,48,1536]{2,1,0:T(8,128)(2,1)}, bf16[1,48,6912]{2,1,0:T(8,128)(2,1)}, bf16[1,48,6912]{2,1,0:T(8,128)(2,1)}, ...) | async-done | bytes 2580496 | tf_op jit(solution)/shard_map/psum | solution.py:298
  (356 shorter events, 116.4 us)
Async XLA Ops:
  7.2 105.2 %copy-start.47 = (bf16[2,64,1536]{2,1,0:T(8,128)(2,1)S(1)}, bf16[2,64,1536]{2,1,0:T(8,128)(2,1)}, u32[]{:S(2)}) copy-start(bf16[2,64,1536]{2,1,0:T(8,128)(2,1)} %param.34) | copy-start | bytes 1179652
  7.2 146.0 %all-gather.14.cloned.1.call-start = ((), (), s32[]{:S(2)}) async-start(), calls=%async_computation.11 | async-start | bytes 14598144 | tf_op jit(solution)/shard_map/all_gather | solution.py:188
  8.0 255.7 %all-gather.16.cloned.1.call-start = ((), (), s32[]{:S(2)}) async-start(), calls=%async_computation.12 | async-start | bytes 4866048 | tf_op jit(solution)/shard_map/all_gather | solution.py:189
  8.7 417.5 %all-gather.18.cloned.1.call-start = ((), (), s32[]{:S(2)}) async-start(), calls=%async_computation.13 | async-start | bytes 21897216 | tf_op jit(solution)/shard_map/all_gather | solution.py:190
  9.4 602.5 %all-gather.20.cloned.1.call-start = ((), (), s32[]{:S(2)}) async-start(), calls=%async_computation.14 | async-start | bytes 21897216 | tf_op jit(solution)/shard_map/all_gather | solution.py:191
  10.0 787.6 %all-gather.22.cloned.1.call-start = ((), (), s32[]{:S(2)}) async-start(), calls=%async_computation.15 | async-start | bytes 21897216 | tf_op jit(solution)/shard_map/all_gather | solution.py:192
  10.6 1394.5 %reduce-scatter.11.cloned.1.call-start = ((), (), s32[]{:S(2)}) async-start(), calls=%async_computation.7 | async-start | bytes 4866048 | tf_op jit(solution)/shard_map/reduce_scatter | solution.py:275
  112.4 685.2 %copy-start.13 = (f32[64,1536]{1,0:T(8,128)}, f32[64,1536]{1,0:T(8,128)S(1)}, u32[]{:S(2)}) copy-start(f32[64,1536]{1,0:T(8,128)S(1)} %bitcast_convert_fusion) | copy-start | bytes 1179652
  153.2 14.3 copy-start.87
  164.0 99.6 %collective-permute-start = (f32[2,1536]{1,0:T(2,128)S(1)}, f32[2,1536]{1,0:T(2,128)S(1)}, u32[]{:S(2)}, u32[]{:S(2)}) collective-permute-start(f32[2,1536]{1,0:T(2,128)S(1)} %slice.207), channel_id=1, source_target_pairs={{0,1},{1,2},{2,3},{3,4},{4,5},{5,6},{6,7},{7,8},{8,9},{9,10},{10,1... | collective-permute-start | bytes 36872 | tf_op jit(solution)/shard_map/ppermute | solution.py:12
  807.8 13.1 copy-start
  826.8 11.9 copy-start.4
  838.7 2.7 collective-permute-start.1
  854.1 9.8 copy-start.83
  854.1 9.8 collective-permute-start.2
  874.2 13.1 copy-start.1
  893.8 11.9 copy-start.6
  905.6 2.7 collective-permute-start.3
  926.8 5.6 collective-permute-start.5
  934.9 12.7 copy-start.36
  935.0 12.7 copy-start.60
  935.0 12.7 copy-start.71
  935.8 66.5 %collective-permute-start.6 = (bf16[64,1536]{1,0:T(8,128)(2,1)}, bf16[64,1536]{1,0:T(8,128)(2,1)}, u32[]{:S(2)}, u32[]{:S(2)}) collective-permute-start(bf16[64,1536]{1,0:T(8,128)(2,1)} %convert_element_type.267), channel_id=1, source_target_pairs={{64,0},{65,1},{66,2},{67,3},{68,4},{69,5},{70,6},{71,7},{72,8},{73... | collective-permute-start | bytes 589832 | tf_op jit(solution)/shard_map/ppermute | solution.py:12
  937.9 9.8 collective-permute-start.4
  954.4 48.9 %copy-start.53 = (bf16[64,1536]{1,0:T(8,128)(2,1)}, bf16[64,1536]{1,0:T(8,128)(2,1)S(1)}, u32[]{:S(2)}) copy-start(bf16[64,1536]{1,0:T(8,128)(2,1)S(1)} %get-tuple-element.834) | copy-start | bytes 589828
  954.4 48.9 %copy-start.25 = (f32[66,1536]{1,0:T(8,128)}, f32[66,1536]{1,0:T(8,128)S(1)}, u32[]{:S(2)}) copy-start(f32[66,1536]{1,0:T(8,128)S(1)} %get-tuple-element.871) | copy-start | bytes 1216516
  954.4 48.9 %copy-start.81 = (f32[64,1]{0,1:T(1,128)}, f32[64,1]{0,1:T(1,128)S(1)}, u32[]{:S(2)}) copy-start(f32[64,1]{0,1:T(1,128)S(1)} %get-tuple-element.860) | copy-start | bytes 772
  1021.8 11.0 copy-start.65
  1021.8 11.0 copy-start.76
  1032.8 14.4 slice-start.2
  1032.8 13.5 copy-start.35
  1032.8 13.5 copy-start.79
  1032.8 14.3 slice-start.3
  1050.0 7.9 copy-start.29
  1050.0 7.8 collective-permute-start.7
  1057.8 63.5 %copy-start.7 = (pred[64,6912]{1,0:T(32,128)(4,1)S(1)}, pred[64,6912]{1,0:T(32,128)(4,1)}, u32[]{:S(2)}) copy-start(pred[64,6912]{1,0:T(32,128)(4,1)} %select_n.391) | copy-start | bytes 1327108
  1057.8 63.5 %copy-start.59 = (bf16[1536]{0:T(1024)(128)(2,1)S(1)}, bf16[1536]{0:T(1024)(128)(2,1)}, u32[]{:S(2)}) copy-start(bf16[1536]{0:T(1024)(128)(2,1)} %get-tuple-element.1063) | copy-start | bytes 9220
  1061.5 9.6 copy-start.44
  1071.3 50.1 %copy-start.38 = (f32[64,1536]{1,0:T(8,128)}, f32[64,1536]{1,0:T(8,128)S(1)}, u32[]{:S(2)}) copy-start(f32[64,1536]{1,0:T(8,128)S(1)} %get-tuple-element.872) | copy-start | bytes 1179652
  1071.3 50.1 %copy-start.62 = (f32[3,1536]{1,0:T(4,128)}, f32[3,1536]{1,0:T(4,128)S(1)}, u32[]{:S(2)}) copy-start(f32[3,1536]{1,0:T(4,128)S(1)} %get-tuple-element.905) | copy-start | bytes 55300
  1071.3 50.1 %copy-start.73 = (f32[1536]{0:T(1024)}, f32[1536]{0:T(1024)S(1)}, u32[]{:S(2)}) copy-start(f32[1536]{0:T(1024)S(1)} %get-tuple-element.908) | copy-start | bytes 18436
  1071.3 49.0 %collective-permute-start.8 = (bf16[64,1536]{1,0:T(8,128)(2,1)S(1)}, bf16[64,1536]{1,0:T(8,128)(2,1)S(1)}, u32[]{:S(2)}, u32[]{:S(2)}) collective-permute-start(bf16[64,1536]{1,0:T(8,128)(2,1)S(1)} %convert_element_type.269), channel_id=1, source_target_pairs={{64,0},{65,1},{66,2},{67,3},{68,4},{69,5},{70,6},{71,7},{72,8},{73... | collective-permute-start | bytes 589832 | tf_op jit(solution)/shard_map/ppermute | solution.py:12
  1121.4 46.2 %copy-start.40 = (bf16[64,1536]{1,0:T(8,128)(2,1)S(1)}, bf16[64,1536]{1,0:T(8,128)(2,1)}, u32[]{:S(2)}) copy-start(bf16[64,1536]{1,0:T(8,128)(2,1)} %get-tuple-element.902) | copy-start | bytes 589828
  1135.9 13.9 copy-start.20
  1149.8 14.0 slice-start.4
  1149.9 13.0 copy-start.33
  1149.9 13.9 slice-start.5
  1175.2 9.3 copy-start.10
  1175.2 9.3 copy-start.17
  1175.2 9.3 copy-start.22
  1175.2 9.3 copy-start.26
  1175.2 9.3 copy-start.84
  1175.2 9.3 copy-start.86
  1175.2 490.6 %reduce-scatter.9.cloned.1.call-start = ((), (), s32[]{:S(2)}) async-start(), calls=%async_computation.6 | async-start | bytes 14598144 | tf_op jit(solution)/shard_map/reduce_scatter | solution.py:272
  1176.2 8.3 collective-permute-start.9
  1210.4 747.0 %reduce-scatter.17.cloned.1.call-start = ((), (), s32[]{:S(2)}) async-start(), calls=%async_computation.10 | async-start | bytes 21897216 | tf_op jit(solution)/shard_map/reduce_scatter | solution.py:284
  1224.5 1024.5 %reduce-scatter.13.cloned.1.call-start = ((), (), s32[]{:S(2)}) async-start(), calls=%async_computation.8 | async-start | bytes 21897216 | tf_op jit(solution)/shard_map/reduce_scatter | solution.py:278
  1236.5 1304.1 %reduce-scatter.15.cloned.1.call-start = ((), (), s32[]{:S(2)}) async-start(), calls=%async_computation.9 | async-start | bytes 21897216 | tf_op jit(solution)/shard_map/reduce_scatter | solution.py:281
  1247.9 1293.5 %copy-start.54 = (bf16[64,1536]{1,0:T(8,128)(2,1)S(1)}, bf16[64,1536]{1,0:T(8,128)(2,1)}, u32[]{:S(2)}) copy-start(bf16[64,1536]{1,0:T(8,128)(2,1)} %copy-done.53) | copy-start | bytes 589828
  1247.9 1516.7 %reduce-scatter.19.cloned.1.call-start = ((), (), s32[]{:S(2)}) async-start(), calls=%async_computation.16 | async-start | bytes 405504
  1249.7 1595.4 %all-reduce.10.cloned.1.call-start = ((), (), s32[]{:S(2)}) async-start(), calls=%async_computation.17 | async-start | bytes 5160960 | tf_op jit(solution)/shard_map/psum | solution.py:298
  2540.6 97.1 %copy-start.37 = (f32[64,1536]{1,0:T(8,128)S(1)}, f32[64,1536]{1,0:T(8,128)}, u32[]{:S(2)}) copy-start(f32[64,1536]{1,0:T(8,128)} %copy-done.36) | copy-start | bytes 1179652
  2540.6 97.1 %copy-start.39 = (f32[64,1536]{1,0:T(8,128)S(1)}, f32[64,1536]{1,0:T(8,128)}, u32[]{:S(2)}) copy-start(f32[64,1536]{1,0:T(8,128)} %copy-done.38) | copy-start | bytes 1179652
  2540.6 97.0 %copy-start.46 = (f32[64,1536]{1,0:T(8,128)S(1)}, f32[64,1536]{1,0:T(8,128)}, u32[]{:S(2)}) copy-start(f32[64,1536]{1,0:T(8,128)} %copy-done.45) | copy-start | bytes 1179652
  (43 other events, 128.4 us)
Sparse Core Ops, SparseCore 0:
  11.1 142.0 all-gather.13
  156.2 82.2 all-gather.15
  241.6 184.5 all-gather.17
  429.1 182.8 all-gather.19
  614.8 182.8 all-gather.21
  1175.3 229.7 reduce-scatter.10
  1410.5 255.2 reduce-scatter.8
  1672.7 284.6 reduce-scatter.16
  1964.4 284.5 reduce-scatter.12
  2255.8 284.7 reduce-scatter.14
  2546.7 217.8 reduce-scatter.18
  2767.3 77.7 all-reduce.9
where the time goes:
time: 2870 us; the launch traced here: 2860 us
  waiting for transfers between devices  2180 us (76%)
  blocking collectives  294 us (10%)
  matrix products  218 us (8%)
  other arithmetic  73.2 us (3%)
  local copies, waits for them, and re-layouts  40.6 us (1%)
  starting transfers between devices  30.6 us (1%)
    reduce_scatter x1, waiting for transfers between devices, local(): lax.psum_scatter(big[4].astype(jnp.bfloat16), 'fsdp', scatter_dimension=0...  292 us
    reduce_scatter x1, waiting for transfers between devices, local(): lax.psum_scatter(big[3].astype(jnp.bfloat16), 'fsdp', scatter_dimension=0...  292 us
    reduce_scatter x1, waiting for transfers between devices, local(): lax.psum_scatter(big[2].astype(jnp.bfloat16), 'fsdp', scatter_dimension=0...  292 us
    reduce_scatter x1, waiting for transfers between devices, local(): lax.psum_scatter(big[0].astype(jnp.bfloat16), 'fsdp', scatter_dimension=0...  261 us
    all_gather x1, waiting for transfers between devices, local(): lax.all_gather(w_up[0], 'fsdp', axis=0, tiled=True)  186 us
    all_gather x1, waiting for transfers between devices, local(): lax.all_gather(w_down[0], 'fsdp', axis=0, tiled=True)  186 us
    all_gather x1, waiting for transfers between devices, local(): lax.all_gather(w_gate[0], 'fsdp', axis=0, tiled=True)  163 us
    reduce_scatter x1, waiting for transfers between devices, local(): lax.psum_scatter(big[1].astype(jnp.bfloat16), 'fsdp', scatter_dimension=0...  155 us
  transfers between devices with their start and end apart: 22, of which 19 were waited for; matrix products, arithmetic and copies ran while one was open for 3% of the time, Pallas kernels for 0%

commit v1 on v0

v1 whole, which is shorter than its diff:
```python
import functools

import jax
import jax.numpy as jnp
from jax import lax
from jax.experimental import pallas as pl
from jax.experimental.pallas import tpu as pltpu
from jax.sharding import Mesh
from jax.sharding import PartitionSpec as P

F32, BF16 = jnp.float32, jnp.bfloat16
MESH = pl.DeviceIdType.MESH
EPS = 1e-06
ANY = pl.BlockSpec(memory_space=pl.ANY)
VMEM = pl.BlockSpec(memory_space=pltpu.VMEM)
ORDER = (1, 3, 2)


def place():
    return tuple(lax.axis_index(name) for name in ("section", "xl", "xh", "y", "z"))


def barrier_all(devices):
    barrier = pltpu.get_barrier_semaphore()
    for device in devices:
        pl.semaphore_signal(barrier, inc=1, device_id=device, device_id_type=MESH)
    pl.semaphore_wait(barrier, len(devices))


def remote(src, dst, send, recv, device):
    return pltpu.make_async_remote_copy(
        src_ref=src, dst_ref=dst, send_sem=send, recv_sem=recv, device_id=device, device_id_type=MESH
    )


def plane_peers():
    section, xl, xh, y, z = place()
    partner = {"xh": 1 - xh, "xl": 1 - xl}
    twin = {"xl": 1 - xl}
    zs = {r: {"z": lax.rem(z + r, 4)} for r in ORDER}
    ys = {r: {"y": lax.rem(y + r, 4)} for r in ORDER}
    return partner, twin, zs, ys


def gather_kernel(
    a_s, a_in, a_g, a_u, w_o, w_d,
    o_s, o_in, o_o, o_g, o_u, o_d,
    z_send, z_recv, y_send, y_recv, p_send, p_recv, q_send, q_recv, local, go,
):
    section, xl, xh, y, z = place()
    partner, twin, zs, ys = plane_peers()
    core = {"section": 1 - section}
    barrier_all([partner, twin, core, *zs.values(), *ys.values()])

    @pl.when(section == 1)
    def _():
        pl.semaphore_wait(go, 1)

    me = xh * 4 + y
    outs = (o_s, o_in, o_o, o_g, o_u, o_d)
    cut = (a_s, a_in, None, a_g, a_u, None)
    whole = (None, None, w_o, None, None, w_d)

    def half(n, ref, row, h):
        if n == 2:
            return ref.at[row, :, pl.ds(pl.multiple_of(h * 768, 128), 768)]
        if n == 5:
            return ref.at[row, pl.ds(pl.multiple_of(h * 112, 16), 112)]
        return ref.at[row, pl.ds(h * 2, 2)]

    sent, locals_, z_copies = [], {}, {}
    for n in range(6):
        if cut[n] is not None:
            block = (lambda zz: a_s) if n == 0 else (lambda zz, a=cut[n]: a.at[zz])
            for r in ORDER:
                copy = remote(block(lax.rem(z + r, 4)), outs[n].at[me, z], z_send.at[n, r - 1], z_recv.at[n, r - 1], zs[r])
                copy.start()
                z_copies[n, r] = copy
                sent.append(copy)
            own = pltpu.make_async_copy(block(z), outs[n].at[me, z], local.at[n])
        else:
            own = pltpu.make_async_copy(whole[n], outs[n].at[me], local.at[n])
        own.start()
        locals_[n] = own

    y_copies, p_copies, q_copies = {}, {}, {}

    def stage_y(n):
        locals_[n].wait()
        if cut[n] is not None:
            for r in ORDER:
                z_copies[n, r].wait_recv()
        for r in ORDER:
            copy = remote(outs[n].at[me], outs[n].at[me], y_send.at[n, r - 1], y_recv.at[n, r - 1], ys[r])
            copy.start()
            y_copies[n, r] = copy
            sent.append(copy)
        push_p(n, 0)

    def push_p(n, r):
        row = xh * 4 + lax.rem(y + 4 - r, 4)
        src = half(n, outs[n], row, xl)
        copy = remote(src, src, p_send.at[n, r], p_recv.at[n, r], partner)
        copy.start()
        p_copies[n, r] = copy
        sent.append(copy)

    def stage_p(n):
        for r in ORDER:
            y_copies[n, r].wait_recv()
            push_p(n, r)

    def stage_q(n):
        for r in (0, *ORDER):
            p_copies[n, r].wait_recv()
            row = (1 - xh) * 4 + lax.rem(y + 4 - r, 4)
            src = half(n, outs[n], row, 1 - xl)
            copy = remote(src, src, q_send.at[n, r], q_recv.at[n, r], twin)
            copy.start()
            q_copies[n, r] = copy
            sent.append(copy)

    for step in range(8):
        if step < 6:
            stage_y(step)
        if 0 <= step - 1 < 6:
            stage_p(step - 1)
        if 0 <= step - 2 < 6:
            stage_q(step - 2)
    for copy in q_copies.values():
        copy.wait_recv()

    @pl.when(section == 0)
    def _():
        pl.semaphore_signal(go, inc=1, device_id=core, device_id_type=MESH)

    for copy in sent:
        copy.wait_send()


def gather(a_s, a_in, a_g, a_u, w_o, w_d):
    shape = jax.ShapeDtypeStruct
    dma = pltpu.SemaphoreType.DMA
    return pl.pallas_call(
        gather_kernel,
        out_shape=(
            shape((8, 4, 16, 128), BF16),
            shape((8, 4, 48, 1152), BF16),
            shape((8, 48, 1536), BF16),
            shape((8, 4, 48, 1792), BF16),
            shape((8, 4, 48, 1792), BF16),
            shape((8, 224, 1536), BF16),
        ),
        in_specs=[ANY] * 6,
        out_specs=[ANY] * 6,
        scratch_shapes=[
            dma((6, 3)), dma((6, 3)), dma((6, 3)), dma((6, 3)),
            dma((6, 4)), dma((6, 4)), dma((6, 4)), dma((6, 4)),
            dma((6,)), pltpu.SemaphoreType.REGULAR,
        ],
        compiler_params=pltpu.CompilerParams(collective_id=0, has_side_effects=True),
        name="gather_weights",
    )(a_s, a_in, a_g, a_u, w_o, w_d)


def dot_nn(a, b):
    return lax.dot_general(a, b, (((1,), (0,)), ((), ())), preferred_element_type=F32)


def dot_nt(a, b):
    return lax.dot_general(a, b, (((1,), (1,)), ((), ())), preferred_element_type=F32)


def dot_tn(a, b):
    return lax.dot_general(a, b, (((0,), (0,)), ((), ())), preferred_element_type=F32)


def cols(j, width):
    return pl.ds(pl.multiple_of(j * width, width), width)


def loop(count, body):
    def step(j, carry):
        body(j)
        return carry

    lax.fori_loop(0, count, step, 0)


def main_kernel(
    x_ref, cot_ref, gains, taps, win_h, wout_h, wg_h, wu_h, wd_h,
    y_ref, gx_ref, gin_h, gout_h, gg_h, gu_h, gd_h, gtap_ref, gmix_ref, gffn_ref,
    xa, xn, n2, ea, fa, part, rr, proj, ge, dce, cv, ha, hb, mx, gt, up, hd, dg, du,
    mid, dmid, dp, g0, win, wout, wg, wu, wd,
    load, store, a_send, a_recv, s_send, s_recv, h_send, h_recv, c_send, c_recv, ready,
):
    section, xl, xh, y, z = place()
    zs = {r: {"z": lax.rem(z + r, 4)} for r in ORDER}
    core = {"section": 1 - section}
    group = xl * 8 + xh * 4 + y
    after, before = lax.rem(group + 1, 16), lax.rem(group + 15, 16)

    def at_group(g):
        return {"xl": g // 8, "xh": lax.rem(g // 4, 2), "y": lax.rem(g, 4)}

    has_after, has_before = group < 15, group > 0
    barrier = pltpu.get_barrier_semaphore()

    def hail(device):
        pl.semaphore_signal(barrier, inc=1, device_id=device, device_id_type=MESH)

    loads = [
        pltpu.make_async_copy(src, dst, load.at[n])
        for n, (src, dst) in enumerate(((win_h, win), (wout_h, wout), (wg_h, wg), (wu_h, wu), (wd_h, wd)))
    ]
    for copy in loads:
        copy.start()

    for r in ORDER:
        hail(zs[r])

    @pl.when(has_after)
    def _():
        hail(at_group(after))

    @pl.when(has_before)
    def _():
        hail(at_group(before))

    @pl.when(section == 0)
    def _():
        hail(core)

    pl.semaphore_wait(barrier, 4 - (group + 1) // 16 + (group + 15) // 16 + section)

    @pl.when(section == 1)
    def _():
        pl.semaphore_signal(ready, inc=1, device_id=core, device_id_type=MESH)

    own = pl.ds(pl.multiple_of(z * 128, 128), 128)

    def rows_from(r):
        return pl.multiple_of(lax.rem(z + 4 - r, 4) * 128, 128)

    def spread(n, buf):
        return {r: remote(buf.at[own], buf.at[own], a_send.at[n, r - 1], a_recv.at[n, r - 1], zs[r]) for r in ORDER}

    def scatter(n):
        found = {}
        for r in ORDER:
            src = part.at[pl.ds(pl.multiple_of(lax.rem(z + r, 4) * 128, 128), 128)]
            found[r] = remote(src, rr.at[n, r - 1], s_send.at[n, r - 1], s_recv.at[n, r - 1], zs[r])
        return found

    def summed(n, i):
        at = pl.ds(i * 32, 32)
        total = part[pl.ds(pl.multiple_of(z * 128 + i * 32, 32), 32), :].astype(F32)
        for r in range(3):
            total = total + rr[n, r, at, :].astype(F32)
        return total

    x_all, n_all, e_all, f_all = spread(0, xa), spread(1, n2), spread(2, ea), spread(3, fa)
    to_core_x = remote(y_ref, xa.at[own], c_send.at[0], c_recv.at[0], core)
    to_core_g = remote(g0, ea.at[own], c_send.at[1], c_recv.at[1], core)

    @pl.when(section == 0)
    def _():
        xa[own, :] = x_ref[...]

    @pl.when(section == 1)
    def _():
        ea[own, :] = cot_ref[...]
        for r in ORDER:
            e_all[r].start()
        to_core_x.wait_recv()

    for r in ORDER:
        x_all[r].start()

    gain_mix, gain_ffn = gains[0:1, :], gains[1:2, :]

    def norm_rows(base):
        def body(i):
            at = pl.ds(pl.multiple_of(base + i * 32, 32), 32)
            values = xa[at, :].astype(F32)
            scale = lax.rsqrt(jnp.mean(values * values, axis=-1, keepdims=True) + EPS)
            xn[at, :] = (values * scale * gain_mix).astype(BF16)

        loop(4, body)

    norm_rows(pl.multiple_of(z * 128, 128))
    for r in ORDER:
        x_all[r].wait_recv()
        norm_rows(rows_from(r))

    loads[0].wait()

    def project(j):
        proj[j] = dot_nn(xn[...], win[:, cols(j, 384)])

    loop(3, project)

    blocks = [(mb, zc, zc * 128 + mb * 64) for mb in range(2) for zc in range(4)]
    for mb, zc, r0 in blocks:
        ge[mb, 8 + 64 * zc : 72 + 64 * zc, :] = proj[0, r0 : r0 + 64, :] * proj[2, r0 : r0 + 64, :]

    to_after = remote(ge.at[:, pl.ds(256, 8)], ha, h_send.at[0], h_recv.at[0], at_group(after))
    to_before = remote(dce.at[:, pl.ds(0, 8)], hb, h_send.at[1], h_recv.at[1], at_group(before))

    @pl.when(has_after)
    def _():
        to_after.start()

    @pl.when(has_before)
    def _():
        to_after.wait_recv()
        ge[:, 0:8, :] = ha[...]

    @pl.when(jnp.logical_not(has_before))
    def _():
        ge[:, 0:8, :] = jnp.zeros((2, 8, 384), F32)

    tap = [taps[k : k + 1, :] for k in range(3)]
    for mb, zc, r0 in blocks:
        t0 = 8 + 64 * zc
        total = tap[0] * ge[mb, t0 : t0 + 64, :]
        for k in (1, 2):
            total = total + tap[k] * ge[mb, t0 - k : t0 - k + 64, :]
        cv[r0 : r0 + 64, :] = total
        mx[r0 : r0 + 64, :] = (proj[1, r0 : r0 + 64, :] * total).astype(BF16)

    loads[1].wait()

    def mix_out(j):
        part[:, cols(j, 512)] = dot_nn(mx[...], wout[:, cols(j, 512)]).astype(BF16)

    loop(3, mix_out)
    sums = [scatter(n) for n in range(4)]
    for r in ORDER:
        sums[0][r].start()
    for r in ORDER:
        sums[0][r].wait_recv()

    def middle(i):
        at = pl.ds(i * 32, 32)
        mine = pl.ds(pl.multiple_of(z * 128 + i * 32, 32), 32)
        values = xa[mine, :].astype(F32) + summed(0, i)
        mid[at, :] = values
        scale = lax.rsqrt(jnp.mean(values * values, axis=-1, keepdims=True) + EPS)
        n2[mine, :] = (values * scale * gain_ffn).astype(BF16)

    loop(4, middle)
    for r in ORDER:
        n_all[r].start()
    for r in ORDER:
        sums[0][r].wait_send()
    loads[2].wait()
    loads[3].wait()
    for r in ORDER:
        n_all[r].wait_recv()

    def gate(j):
        at = cols(j, 256)
        gating = dot_nn(n2[...], wg[:, at])
        up_part = dot_nn(n2[...], wu[:, at])
        gt[:, at] = gating
        up[:, at] = up_part
        hd[:, at] = (gating * jax.nn.sigmoid(gating) * up_part).astype(BF16)

    loop(7, gate)
    loads[4].wait()

    def ffn_out(j):
        part[:, cols(j, 256)] = dot_nn(hd[...], wd[:, cols(j, 256)]).astype(BF16)

    loop(6, ffn_out)
    for r in ORDER:
        sums[1][r].start()
    for r in ORDER:
        sums[1][r].wait_recv()

    def finish(i):
        at = pl.ds(i * 32, 32)
        y_ref[at, :] = (mid[at, :] + summed(1, i)).astype(BF16)

    loop(4, finish)

    @pl.when(section == 0)
    def _():
        pl.semaphore_wait(ready, 1)
        to_core_x.start()
        to_core_g.wait_recv()
        for r in ORDER:
            e_all[r].start()

    for r in ORDER:
        sums[1][r].wait_send()
    for r in ORDER:
        e_all[r].wait_recv()

    def back_hidden(j):
        at = cols(j, 256)
        dh = dot_nt(ea[...], wd[at, :])
        gating, up_part = gt[:, at], up[:, at]
        sg = jax.nn.sigmoid(gating)
        dg[:, at] = (dh * up_part * sg * (1.0 + gating * (1.0 - sg))).astype(BF16)
        du[:, at] = (dh * gating * sg).astype(BF16)

    loop(7, back_hidden)

    def back_ffn(j):
        at = cols(j, 256)
        part[:, at] = (dot_nt(dg[...], wg[at, :]) + dot_nt(du[...], wu[at, :])).astype(BF16)

    loop(6, back_ffn)
    for r in ORDER:
        sums[2][r].start()

    def grad_down(j):
        at = cols(j, 256)
        wd[at, :] = dot_tn(hd[:, at], ea[...]).astype(BF16)

    loop(7, grad_down)
    stores = [
        pltpu.make_async_copy(src, dst, store.at[n])
        for n, (src, dst) in enumerate(((win, gin_h), (wout, gout_h), (wg, gg_h), (wu, gu_h), (wd, gd_h)))
    ]
    stores[4].start()
    for r in ORDER:
        sums[2][r].wait_recv()
    gffn_ref[...] = jnp.zeros((1, 1536), F32)
    gmix_ref[...] = jnp.zeros((1, 1536), F32)

    def back_middle(i):
        at = pl.ds(i * 32, 32)
        mine = pl.ds(pl.multiple_of(z * 128 + i * 32, 32), 32)
        dn2 = summed(2, i)
        values = mid[at, :]
        scale = lax.rsqrt(jnp.mean(values * values, axis=-1, keepdims=True) + EPS)
        weighted = dn2 * gain_ffn
        mean_term = jnp.mean(weighted * values, axis=-1, keepdims=True)
        grad = ea[mine, :].astype(F32) + scale * weighted - values * (scale * scale * scale) * mean_term
        gffn_ref[...] += jnp.sum(dn2 * values * scale, axis=0, keepdims=True)
        dmid[at, :] = grad
        fa[mine, :] = grad.astype(BF16)

    loop(4, back_middle)
    for r in ORDER:
        f_all[r].start()

    def grad_gate(j):
        at = cols(j, 256)
        wg[at, :] = dot_tn(n2[:, at], dg[...]).astype(BF16)

    loop(6, grad_gate)
    stores[2].start()

    def grad_up(j):
        at = cols(j, 256)
        wu[at, :] = dot_tn(n2[:, at], du[...]).astype(BF16)

    loop(6, grad_up)
    stores[3].start()
    for r in ORDER:
        sums[2][r].wait_send()
    for r in ORDER:
        f_all[r].wait_recv()

    for zc in range(4):
        dm = dot_nt(fa[zc * 128 : zc * 128 + 128, :], wout[...])
        for mb in range(2):
            r0 = zc * 128 + mb * 64
            piece = dm[mb * 64 : mb * 64 + 64, :]
            dp[r0 : r0 + 64, 384:768] = (piece * cv[r0 : r0 + 64, :]).astype(BF16)
            dce[mb, 64 * zc : 64 * zc + 64, :] = piece * proj[1, r0 : r0 + 64, :]

    @pl.when(has_before)
    def _():
        to_before.start()

    def grad_out(j):
        at = cols(j, 128)
        wout[at, :] = dot_tn(mx[:, at], fa[...]).astype(BF16)

    loop(3, grad_out)
    stores[1].start()
    for k in range(3):
        total = jnp.zeros((1, 384), F32)
        for mb, zc, r0 in blocks:
            t0 = 8 + 64 * zc - k
            total = total + jnp.sum(
                dce[mb, 64 * zc : 64 * zc + 64, :] * ge[mb, t0 : t0 + 64, :], axis=0, keepdims=True
            )
        gtap_ref[k : k + 1, :] = total

    @pl.when(has_after)
    def _():
        to_before.wait_recv()
        dce[:, 256:264, :] = hb[...]

    @pl.when(jnp.logical_not(has_after))
    def _():
        dce[:, 256:264, :] = jnp.zeros((2, 8, 384), F32)

    for mb, zc, r0 in blocks:
        t0 = 64 * zc
        total = tap[0] * dce[mb, t0 : t0 + 64, :]
        for k in (1, 2):
            total = total + tap[k] * dce[mb, t0 + k : t0 + k + 64, :]
        dp[r0 : r0 + 64, 0:384] = (total * proj[2, r0 : r0 + 64, :]).astype(BF16)
        dp[r0 : r0 + 64, 768:1152] = (total * proj[0, r0 : r0 + 64, :]).astype(BF16)

    def back_in(j):
        at = cols(j, 256)
        part[:, at] = dot_nt(dp[...], win[at, :]).astype(BF16)

    loop(6, back_in)
    for r in ORDER:
        sums[3][r].start()

    def grad_in(j):
        at = cols(j, 256)
        win[at, :] = dot_tn(xn[:, at], dp[...]).astype(BF16)

    loop(6, grad_in)
    stores[0].start()
    for r in ORDER:
        sums[3][r].wait_recv()

    def back_input(i):
        at = pl.ds(i * 32, 32)
        mine = pl.ds(pl.multiple_of(z * 128 + i * 32, 32), 32)
        dn = summed(3, i)
        values = xa[mine, :].astype(F32)
        scale = lax.rsqrt(jnp.mean(values * values, axis=-1, keepdims=True) + EPS)
        weighted = dn * gain_mix
        mean_term = jnp.mean(weighted * values, axis=-1, keepdims=True)
        grad = dmid[at, :] + scale * weighted - values * (scale * scale * scale) * mean_term
        gmix_ref[...] += jnp.sum(dn * values * scale, axis=0, keepdims=True)
        gx_ref[at, :] = grad
        g0[at, :] = grad.astype(BF16)

    loop(4, back_input)

    @pl.when(section == 1)
    def _():
        to_core_g.start()
        to_core_g.wait_send()

    @pl.when(section == 0)
    def _():
        to_core_x.wait_send()

    @pl.when(has_after)
    def _():
        to_after.wait_send()

    @pl.when(has_before)
    def _():
        to_before.wait_send()

    for r in ORDER:
        sums[3][r].wait_send()
        for copies in (x_all, n_all, e_all, f_all):
            copies[r].wait_send()
    for copy in stores:
        copy.wait()


def main(x, cot, gains, taps, win, wout, wg, wu, wd):
    shape = jax.ShapeDtypeStruct
    dma = pltpu.SemaphoreType.DMA
    vm = pltpu.VMEM
    return pl.pallas_call(
        main_kernel,
        out_shape=(
            shape((128, 1536), BF16),
            shape((128, 1536), F32),
            shape((1536, 1152), BF16),
            shape((384, 1536), BF16),
            shape((1536, 1792), BF16),
            shape((1536, 1792), BF16),
            shape((1792, 1536), BF16),
            shape((3, 384), F32),
            shape((1, 1536), F32),
            shape((1, 1536), F32),
        ),
        in_specs=[VMEM] * 4 + [ANY] * 5,
        out_specs=[VMEM] * 2 + [ANY] * 5 + [VMEM] * 3,
        scratch_shapes=[
            vm((512, 1536), BF16), vm((512, 1536), BF16), vm((512, 1536), BF16), vm((512, 1536), BF16),
            vm((512, 1536), BF16), vm((512, 1536), BF16), vm((4, 3, 128, 1536), BF16),
            vm((3, 512, 384), F32), vm((2, 264, 384), F32), vm((2, 264, 384), F32), vm((512, 384), F32),
            vm((2, 8, 384), F32), vm((2, 8, 384), F32), vm((512, 384), BF16),
            vm((512, 1792), F32), vm((512, 1792), F32), vm((512, 1792), BF16), vm((512, 1792), BF16),
            vm((512, 1792), BF16), vm((128, 1536), F32), vm((128, 1536), F32), vm((512, 1152), BF16),
            vm((128, 1536), BF16),
            vm((1536, 1152), BF16), vm((384, 1536), BF16), vm((1536, 1792), BF16), vm((1536, 1792), BF16),
            vm((1792, 1536), BF16),
            dma((5,)), dma((5,)), dma((4, 3)), dma((4, 3)), dma((4, 3)), dma((4, 3)),
            dma((2,)), dma((2,)), dma((2,)), dma((2,)), pltpu.SemaphoreType.REGULAR,
        ],
        compiler_params=pltpu.CompilerParams(
            collective_id=1, has_side_effects=True, vmem_limit_bytes=63 * 2**20
        ),
        name="two_blocks",
    )(x, cot, gains, taps, win, wout, wg, wu, wd)


def reduce_kernel(
    g_d, g_g, g_u, g_o, g_in, g_s,
    o_d, o_g, o_u, o_o, o_in, o_s,
    v_d, v_g, v_u, v_o, v_in, v_s,
    q1_g, q1_u, q1_o, q1_in, q1_s,
    p_d, p_g, p_u, p_o, p_in, p_s,
    y_d, y_g, y_u, y_o, y_in, y_s,
    f_d, f_g, f_u, f_o, f_in, f_s,
    t_d, t_g, t_u, t_o, t_in, t_s,
    e_g, e_u, e_in, e_s, b_s,
    load, q_send, q_recv, p_send, p_recv, y_send, y_recv, t_send, t_recv, z_send, z_recv, keep,
):
    section, xl, xh, y, z = place()
    partner, twin, zs, ys = plane_peers()
    grads = (g_d, g_g, g_u, g_o, g_in, g_s)
    held = (v_d, v_g, v_u, v_o, v_in, v_s)
    from_twin = (None, q1_g, q1_u, q1_o, q1_in, q1_s)
    from_partner = (p_d, p_g, p_u, p_o, p_in, p_s)
    from_y = (y_d, y_g, y_u, y_o, y_in, y_s)
    mine = (f_d, f_g, f_u, f_o, f_in, f_s)
    theirs = (t_d, t_g, t_u, t_o, t_in, t_s)
    ended = (None, e_g, e_u, None, e_in, e_s)
    outs = (o_d, o_g, o_u, o_o, o_in, b_s)
    loads = [pltpu.make_async_copy(grads[n], held[n], load.at[n]) for n in range(6)]
    for copy in loads:
        copy.start()
    barrier_all([partner, twin, *zs.values(), *ys.values()])
    near, far = xh * 4, (1 - xh) * 4
    me = near + y
    sent = []
    copies = {}

    def begin(key, copy):
        copy.start()
        copies[key] = copy
        sent.append(copy)

    def half(n, ref, first, h):
        if n == 3:
            return ref.at[pl.ds(first, 4), :, pl.ds(pl.multiple_of(h * 768, 128), 768)]
        return ref.at[pl.ds(first, 4), pl.ds(h * 2, 2)]

    def add(n, first, h, other):
        if n == 0:
            def body(i):
                row, at = i // 7, pl.ds(lax.rem(i, 7) * 32, 32)
                v_d[first + row, at, :] = (v_d[first + row, at, :].astype(F32) + other[row, at, :].astype(F32)).astype(BF16)

            loop(28, body)
        elif n == 3:
            at = pl.ds(pl.multiple_of(h * 768, 128), 768)

            def body(i):
                v_o[first + i, :, at] = (v_o[first + i, :, at].astype(F32) + other[i].astype(F32)).astype(BF16)

            loop(4, body)
        else:
            ref = held[n]

            def body(i):
                a, b = first + i // 2, h * 2 + lax.rem(i, 2)
                ref[a, b] = (ref[a, b].astype(F32) + other[i // 2, lax.rem(i, 2)].astype(F32)).astype(ref.dtype)

            loop(8, body)

    def stage_0(n):
        loads[n].wait()
        if n:
            begin(("q", n), remote(half(n, held[n], far, 1 - xl), from_twin[n], q_send.at[n], q_recv.at[n], twin))
        else:
            begin(("p", n), remote(held[n].at[pl.ds(far, 4)], from_partner[n], p_send.at[n], p_recv.at[n], partner))

    def stage_1(n):
        if n:
            copies["q", n].wait_recv()
            add(n, far, xl, from_twin[n])
            begin(("p", n), remote(half(n, held[n], far, xl), from_partner[n], p_send.at[n], p_recv.at[n], partner))

    def stage_2(n):
        copies["p", n].wait_recv()
        add(n, near, 1 - xl, from_partner[n])
        for r in ORDER:
            row = near + lax.rem(y + r, 4)
            begin(("y", n, r), remote(held[n].at[row], from_y[n].at[r - 1], y_send.at[n, r - 1], y_recv.at[n, r - 1], ys[r]))

    def pieces(n):
        if n == 0:
            return 7, lambda ref, i: ref[pl.ds(i * 32, 32), :]
        if n == 3:
            return 3, lambda ref, i: ref[pl.ds(i * 16, 16), :]
        return 4, lambda ref, i: ref[i]

    def put(n, ref, i, value):
        if n == 0:
            ref[pl.ds(i * 32, 32), :] = value
        elif n == 3:
            ref[pl.ds(i * 16, 16), :] = value
        else:
            ref[i] = value

    def stage_3(n):
        for r in ORDER:
            copies["y", n, r].wait_recv()
        count, get = pieces(n)

        def body(i):
            total = get(held[n].at[me], i).astype(F32)
            for r in range(3):
                total = total + get(from_y[n].at[r], i).astype(F32)
            put(n, mine[n], i, total.astype(mine[n].dtype))

        loop(count, body)
        begin(("t", n), remote(mine[n], theirs[n], t_send.at[n], t_recv.at[n], twin))

    def stage_4(n):
        copies["t", n].wait_recv()
        count, get = pieces(n)
        target = outs[n] if ended[n] is None else ended[n]

        def body(i):
            total = get(mine[n], i).astype(F32) + get(theirs[n], i).astype(F32)
            put(n, target, i, total.astype(target.dtype))

        loop(count, body)
        if ended[n] is not None:
            for r in ORDER:
                begin(("z", n, r), remote(target.at[lax.rem(z + r, 4)], outs[n].at[z], z_send.at[n, r - 1], z_recv.at[n, r - 1], zs[r]))
            copy = pltpu.make_async_copy(target.at[z], outs[n].at[z], keep.at[n])
            copy.start()
            copies["keep", n] = copy

    stages = (stage_0, stage_1, stage_2, stage_3, stage_4)
    for step in range(10):
        for s, stage in enumerate(stages):
            if 0 <= step - s < 6:
                stage(step - s)
    for n in (1, 2, 4, 5):
        copies["keep", n].wait()
        for r in ORDER:
            copies["z", n, r].wait_recv()
    o_s[...] = b_s[0] + b_s[1] + b_s[2] + b_s[3]
    for copy in sent:
        copy.wait_send()


def reduce(g_d, g_g, g_u, g_o, g_in, g_s):
    shape = jax.ShapeDtypeStruct
    dma = pltpu.SemaphoreType.DMA
    vm = pltpu.VMEM
    big = ((4, 48, 1792), (4, 48, 1792), (4, 48, 1152))
    return pl.pallas_call(
        reduce_kernel,
        out_shape=(
            shape((224, 1536), F32),
            shape((4, 48, 1792), BF16),
            shape((4, 48, 1792), BF16),
            shape((48, 1536), F32),
            shape((4, 48, 1152), BF16),
            shape((8, 128), F32),
        ),
        in_specs=[ANY] * 6,
        out_specs=[VMEM, ANY, ANY, VMEM, ANY, VMEM],
        scratch_shapes=[
            vm((8, 224, 1536), BF16), vm((8, 4, 48, 1792), BF16), vm((8, 4, 48, 1792), BF16),
            vm((8, 48, 1536), BF16), vm((8, 4, 48, 1152), BF16), vm((8, 4, 8, 128), F32),
            vm((4, 2, 48, 1792), BF16), vm((4, 2, 48, 1792), BF16), vm((4, 48, 768), BF16),
            vm((4, 2, 48, 1152), BF16), vm((4, 2, 8, 128), F32),
            vm((4, 224, 1536), BF16), vm((4, 2, 48, 1792), BF16), vm((4, 2, 48, 1792), BF16),
            vm((4, 48, 768), BF16), vm((4, 2, 48, 1152), BF16), vm((4, 2, 8, 128), F32),
            vm((3, 224, 1536), BF16), vm((3, 4, 48, 1792), BF16), vm((3, 4, 48, 1792), BF16),
            vm((3, 48, 1536), BF16), vm((3, 4, 48, 1152), BF16), vm((3, 4, 8, 128), F32),
            vm((224, 1536), BF16), vm(big[0], BF16), vm(big[1], BF16), vm((48, 1536), BF16), vm(big[2], BF16),
            vm((4, 8, 128), F32),
            vm((224, 1536), BF16), vm(big[0], BF16), vm(big[1], BF16), vm((48, 1536), BF16), vm(big[2], BF16),
            vm((4, 8, 128), F32),
            vm(big[0], BF16), vm(big[1], BF16), vm(big[2], BF16), vm((4, 8, 128), F32), vm((4, 8, 128), F32),
            dma((6,)), dma((6,)), dma((6,)), dma((6,)), dma((6,)), dma((6, 3)), dma((6, 3)),
            dma((6,)), dma((6,)), dma((6, 3)), dma((6, 3)), dma((6,)),
        ],
        compiler_params=pltpu.CompilerParams(
            collective_id=2, has_side_effects=True, vmem_limit_bytes=63 * 2**20
        ),
        name="reduce_grads",
    )(g_d, g_g, g_u, g_o, g_in, g_s)


def cut_ffn(weight):
    tiles = jnp.pad(weight.reshape(48, 8, 4, 216), ((0, 0), (0, 0), (0, 0), (0, 8)))
    return tiles.transpose(2, 0, 1, 3).reshape(4, 48, 1792)


def uncut_ffn(value):
    tiles = value.reshape(4, 48, 8, 224)[..., :216]
    return tiles.transpose(1, 2, 0, 3).reshape(1, 48, 6912).astype(F32)


def local(inputs, cotangent, w_in, w_out, w_gate, w_up, w_down, kernel, gain_mix, gain_ffn):
    a_in = w_in.reshape(48, 3, 8, 4, 48).transpose(3, 0, 1, 2, 4).reshape(4, 48, 1152)
    small = jnp.concatenate([kernel[0], gain_mix, gain_ffn], axis=0)
    small = jnp.pad(small, ((0, 11), (0, 80)))
    s_all, win, wout, wg, wu, wd = gather(
        small, a_in, cut_ffn(w_gate[0]), cut_ffn(w_up[0]), w_out[0], jnp.pad(w_down[0], ((0, 8), (0, 0)))
    )
    z = lax.axis_index("z")
    gains = s_all[:, :, 3:5, :48].astype(F32).transpose(2, 0, 1, 3).reshape(2, 1536)
    own_taps = lax.dynamic_index_in_dim(s_all, z, axis=1, keepdims=False)[:, 0:3, :48]
    taps = own_taps.astype(F32).transpose(1, 0, 2).reshape(3, 384)
    y, gx, g_in, g_o, g_g, g_u, g_d, g_tap, g_mix, g_ffn = main(
        inputs.reshape(128, 1536),
        cotangent.reshape(128, 1536),
        gains,
        taps,
        win.reshape(1536, 1152),
        wout.reshape(384, 1536),
        wg.reshape(1536, 1792),
        wu.reshape(1536, 1792),
        wd.reshape(1792, 1536),
    )
    tap_rows = g_tap.reshape(3, 8, 48).transpose(1, 0, 2)
    at_z = (lax.broadcasted_iota(jnp.int32, (1, 4, 1, 1), 1) == z).astype(F32)
    tap_rows = tap_rows[:, None] * at_z
    gain_rows = jnp.stack([g_mix.reshape(8, 4, 48), g_ffn.reshape(8, 4, 48)], axis=2)
    g_s = jnp.pad(jnp.concatenate([tap_rows, gain_rows], axis=2), ((0, 0), (0, 0), (0, 3), (0, 80)))
    o_d, o_g, o_u, o_o, o_in, o_s = reduce(
        g_d.reshape(8, 224, 1536),
        g_g.reshape(8, 4, 48, 1792),
        g_u.reshape(8, 4, 48, 1792),
        g_o.reshape(8, 48, 1536),
        g_in.reshape(8, 4, 48, 1152),
        g_s,
    )
    grad_in = o_in.reshape(4, 48, 3, 8, 48).transpose(1, 2, 3, 0, 4).reshape(1, 48, 4608).astype(F32)
    return (
        y.reshape(1, 2, 64, 1536),
        gx.reshape(1, 2, 64, 1536),
        grad_in,
        o_o[None],
        uncut_ffn(o_g),
        uncut_ffn(o_u),
        o_d[None, :216],
        o_s[None, 0:3, :48],
        o_s[3:4, :48],
        o_s[4:5, :48],
    )


def solution(mesh):
    names = ("section", "xl", "xh", "y", "z")
    fine = Mesh(mesh.devices.reshape(2, 2, 2, 4, 4), names)
    tokens, shard = ("xl", "xh", "y", "z"), ("xh", "y", "z")
    weight = P("section", shard, None)
    acts = P("section", None, tokens, None)
    return jax.shard_map(
        local,
        mesh=fine,
        in_specs=(
            P(None, tokens, None),
            P(None, tokens, None),
            weight,
            weight,
            weight,
            weight,
            weight,
            P("section", None, shard),
            P("section", shard),
            P("section", shard),
        ),
        out_specs=(
            acts,
            acts,
            weight,
            weight,
            weight,
            weight,
            weight,
            P("section", None, shard),
            P("section", shard),
            P("section", shard),
        ),
        check_vma=False,
    )
```

time: 2870 us -> 580 us (0.20)
  waiting for transfers between devices: 2180 us -> 0 us
  Pallas kernels: 0 us -> 532 us
  blocking collectives: 294 us -> 0 us
  matrix products: 218 us -> 0 us
  other arithmetic: 73.2 us -> 4.75 us
  starting transfers between devices: 30.6 us -> 0 us
    reduce_scatter x5 -> x0, waiting for transfers between devices: 1290 us -> none  [the longest x1 292 us: local(): lax.psum_scatter(big[4].astype(jnp.bfloat16), 'fsdp', scatter_dimension=0...]
    all_gather x5 -> x0, waiting for transfers between devices: 575 us -> none  [the longest x1 186 us: local(): lax.all_gather(w_up[0], 'fsdp', axis=0, tiled=True)]
    pallas_call x0 -> x3, Pallas kernels: none -> 532 us  [the longest x1 296 us: main(): pl.pallas_call(main_kernel, out_shape=(shape((128, 1536), BF16), shape((1...]
    dot_general x25 -> x0, matrix products: 218 us -> none  [the longest x10 96.4 us: contract_last(): lax.dot_general(left_side, right_side, (((1,), (1,)), ((), ())), preferre...]
    all_gather x2 -> x0, blocking collectives: 196 us -> none  [the longest x1 100 us: local(): lax.all_gather(gain_mix[0], 'fsdp', axis=0, tiled=True)]
    unnamed x13 -> x0, waiting for transfers between devices: 129 us -> none
    ppermute x10 -> x0, waiting for transfers between devices: 116 us -> none  [from_behind(): lax.ppermute(value, axis, [(source, source + steps) for source in range(f...]
    unnamed x1 -> x0, blocking collectives: 93.6 us -> none
  transfers between devices with their start and end apart: 22 -> 0, of which waited for: 19 -> 0; matrix products, arithmetic and copies ran while one was open for 3% -> 0% of each run, Pallas kernels for 0% -> 0%
where the time goes in v1:
time: 580 us; the launch traced here: 579 us
  Pallas kernels  532 us (92%)
  local copies, waits for them, and re-layouts  42.1 us (7%)
    pallas_call x1, Pallas kernels, main(): pl.pallas_call(main_kernel, out_shape=(shape((128, 1536), BF16), shape((1...  296 us
    pallas_call x1, Pallas kernels, reduce(): pl.pallas_call(reduce_kernel, out_shape=(shape((224, 1536), F32), shape((...  129 us
    pallas_call x1, Pallas kernels, gather(): pl.pallas_call(gather_kernel, out_shape=(shape((8, 4, 16, 128), BF16), sh...  107 us

profile of v1, /device:TPU:2, one launch (start us, length us, event | category | flops | bytes accessed | tf_op | source)
XLA Modules:
  0.0 579.4 jit_solution(16063957137428102497)
XLA Ops:
  0.6 0.0 copy-start.3
  0.7 1.4 fusion.8.a_s
  2.0 2.0 pad.22.w_d
  4.0 0.0 copy-done.3
  4.0 2.4 reshape_squeeze.6
  6.4 0.1 copy.30
  6.5 0.0 copy-start.4
  6.5 0.1 pad_bitcast_fusion.1
  6.7 1.8 reshape.153.a_g
  8.5 0.0 copy-done.4
  8.5 2.4 reshape_squeeze.7
  10.9 0.1 copy.31
  11.0 0.0 copy-start.5
  11.0 0.1 pad_bitcast_fusion
  11.2 1.8 reshape.154.a_u
  13.0 0.0 copy-done.5
  13.0 1.2 reshape.151
  14.2 0.2 copy.41
  14.3 1.7 reshape.152.a_in
  16.0 106.8 %gather_weights.1 = (bf16[8,4,16,128]{3,2,1,0:T(8,128)(2,1)}, bf16[8,4,48,1152]{3,2,1,0:T(8,128)(2,1)}, bf16[8,48,1536]{2,1,0:T(8,128)(2,1)}, bf16[8,4,48,1792]{...) custom-call(bf16[16,128]{1,0:T(8,128)(2,1)} %fusion.8.a_s, ...), custom_call_target="tpu_custom_call" | custom-call | tf_op jit(solution)/shard_map/gather_weights/pallas_call | solution.py:144
  122.8 0.8 dynamic-slice_bitcast_fusion
  123.5 0.9 convert_bitcast_fusion.2
  124.4 0.7 reshape.177.taps
  125.1 0.7 reshape.175.gains
  125.8 296.2 %two_blocks.1 = (bf16[128,1536]{1,0:T(8,128)(2,1)}, f32[128,1536]{1,0:T(8,128)}, bf16[1536,1152]{1,0:T(8,128)(2,1)}, bf16[384,1536]{1,0:T(8,128)(2,1)}, bf16[153...) custom-call(bf16[128,1536]{1,0:T(8,128)(2,1)} %bitcast.64, ...), custom_call_target="tpu_custom_call" | custom-call | tf_op jit(solution)/shard_map/two_blocks/pallas_call | solution.py:574
  422.0 0.7 reduce
  422.7 0.7 reduce.1
  423.4 0.1 stack_reshape.7
  423.5 0.1 stack_reshape.6
  423.6 0.8 reshape.171
  424.4 0.1 broadcast_multiply_fusion
  424.5 0.7 select_maximum_fusion.g_s
  425.2 128.7 %reduce_grads.1 = (f32[224,1536]{1,0:T(8,128)}, bf16[4,48,1792]{2,1,0:T(8,128)(2,1)}, bf16[4,48,1792]{2,1,0:T(8,128)(2,1)}, f32[48,1536]{1,0:T(8,128)}, bf16[4,48,1152]{2,1,0:T(8,128)(2,1)}, /*index=5*/f32[8,128]{1,0:T(8,128)}) custom-call(bf16[8,224,1536]{2,1,0:T(8,128)(2,1)} %bitcast.52, bf16[8,4,48,1792]{3,2,1,0:T(8,128)(2,1)} %bitcast.50, ...), custom_call_target="tpu_custom_call" | custom-call | tf_op jit(solution)/shard_map/reduce_grads/pallas_call | solution.py:760
  553.9 1.3 fusion.9
  555.2 0.7 slice_bitcast_fusion.1
  555.8 0.6 copy.38
  556.4 2.5 reshape.172
  558.9 0.1 convert_bitcast_fusion.1
  559.0 1.0 copy.36
  560.1 0.0 copy-start.2
  560.1 2.6 reshape.179
  562.7 0.0 copy-done.2
  562.7 1.1 reshape.173
  563.8 0.1 convert_bitcast_fusion
  564.0 1.0 copy.37
  565.0 0.0 copy-start
  565.0 2.6 reshape.180
  567.6 0.0 copy-done
  567.6 0.0 copy-start.6
  567.6 1.1 slice_bitcast_fusion
  568.7 0.0 copy-done.6
  568.7 1.0 reshape.183
  569.8 2.9 copy.35
  572.7 0.0 copy-start.7
  572.7 0.0 copy-start.1
  572.7 4.3 reshape.178
  577.0 0.0 copy-done.7
  577.0 0.0 copy-start.8
  577.0 0.7 copy.46
  577.8 0.0 copy-done.1
  577.8 0.9 copy.47
  578.7 0.0 copy-done.8
  578.7 0.7 copy.48
  (5 shorter events, 0.0 us)
Async XLA Ops:
  0.6 3.4 copy-start.3
  6.5 2.0 copy-start.4
  11.0 2.0 copy-start.5
  560.1 2.6 copy-start.2
  565.0 2.6 copy-start
  567.6 1.2 copy-start.6
  572.7 4.3 copy-start.7
  572.7 5.1 copy-start.1
  577.0 1.6 copy-start.8

commit v2 on v1

--- a/solution.py
+++ b/solution.py
@@ -14,6 +14,17 @@
 ANY = pl.BlockSpec(memory_space=pl.ANY)
 VMEM = pl.BlockSpec(memory_space=pltpu.VMEM)
 ORDER = (1, 3, 2)
+
+GATHER_UNITS = (
+    (0, 0, 128), (1, 0, 1152), (2, 0, 1536),
+    (3, 0, 640), (4, 0, 640), (3, 640, 640), (4, 640, 640), (3, 1280, 512), (4, 1280, 512),
+    (5, 0, 80), (5, 80, 80), (5, 160, 64),
+)
+REDUCE_UNITS = (
+    (0, 0, 80), (0, 80, 80), (0, 160, 64),
+    (1, 0, 640), (1, 640, 640), (1, 1280, 512), (2, 0, 640), (2, 640, 640), (2, 1280, 512),
+    (3, 0, 1536), (4, 0, 640), (4, 640, 512), (5, 0, 128),
+)
 
 
 def place():
@@ -61,12 +72,21 @@
     cut = (a_s, a_in, None, a_g, a_u, None)
     whole = (None, None, w_o, None, None, w_d)
 
-    def half(n, ref, row, h):
+    def piece(u, row):
+        n, first, size = GATHER_UNITS[u]
         if n == 2:
-            return ref.at[row, :, pl.ds(pl.multiple_of(h * 768, 128), 768)]
+            return outs[n].at[row]
         if n == 5:
-            return ref.at[row, pl.ds(pl.multiple_of(h * 112, 16), 112)]
-        return ref.at[row, pl.ds(h * 2, 2)]
+            return outs[n].at[row, pl.ds(first, size)]
+        return outs[n].at[row, :, :, pl.ds(first, size)]
+
+    def half(u, row, h):
+        n, first, size = GATHER_UNITS[u]
+        if n == 2:
+            return outs[n].at[row, :, pl.ds(pl.multiple_of(h * 768, 128), 768)]
+        if n == 5:
+            return outs[n].at[row, pl.ds(first, size), pl.ds(pl.multiple_of(h * 768, 128), 768)]
+        return outs[n].at[row, pl.ds(h * 2, 2), :, pl.ds(first, size)]
 
     sent, locals_, z_copies = [], {}, {}
     for n in range(6):
@@ -83,57 +103,61 @@
         own.start()
         locals_[n] = own
 
-    y_copies, p_copies, q_copies = {}, {}, {}
-
-    def stage_y(n):
-        locals_[n].wait()
-        if cut[n] is not None:
-            for r in ORDER:
-                z_copies[n, r].wait_recv()
+    y_copies, p_copies, q_copies, ready = {}, {}, {}, set()
+
+    def stage_y(u):
+        n = GATHER_UNITS[u][0]
+        if n not in ready:
+            ready.add(n)
+            locals_[n].wait()
+            if cut[n] is not None:
+                for r in ORDER:
+                    z_copies[n, r].wait_recv()
         for r in ORDER:
-            copy = remote(outs[n].at[me], outs[n].at[me], y_send.at[n, r - 1], y_recv.at[n, r - 1], ys[r])
+            src = piece(u, me)
+            copy = remote(src, src, y_send.at[u, r - 1], y_recv.at[u, r - 1], ys[r])
             copy.start()
-            y_copies[n, r] = copy
+            y_copies[u, r] = copy
             sent.append(copy)
-        push_p(n, 0)
-
-    def push_p(n, r):
-        row = xh * 4 + lax.rem(y + 4 - r, 4)
-        src = half(n, outs[n], row, xl)
-        copy = remote(src, src, p_send.at[n, r], p_recv.at[n, r], partner)
+        push_p(u, 0)
+
+    def push_p(u, r):
+        src = half(u, xh * 4 + lax.rem(y + 4 - r, 4), xl)
+        copy = remote(src, src, p_send.at[u, r], p_recv.at[u, r], partner)
         copy.start()
-        p_copies[n, r] = copy
+        p_copies[u, r] = copy
         sent.append(copy)
 
-    def stage_p(n):
+    def stage_p(u):
         for r in ORDER:
-            y_copies[n, r].wait_recv()
-            push_p(n, r)
-
-    def stage_q(n):
+            y_copies[u, r].wait_recv()
+            push_p(u, r)
+
+    def stage_q(u):
         for r in (0, *ORDER):
-            p_copies[n, r].wait_recv()
-            row = (1 - xh) * 4 + lax.rem(y + 4 - r, 4)
-            src = half(n, outs[n], row, 1 - xl)
-            copy = remote(src, src, q_send.at[n, r], q_recv.at[n, r], twin)
+            p_copies[u, r].wait_recv()
+            src = half(u, (1 - xh) * 4 + lax.rem(y + 4 - r, 4), 1 - xl)
+            copy = remote(src, src, q_send.at[u, r], q_recv.at[u, r], twin)
             copy.start()
-            q_copies[n, r] = copy
+            q_copies[u, r] = copy
             sent.append(copy)
 
-    for step in range(8):
-        if step < 6:
+    count = len(GATHER_UNITS)
+    for step in range(count + 4):
+        if step < count:
             stage_y(step)
-        if 0 <= step - 1 < 6:
-            stage_p(step - 1)
-        if 0 <= step - 2 < 6:
-            stage_q(step - 2)
+        if 0 <= step - 2 < count:
+            stage_p(step - 2)
+        if step - 2 == count - 1:
+
+            @pl.when(section == 0)
+            def _():
+                pl.semaphore_signal(go, inc=1, device_id=core, device_id_type=MESH)
+
+        if 0 <= step - 4 < count:
+            stage_q(step - 4)
     for copy in q_copies.values():
         copy.wait_recv()
-
-    @pl.when(section == 0)
-    def _():
-        pl.semaphore_signal(go, inc=1, device_id=core, device_id_type=MESH)
-
     for copy in sent:
         copy.wait_send()
 
@@ -141,6 +165,7 @@
 def gather(a_s, a_in, a_g, a_u, w_o, w_d):
     shape = jax.ShapeDtypeStruct
     dma = pltpu.SemaphoreType.DMA
+    count = len(GATHER_UNITS)
     return pl.pallas_call(
         gather_kernel,
         out_shape=(
@@ -154,8 +179,8 @@
         in_specs=[ANY] * 6,
         out_specs=[ANY] * 6,
         scratch_shapes=[
-            dma((6, 3)), dma((6, 3)), dma((6, 3)), dma((6, 3)),
-            dma((6, 4)), dma((6, 4)), dma((6, 4)), dma((6, 4)),
+            dma((6, 3)), dma((6, 3)), dma((count, 3)), dma((count, 3)),
+            dma((count, 4)), dma((count, 4)), dma((count, 4)), dma((count, 4)),
             dma((6,)), pltpu.SemaphoreType.REGULAR,
         ],
         compiler_params=pltpu.CompilerParams(collective_id=0, has_side_effects=True),
@@ -245,12 +270,32 @@
     def spread(n, buf):
         return {r: remote(buf.at[own], buf.at[own], a_send.at[n, r - 1], a_recv.at[n, r - 1], zs[r]) for r in ORDER}
 
-    def scatter(n):
-        found = {}
-        for r in ORDER:
-            src = part.at[pl.ds(pl.multiple_of(lax.rem(z + r, 4) * 128, 128), 128)]
-            found[r] = remote(src, rr.at[n, r - 1], s_send.at[n, r - 1], s_recv.at[n, r - 1], zs[r])
-        return found
+    def scatter(n, j, r):
+        at = cols(j, 256)
+        src = part.at[pl.ds(pl.multiple_of(lax.rem(z + r, 4) * 128, 128), 128), at]
+        return remote(src, rr.at[n, r - 1, :, at], s_send.at[n, j, r - 1], s_recv.at[n, j, r - 1], zs[r])
+
+    def sum_over_z(n, block):
+        def body(j):
+            part[:, cols(j, 256)] = block(j).astype(BF16)
+            for r in ORDER:
+                scatter(n, j, r).start()
+
+        loop(6, body)
+
+    def sum_arrived(n):
+        def body(j):
+            for r in ORDER:
+                scatter(n, j, r).wait_recv()
+
+        loop(6, body)
+
+    def sum_sent(n):
+        def body(j):
+            for r in ORDER:
+                scatter(n, j, r).wait_send()
+
+        loop(6, body)
 
     def summed(n, i):
         at = pl.ds(i * 32, 32)
@@ -331,15 +376,8 @@
 
     loads[1].wait()
 
-    def mix_out(j):
-        part[:, cols(j, 512)] = dot_nn(mx[...], wout[:, cols(j, 512)]).astype(BF16)
-
-    loop(3, mix_out)
-    sums = [scatter(n) for n in range(4)]
-    for r in ORDER:
-        sums[0][r].start()
-    for r in ORDER:
-        sums[0][r].wait_recv()
+    sum_over_z(0, lambda j: dot_nn(mx[...], wout[:, cols(j, 256)]))
+    sum_arrived(0)
 
     def middle(i):
         at = pl.ds(i * 32, 32)
@@ -352,8 +390,7 @@
     loop(4, middle)
     for r in ORDER:
         n_all[r].start()
-    for r in ORDER:
-        sums[0][r].wait_send()
+    sum_sent(0)
     loads[2].wait()
     loads[3].wait()
     for r in ORDER:
@@ -370,14 +407,8 @@
     loop(7, gate)
     loads[4].wait()
 
-    def ffn_out(j):
-        part[:, cols(j, 256)] = dot_nn(hd[...], wd[:, cols(j, 256)]).astype(BF16)
-
-    loop(6, ffn_out)
-    for r in ORDER:
-        sums[1][r].start()
-    for r in ORDER:
-        sums[1][r].wait_recv()
+    sum_over_z(1, lambda j: dot_nn(hd[...], wd[:, cols(j, 256)]))
+    sum_arrived(1)
 
     def finish(i):
         at = pl.ds(i * 32, 32)
@@ -393,8 +424,7 @@
         for r in ORDER:
             e_all[r].start()
 
-    for r in ORDER:
-        sums[1][r].wait_send()
+    sum_sent(1)
     for r in ORDER:
         e_all[r].wait_recv()
 
@@ -408,13 +438,7 @@
 
     loop(7, back_hidden)
 
-    def back_ffn(j):
-        at = cols(j, 256)
-        part[:, at] = (dot_nt(dg[...], wg[at, :]) + dot_nt(du[...], wu[at, :])).astype(BF16)
-
-    loop(6, back_ffn)
-    for r in ORDER:
-        sums[2][r].start()
+    sum_over_z(2, lambda j: dot_nt(dg[...], wg[cols(j, 256), :]) + dot_nt(du[...], wu[cols(j, 256), :]))
 
     def grad_down(j):
         at = cols(j, 256)
@@ -426,8 +450,7 @@
         for n, (src, dst) in enumerate(((win, gin_h), (wout, gout_h), (wg, gg_h), (wu, gu_h), (wd, gd_h)))
     ]
     stores[4].start()
-    for r in ORDER:
-        sums[2][r].wait_recv()
+    sum_arrived(2)
     gffn_ref[...] = jnp.zeros((1, 1536), F32)
     gmix_ref[...] = jnp.zeros((1, 1536), F32)
 
@@ -461,8 +484,7 @@
 
     loop(6, grad_up)
     stores[3].start()
-    for r in ORDER:
-        sums[2][r].wait_send()
+    sum_sent(2)
     for r in ORDER:
         f_all[r].wait_recv()
 
@@ -510,13 +532,7 @@
         dp[r0 : r0 + 64, 0:384] = (total * proj[2, r0 : r0 + 64, :]).astype(BF16)
         dp[r0 : r0 + 64, 768:1152] = (total * proj[0, r0 : r0 + 64, :]).astype(BF16)
 
-    def back_in(j):
-        at = cols(j, 256)
-        part[:, at] = dot_nt(dp[...], win[at, :]).astype(BF16)
-
-    loop(6, back_in)
-    for r in ORDER:
-        sums[3][r].start()
+    sum_over_z(3, lambda j: dot_nt(dp[...], win[cols(j, 256), :]))
 
     def grad_in(j):
         at = cols(j, 256)
@@ -524,8 +540,7 @@
 
     loop(6, grad_in)
     stores[0].start()
-    for r in ORDER:
-        sums[3][r].wait_recv()
+    sum_arrived(3)
 
     def back_input(i):
         at = pl.ds(i * 32, 32)
@@ -559,8 +574,8 @@
     def _():
         to_before.wait_send()
 
+    sum_sent(3)
     for r in ORDER:
-        sums[3][r].wait_send()
         for copies in (x_all, n_all, e_all, f_all):
             copies[r].wait_send()
     for copy in stores:
@@ -597,7 +612,7 @@
             vm((128, 1536), BF16),
             vm((1536, 1152), BF16), vm((384, 1536), BF16), vm((1536, 1792), BF16), vm((1536, 1792), BF16),
             vm((1792, 1536), BF16),
-            dma((5,)), dma((5,)), dma((4, 3)), dma((4, 3)), dma((4, 3)), dma((4, 3)),
+            dma((5,)), dma((5,)), dma((4, 3)), dma((4, 3)), dma((4, 6, 3)), dma((4, 6, 3)),
             dma((2,)), dma((2,)), dma((2,)), dma((2,)), pltpu.SemaphoreType.REGULAR,
         ],
         compiler_params=pltpu.CompilerParams(
@@ -644,109 +659,138 @@
         copies[key] = copy
         sent.append(copy)
 
-    def half(n, ref, first, h):
+    def half(u, ref, first, h):
+        n, c0, size = REDUCE_UNITS[u]
         if n == 3:
             return ref.at[pl.ds(first, 4), :, pl.ds(pl.multiple_of(h * 768, 128), 768)]
-        return ref.at[pl.ds(first, 4), pl.ds(h * 2, 2)]
-
-    def add(n, first, h, other):
+        return ref.at[pl.ds(first, 4), pl.ds(h * 2, 2), :, pl.ds(c0, size)]
+
+    def arrived(u, ref):
+        n, c0, size = REDUCE_UNITS[u]
+        return ref if n == 3 else ref.at[:, :, :, pl.ds(c0, size)]
+
+    def row_of(u, ref, *lead):
+        n, c0, size = REDUCE_UNITS[u]
         if n == 0:
+            return ref.at[*lead, pl.ds(c0, size)]
+        if n == 3:
+            return ref.at[*lead] if lead else ref
+        return ref.at[*lead, :, :, pl.ds(c0, size)]
+
+    def add(u, first, h, other):
+        n, c0, size = REDUCE_UNITS[u]
+        if n == 0:
+            rows = size // 16
+
             def body(i):
-                row, at = i // 7, pl.ds(lax.rem(i, 7) * 32, 32)
-                v_d[first + row, at, :] = (v_d[first + row, at, :].astype(F32) + other[row, at, :].astype(F32)).astype(BF16)
-
-            loop(28, body)
+                row, at = i // rows, pl.ds(pl.multiple_of(c0 + lax.rem(i, rows) * 16, 16), 16)
+                v_d[first + row, at, :] = v_d[first + row, at, :] + other[row, at, :]
+
+            loop(4 * rows, body)
         elif n == 3:
             at = pl.ds(pl.multiple_of(h * 768, 128), 768)
 
             def body(i):
-                v_o[first + i, :, at] = (v_o[first + i, :, at].astype(F32) + other[i].astype(F32)).astype(BF16)
+                v_o[first + i, :, at] = v_o[first + i, :, at] + other[i]
 
             loop(4, body)
         else:
-            ref = held[n]
+            ref, at = held[n], slice(c0, c0 + size)
 
             def body(i):
                 a, b = first + i // 2, h * 2 + lax.rem(i, 2)
-                ref[a, b] = (ref[a, b].astype(F32) + other[i // 2, lax.rem(i, 2)].astype(F32)).astype(ref.dtype)
+                ref[a, b, :, at] = ref[a, b, :, at] + other[i // 2, lax.rem(i, 2), :, at]
 
             loop(8, body)
 
-    def stage_0(n):
-        loads[n].wait()
+    def stage_0(u):
+        n = REDUCE_UNITS[u][0]
+        if n not in ready:
+            ready.add(n)
+            loads[n].wait()
         if n:
-            begin(("q", n), remote(half(n, held[n], far, 1 - xl), from_twin[n], q_send.at[n], q_recv.at[n], twin))
+            dst = arrived(u, from_twin[n])
+            begin(("q", u), remote(half(u, held[n], far, 1 - xl), dst, q_send.at[u], q_recv.at[u], twin))
         else:
-            begin(("p", n), remote(held[n].at[pl.ds(far, 4)], from_partner[n], p_send.at[n], p_recv.at[n], partner))
-
-    def stage_1(n):
+            begin_p(u, held[n].at[pl.ds(far, 4), pl.ds(*REDUCE_UNITS[u][1:])])
+
+    def begin_p(u, src):
+        n, c0, size = REDUCE_UNITS[u]
+        dst = from_partner[n].at[:, pl.ds(c0, size)] if n == 0 else arrived(u, from_partner[n])
+        begin(("p", u), remote(src, dst, p_send.at[u], p_recv.at[u], partner))
+
+    def stage_1(u):
+        n = REDUCE_UNITS[u][0]
         if n:
-            copies["q", n].wait_recv()
-            add(n, far, xl, from_twin[n])
-            begin(("p", n), remote(half(n, held[n], far, xl), from_partner[n], p_send.at[n], p_recv.at[n], partner))
-
-    def stage_2(n):
-        copies["p", n].wait_recv()
-        add(n, near, 1 - xl, from_partner[n])
+            copies["q", u].wait_recv()
+            add(u, far, xl, from_twin[n])
+            begin_p(u, half(u, held[n], far, xl))
+
+    def stage_2(u):
+        n = REDUCE_UNITS[u][0]
+        copies["p", u].wait_recv()
+        add(u, near, 1 - xl, from_partner[n])
         for r in ORDER:
-            row = near + lax.rem(y + r, 4)
-            begin(("y", n, r), remote(held[n].at[row], from_y[n].at[r - 1], y_send.at[n, r - 1], y_recv.at[n, r - 1], ys[r]))
-
-    def pieces(n):
+            src, dst = row_of(u, held[n], near + lax.rem(y + r, 4)), row_of(u, from_y[n], r - 1)
+            begin(("y", u, r), remote(src, dst, y_send.at[u, r - 1], y_recv.at[u, r - 1], ys[r]))
+
+    def blocks(u):
+        n, c0, size = REDUCE_UNITS[u]
         if n == 0:
-            return 7, lambda ref, i: ref[pl.ds(i * 32, 32), :]
+            return size // 16, lambda i: (pl.ds(pl.multiple_of(c0 + i * 16, 16), 16), slice(None))
         if n == 3:
-            return 3, lambda ref, i: ref[pl.ds(i * 16, 16), :]
-        return 4, lambda ref, i: ref[i]
-
-    def put(n, ref, i, value):
-        if n == 0:
-            ref[pl.ds(i * 32, 32), :] = value
-        elif n == 3:
-            ref[pl.ds(i * 16, 16), :] = value
-        else:
-            ref[i] = value
-
-    def stage_3(n):
+            return 3, lambda i: (pl.ds(pl.multiple_of(i * 16, 16), 16), slice(None))
+        return 4, lambda i: (i, slice(None), slice(c0, c0 + size))
+
+    def stage_3(u):
+        n = REDUCE_UNITS[u][0]
         for r in ORDER:
-            copies["y", n, r].wait_recv()
-        count, get = pieces(n)
+            copies["y", u, r].wait_recv()
+        number, at = blocks(u)
 
         def body(i):
-            total = get(held[n].at[me], i).astype(F32)
+            total = held[n][me, *at(i)].astype(F32)
             for r in range(3):
-                total = total + get(from_y[n].at[r], i).astype(F32)
-            put(n, mine[n], i, total.astype(mine[n].dtype))
-
-        loop(count, body)
-        begin(("t", n), remote(mine[n], theirs[n], t_send.at[n], t_recv.at[n], twin))
-
-    def stage_4(n):
-        copies["t", n].wait_recv()
-        count, get = pieces(n)
+                total = total + from_y[n][r, *at(i)].astype(F32)
+            mine[n][at(i)] = total.astype(mine[n].dtype)
+
+        loop(number, body)
+        begin(("t", u), remote(row_of(u, mine[n]), row_of(u, theirs[n]), t_send.at[u], t_recv.at[u], twin))
+
+    def stage_4(u):
+        n, c0, size = REDUCE_UNITS[u]
+        copies["t", u].wait_recv()
+        number, at = blocks(u)
         target = outs[n] if ended[n] is None else ended[n]
 
         def body(i):
-            total = get(mine[n], i).astype(F32) + get(theirs[n], i).astype(F32)
-            put(n, target, i, total.astype(target.dtype))
-
-        loop(count, body)
+            if ended[n] is None:
+                target[at(i)] = mine[n][at(i)].astype(F32) + theirs[n][at(i)].astype(F32)
+            else:
+                target[at(i)] = mine[n][at(i)] + theirs[n][at(i)]
+
+        loop(number, body)
         if ended[n] is not None:
+            part = (slice(None), pl.ds(c0, size))
             for r in ORDER:
-                begin(("z", n, r), remote(target.at[lax.rem(z + r, 4)], outs[n].at[z], z_send.at[n, r - 1], z_recv.at[n, r - 1], zs[r]))
-            copy = pltpu.make_async_copy(target.at[z], outs[n].at[z], keep.at[n])
+                src, dst = target.at[lax.rem(z + r, 4), *part], outs[n].at[z, *part]
+                begin(("z", u, r), remote(src, dst, z_send.at[u, r - 1], z_recv.at[u, r - 1], zs[r]))
+            copy = pltpu.make_async_copy(target.at[z, *part], outs[n].at[z, *part], keep.at[u])
             copy.start()
-            copies["keep", n] = copy
-
+            copies["keep", u] = copy
+
+    ready = set()
+    count = len(REDUCE_UNITS)
     stages = (stage_0, stage_1, stage_2, stage_3, stage_4)
-    for step in range(10):
+    for step in range(count + 8):
         for s, stage in enumerate(stages):
-            if 0 <= step - s < 6:
-                stage(step - s)
-    for n in (1, 2, 4, 5):
-        copies["keep", n].wait()
-        for r in ORDER:
-            copies["z", n, r].wait_recv()
+            if 0 <= step - 2 * s < count:
+                stage(step - 2 * s)
+    for u in range(count):
+        if ("keep", u) in copies:
+            copies["keep", u].wait()
+            for r in ORDER:
+                copies["z", u, r].wait_recv()
     o_s[...] = b_s[0] + b_s[1] + b_s[2] + b_s[3]
     for copy in sent:
         copy.wait_send()
@@ -756,6 +800,7 @@
     shape = jax.ShapeDtypeStruct
     dma = pltpu.SemaphoreType.DMA
     vm = pltpu.VMEM
+    count = len(REDUCE_UNITS)
     big = ((4, 48, 1792), (4, 48, 1792), (4, 48, 1152))
     return pl.pallas_call(
         reduce_kernel,
@@ -783,8 +828,8 @@
             vm((224, 1536), BF16), vm(big[0], BF16), vm(big[1], BF16), vm((48, 1536), BF16), vm(big[2], BF16),
             vm((4, 8, 128), F32),
             vm(big[0], BF16), vm(big[1], BF16), vm(big[2], BF16), vm((4, 8, 128), F32), vm((4, 8, 128), F32),
-            dma((6,)), dma((6,)), dma((6,)), dma((6,)), dma((6,)), dma((6, 3)), dma((6, 3)),
-            dma((6,)), dma((6,)), dma((6, 3)), dma((6, 3)), dma((6,)),
+            dma((6,)), dma((count,)), dma((count,)), dma((count,)), dma((count,)), dma((count, 3)), dma((count, 3)),
+            dma((count,)), dma((count,)), dma((count, 3)), dma((count, 3)), dma((count,)),
         ],
         compiler_params=pltpu.CompilerParams(
             collective_id=2, has_side_effects=True, vmem_limit_bytes=63 * 2**20

time: 580 us -> 505 us (0.87)
  Pallas kernels: 532 us -> 455 us
    pallas_call x1, Pallas kernels: 296 us -> 242 us  [main(): pl.pallas_call(main_kernel, out_shape=(shape((128, 1536), BF16), shape((1...]
    pallas_call x1, Pallas kernels: 129 us -> 116 us  [reduce(): pl.pallas_call(reduce_kernel, out_shape=(shape((224, 1536), F32), shape((...]
    pallas_call x1, Pallas kernels: 107 us -> 96.5 us  [gather(): pl.pallas_call(gather_kernel, out_shape=(shape((8, 4, 16, 128), BF16), sh...]
where the time goes in v2:
time: 505 us; the launch traced here: 503 us
  Pallas kernels  455 us (90%)
  local copies, waits for them, and re-layouts  42.1 us (8%)
    pallas_call x1, Pallas kernels, main(): pl.pallas_call(main_kernel, out_shape=(shape((128, 1536), BF16), shape((1...  242 us
    pallas_call x1, Pallas kernels, reduce(): pl.pallas_call(reduce_kernel, out_shape=(shape((224, 1536), F32), shape((...  116 us
    pallas_call x1, Pallas kernels, gather(): pl.pallas_call(gather_kernel, out_shape=(shape((8, 4, 16, 128), BF16), sh...  96.5 us

profile of v2, /device:TPU:2, one launch (start us, length us, event | category | flops | bytes accessed | tf_op | source)
XLA Modules:
  0.0 503.0 jit_solution(12363473736622293460)
XLA Ops:
  0.6 0.0 copy-start.3
  0.7 1.4 fusion.8.a_s
  2.0 2.0 pad.22.w_d
  4.0 0.0 copy-done.3
  4.0 2.4 reshape_squeeze.6
  6.4 0.1 copy.30
  6.5 0.0 copy-start.4
  6.5 0.1 pad_bitcast_fusion.1
  6.7 1.8 reshape.153.a_g
  8.5 0.0 copy-done.4
  8.5 2.4 reshape_squeeze.7
  10.9 0.1 copy.31
  11.0 0.0 copy-start.5
  11.0 0.1 pad_bitcast_fusion
  11.2 1.8 reshape.154.a_u
  13.0 0.0 copy-done.5
  13.0 1.2 reshape.151
  14.2 0.2 copy.41
  14.3 1.7 reshape.152.a_in
  16.0 96.5 %gather_weights.1 = (bf16[8,4,16,128]{3,2,1,0:T(8,128)(2,1)}, bf16[8,4,48,1152]{3,2,1,0:T(8,128)(2,1)}, bf16[8,48,1536]{2,1,0:T(8,128)(2,1)}, bf16[8,4,48,1792]{...) custom-call(bf16[16,128]{1,0:T(8,128)(2,1)} %fusion.8.a_s, ...), custom_call_target="tpu_custom_call" | custom-call | tf_op jit(solution)/shard_map/gather_weights/pallas_call | solution.py:169
  112.5 0.8 dynamic-slice_bitcast_fusion
  113.2 0.9 convert_bitcast_fusion.2
  114.1 0.7 reshape.177.taps
  114.8 0.7 reshape.175.gains
  115.5 242.3 %two_blocks.1 = (bf16[128,1536]{1,0:T(8,128)(2,1)}, f32[128,1536]{1,0:T(8,128)}, bf16[1536,1152]{1,0:T(8,128)(2,1)}, bf16[384,1536]{1,0:T(8,128)(2,1)}, bf16[153...) custom-call(bf16[128,1536]{1,0:T(8,128)(2,1)} %bitcast.64, ...), custom_call_target="tpu_custom_call" | custom-call | tf_op jit(solution)/shard_map/two_blocks/pallas_call | solution.py:589
  357.8 0.7 reduce
  358.6 0.7 reduce.1
  359.3 0.1 stack_reshape.7
  359.4 0.1 stack_reshape.6
  359.5 0.8 reshape.171
  360.2 0.1 broadcast_multiply_fusion
  360.3 0.7 select_maximum_fusion.g_s
  361.1 116.5 %reduce_grads.1 = (f32[224,1536]{1,0:T(8,128)}, bf16[4,48,1792]{2,1,0:T(8,128)(2,1)}, bf16[4,48,1792]{2,1,0:T(8,128)(2,1)}, f32[48,1536]{1,0:T(8,128)}, bf16[4,48,1152]{2,1,0:T(8,128)(2,1)}, /*index=5*/f32[8,128]{1,0:T(8,128)}) custom-call(bf16[8,224,1536]{2,1,0:T(8,128)(2,1)} %bitcast.52, bf16[8,4,48,1792]{3,2,1,0:T(8,128)(2,1)} %bitcast.50, ...), custom_call_target="tpu_custom_call" | custom-call | tf_op jit(solution)/shard_map/reduce_grads/pallas_call | solution.py:805
  477.6 1.3 fusion.9
  478.8 0.7 slice_bitcast_fusion.1
  479.5 0.6 copy.38
  480.1 2.5 reshape.172
  482.5 0.1 convert_bitcast_fusion.1
  482.7 1.0 copy.36
  483.7 0.0 copy-start.2
  483.7 2.6 reshape.179
  486.3 0.0 copy-done.2
  486.3 1.1 reshape.173
  487.5 0.1 convert_bitcast_fusion
  487.6 1.0 copy.37
  488.6 0.0 copy-start
  488.6 2.6 reshape.180
  491.2 0.0 copy-done
  491.2 0.0 copy-start.6
  491.2 1.1 slice_bitcast_fusion
  492.4 0.0 copy-done.6
  492.4 1.0 reshape.183
  493.4 2.9 copy.35
  496.3 0.0 copy-start.7
  496.3 0.0 copy-start.1
  496.3 4.3 reshape.178
  500.7 0.0 copy-done.7
  500.7 0.0 copy-start.8
  500.7 0.7 copy.46
  501.4 0.0 copy-done.1
  501.4 0.9 copy.47
  502.3 0.0 copy-done.8
  502.3 0.7 copy.48
  (5 shorter events, 0.0 us)
Async XLA Ops:
  0.6 3.4 copy-start.3
  6.5 2.0 copy-start.4
  11.0 2.0 copy-start.5
  483.7 2.6 copy-start.2
  488.6 2.6 copy-start
  491.2 1.2 copy-start.6
  496.3 4.3 copy-start.7
  496.3 5.1 %copy-start.1 = (f32[128,1536]{1,0:T(8,128)S(1)}, f32[128,1536]{1,0:T(8,128)}, u32[]{:S(2)}) copy-start(f32[128,1536]{1,0:T(8,128)} %get-tuple-element.39) | copy-start | bytes 2359300
  500.7 1.6 copy-start.8

commit v3 on v2

v3 whole, which is shorter than its diff:
```python
import functools

import jax
import jax.numpy as jnp
from jax import lax
from jax.experimental import pallas as pl
from jax.experimental.pallas import tpu as pltpu
from jax.sharding import Mesh
from jax.sharding import PartitionSpec as P

F32, BF16 = jnp.float32, jnp.bfloat16
MESH = pl.DeviceIdType.MESH
EPS = 1e-06
ANY = pl.BlockSpec(memory_space=pl.ANY)
VMEM = pl.BlockSpec(memory_space=pltpu.VMEM)
ORDER = (1, 3, 2)

GATHER_UNITS = (
    (0, 0, 128), (1, 0, 1152), (2, 0, 1536),
    (3, 0, 640), (4, 0, 640), (3, 640, 640), (4, 640, 640), (3, 1280, 512), (4, 1280, 512),
    (5, 0, 80), (5, 80, 80), (5, 160, 64),
)
REDUCE_UNITS = (
    (0, 0, 80), (0, 80, 80), (0, 160, 64),
    (1, 0, 640), (1, 640, 640), (1, 1280, 512), (2, 0, 640), (2, 640, 640), (2, 1280, 512),
    (3, 0, 1536), (4, 0, 640), (4, 640, 512), (5, 0, 128),
)


def place():
    return tuple(lax.axis_index(name) for name in ("section", "xl", "xh", "y", "z"))


def barrier_all(devices):
    barrier = pltpu.get_barrier_semaphore()
    for device in devices:
        pl.semaphore_signal(barrier, inc=1, device_id=device, device_id_type=MESH)
    pl.semaphore_wait(barrier, len(devices))


def remote(src, dst, send, recv, device):
    return pltpu.make_async_remote_copy(
        src_ref=src, dst_ref=dst, send_sem=send, recv_sem=recv, device_id=device, device_id_type=MESH
    )


def plane_peers():
    section, xl, xh, y, z = place()
    partner = {"xh": 1 - xh, "xl": 1 - xl}
    twin = {"xl": 1 - xl}
    zs = {r: {"z": lax.rem(z + r, 4)} for r in ORDER}
    ys = {r: {"y": lax.rem(y + r, 4)} for r in ORDER}
    return partner, twin, zs, ys


def dot_nn(a, b):
    return lax.dot_general(a, b, (((1,), (0,)), ((), ())), preferred_element_type=F32)


def dot_nt(a, b):
    return lax.dot_general(a, b, (((1,), (1,)), ((), ())), preferred_element_type=F32)


def dot_tn(a, b):
    return lax.dot_general(a, b, (((0,), (0,)), ((), ())), preferred_element_type=F32)


def cols(j, width):
    return pl.ds(pl.multiple_of(j * width, width), width)


def loop(count, body):
    def step(j, carry):
        body(j)
        return carry

    lax.fori_loop(0, count, step, 0)


def blocks_kernel(
    x_ref, cot_ref, small, w_in, w_out, w_gate, w_up, w_down,
    y_ref, gx_ref, gin_h, gout_h, gg_h, gu_h, gd_h, gs_ref,
    xa, xn, n2, ea, fa, part, rr, proj, ge, dce, cv, ha, hb, mx, gt, up, hd, dg, du,
    mid, dmid, dp, g0, win, wout, wg, wu, wd, sm, gains, taps, gtap, ggain,
    store, a_send, a_recv, s_send, s_recv, h_send, h_recv, c_send, c_recv,
    z_send, z_recv, y_send, y_recv, p_send, p_recv, q_send, q_recv, go,
):
    section, xl, xh, y, z = place()
    partner, twin, zs, ys = plane_peers()
    core = {"section": 1 - section}
    group = xl * 8 + xh * 4 + y
    after, before = lax.rem(group + 1, 16), lax.rem(group + 15, 16)
    has_after, has_before = group < 15, group > 0

    def at_group(g):
        return {"xl": g // 8, "xh": lax.rem(g // 4, 2), "y": lax.rem(g, 4)}

    barrier = pltpu.get_barrier_semaphore()

    def hail(device):
        pl.semaphore_signal(barrier, inc=1, device_id=device, device_id_type=MESH)

    for device in (partner, twin, core, *zs.values(), *ys.values()):
        hail(device)

    @pl.when(has_after)
    def _():
        hail(at_group(after))

    @pl.when(has_before)
    def _():
        hail(at_group(before))

    me = xh * 4 + y
    weights = (sm, win, wout, wg, wu, wd)
    cut = (None, dp, None, hd, dg, None)
    rows = (32, 192, 48, 192, 192, 224)
    cut_conv(w_in, dp)
    wout[pl.ds(pl.multiple_of(me * 48, 16), 48), :] = w_out[...]
    pl.semaphore_wait(barrier, 10 - (group + 1) // 16 + (group + 15) // 16)

    def of_z(n, ref, first, zz):
        size = rows[n] // 4
        return ref.at[pl.ds(pl.multiple_of(first + zz * size, 8 if n == 0 else 16), size)]

    def rows_q(n, q):
        return pl.multiple_of(q * rows[n], 8 if n == 0 else 16)

    sent, z_copies = [], {}

    def push_z(n):
        size = rows[n] // 4
        for r in ORDER:
            src = small if n == 0 else of_z(n, cut[n], 0, lax.rem(z + r, 4))
            dst = of_z(n, weights[n], me * rows[n], z)
            copy = remote(src, dst, z_send.at[n, r - 1], z_recv.at[n, r - 1], zs[r])
            copy.start()
            z_copies[n, r] = copy
            sent.append(copy)
        mine = pl.ds(pl.multiple_of(me * rows[n] + z * size, 8 if n == 0 else 16), size)
        if n == 0:
            sm[mine, :] = small[...]
        else:
            weights[n][mine, :] = cut[n][pl.ds(pl.multiple_of(z * size, 16), size), 0 : weights[n].shape[1]]

    @pl.when(section == 1)
    def _():
        pl.semaphore_wait(go, 1)

    def own_rows(mb):
        return pl.ds(pl.multiple_of(mb * 256 + z * 64, 64), 64)

    def spread(n, buf, mb):
        at = buf.at[own_rows(mb)]
        return [remote(at, at, a_send.at[n, mb, r - 1], a_recv.at[n, mb, r - 1], zs[r]) for r in ORDER]

    x_all, n_all, e_all, f_all = ([spread(n, buf, mb) for mb in range(2)] for n, buf in enumerate((xa, n2, ea, fa)))

    def begin(copies):
        for copy in copies:
            copy.start()

    def arrived(copies):
        for copy in copies:
            copy.wait_recv()

    mb_rows = [slice(0, 256), slice(256, 512)]
    core_x, core_g = [], []
    for mb in range(2):
        at = pl.ds(mb * 64, 64)
        core_x.append(remote(y_ref.at[at], xa.at[own_rows(mb)], c_send.at[0, mb], c_recv.at[0, mb], core))
        core_g.append(remote(g0.at[at], ea.at[own_rows(mb)], c_send.at[1, mb], c_recv.at[1, mb], core))

    push_z(0)
    push_z(1)

    @pl.when(section == 0)
    def _():
        for mb in range(2):
            xa[own_rows(mb), :] = x_ref[mb * 64 : mb * 64 + 64, :]
            begin(x_all[mb])

    @pl.when(section == 1)
    def _():
        for mb in range(2):
            ea[own_rows(mb), :] = cot_ref[mb * 64 : mb * 64 + 64, :]
            begin(e_all[mb])

    cut_ffn(w_gate, hd)
    push_z(3)
    cut_ffn(w_up, dg)
    push_z(4)
    first_d = pl.multiple_of(me * 224, 16)
    wd[pl.ds(first_d, 224), :] = jnp.concatenate([w_down[...], jnp.zeros((8, 1536), BF16)], axis=0)

    def piece(u, q):
        n, first, size = GATHER_UNITS[u]
        if n == 5:
            return wd.at[pl.ds(pl.multiple_of(q * 224 + first, 16), size)]
        if n == 2:
            return wout.at[pl.ds(rows_q(2, q), 48)]
        return weights[n].at[pl.ds(rows_q(n, q), rows[n]), pl.ds(first, size)]

    def half(u, q, h):
        n, first, size = GATHER_UNITS[u]
        if n in (2, 5):
            left = pl.ds(pl.multiple_of(h * 768, 128), 768)
            if n == 5:
                return wd.at[pl.ds(pl.multiple_of(q * 224 + first, 16), size), left]
            return wout.at[pl.ds(rows_q(2, q), 48), left]
        part_rows = rows[n] // 2
        return weights[n].at[
            pl.ds(pl.multiple_of(q * rows[n] + h * part_rows, 8 if n == 0 else 16), part_rows), pl.ds(first, size)
        ]

    y_copies, p_copies, q_copies, started = {}, {}, {}, set()

    def stage_y(u):
        n = GATHER_UNITS[u][0]
        if n not in started:
            started.add(n)
            if n not in (2, 5):
                for r in ORDER:
                    z_copies[n, r].wait_recv()
        for r in ORDER:
            src = piece(u, me)
            copy = remote(src, src, y_send.at[u, r - 1], y_recv.at[u, r - 1], ys[r])
            copy.start()
            y_copies[u, r] = copy
            sent.append(copy)
        push_p(u, 0)

    def push_p(u, r):
        src = half(u, xh * 4 + lax.rem(y + 4 - r, 4), xl)
        copy = remote(src, src, p_send.at[u, r], p_recv.at[u, r], partner)
        copy.start()
        p_copies[u, r] = copy
        sent.append(copy)

    def stage_p(u):
        for r in ORDER:
            y_copies[u, r].wait_recv()
            push_p(u, r)

    def stage_q(u):
        for r in (0, *ORDER):
            p_copies[u, r].wait_recv()
            src = half(u, (1 - xh) * 4 + lax.rem(y + 4 - r, 4), 1 - xl)
            copy = remote(src, src, q_send.at[u, r], q_recv.at[u, r], twin)
            copy.start()
            q_copies[u, r] = copy
            sent.append(copy)

    def need(n):
        for u, unit in enumerate(GATHER_UNITS):
            if unit[0] == n:
                for r in (0, *ORDER):
                    q_copies[u, r].wait_recv()

    def scatter(n, mb, j, r):
        at = cols(j, 512)
        src = part.at[pl.ds(pl.multiple_of(mb * 256 + lax.rem(z + r, 4) * 64, 64), 64), at]
        dst = rr.at[n, r - 1, pl.ds(mb * 64, 64), at]
        return remote(src, dst, s_send.at[n, mb, j, r - 1], s_recv.at[n, mb, j, r - 1], zs[r])

    def sum_over_z(n, mb, block):
        def body(j):
            part[mb_rows[mb], cols(j, 512)] = block(cols(j, 512)).astype(BF16)
            for r in ORDER:
                scatter(n, mb, j, r).start()

        loop(3, body)

    def sum_arrived(n, mb):
        def body(j):
            for r in ORDER:
                scatter(n, mb, j, r).wait_recv()

        loop(3, body)

    def sum_sent(n, mb):
        def body(j):
            for r in ORDER:
                scatter(n, mb, j, r).wait_send()

        loop(3, body)

    def summed(n, at, mine):
        total = part[mine, :].astype(F32)
        for r in range(3):
            total = total + rr[n, r, at, :].astype(F32)
        return total

    def own_blocks(mb, body):
        def step(i):
            at = pl.ds(pl.multiple_of(mb * 64 + i * 32, 32), 32)
            mine = pl.ds(pl.multiple_of(mb * 256 + z * 64 + i * 32, 32), 32)
            body(at, mine)

        loop(2, step)

    def rms(values):
        return lax.rsqrt(jnp.mean(values * values, axis=-1, keepdims=True) + EPS)

    def take_input():
        for f in range(32):
            gains[0:2, 48 * f : 48 * f + 48] = sm[8 * f + 3 : 8 * f + 5, 0:48]
        for q in range(8):
            taps[0:3, 48 * q : 48 * q + 48] = sm[pl.ds(pl.multiple_of(q * 32 + z * 8, 8), 8), :][0:3, 0:48]

    halo_after = [
        remote(ge.at[mb, pl.ds(256, 8)], ha.at[mb], h_send.at[0, mb], h_recv.at[0, mb], at_group(after)) for mb in range(2)
    ]
    halo_before = [
        remote(dce.at[mb, pl.ds(0, 8)], hb.at[mb], h_send.at[1, mb], h_recv.at[1, mb], at_group(before)) for mb in range(2)
    ]

    def project(mb):
        arrived(x_all[mb])

        def norm(i):
            at = pl.ds(pl.multiple_of(mb * 256 + i * 32, 32), 32)
            values = xa[at, :].astype(F32)
            xn[at, :] = (values * rms(values) * gains[0:1, :]).astype(BF16)

        loop(8, norm)

        def body(j):
            proj[j, mb_rows[mb], :] = dot_nn(xn[mb_rows[mb], :], win[:, cols(j, 384)])

        loop(3, body)
        ge[mb, 8:264, :] = proj[0, mb_rows[mb], :] * proj[2, mb_rows[mb], :]

        @pl.when(has_after)
        def _():
            halo_after[mb].start()

    def tap(k):
        return taps[k : k + 1, :]

    def mix(mb):
        @pl.when(has_before)
        def _():
            halo_after[mb].wait_recv()
            ge[mb, 0:8, :] = ha[mb]

        @pl.when(jnp.logical_not(has_before))
        def _():
            ge[mb, 0:8, :] = jnp.zeros((8, 384), F32)

        for zc in range(4):
            t0, at = 8 + 64 * zc, slice(mb * 256 + 64 * zc, mb * 256 + 64 * zc + 64)
            total = tap(0) * ge[mb, t0 : t0 + 64, :]
            for k in (1, 2):
                total = total + tap(k) * ge[mb, t0 - k : t0 - k + 64, :]
            cv[at, :] = total
            mx[at, :] = (proj[1, at, :] * total).astype(BF16)
        sum_over_z(0, mb, lambda at: dot_nn(mx[mb_rows[mb], :], wout[:, at]))

    def middle(mb):
        sum_arrived(0, mb)

        def body(at, mine):
            values = xa[mine, :].astype(F32) + summed(0, at, mine)
            mid[at, :] = values
            n2[mine, :] = (values * rms(values) * gains[1:2, :]).astype(BF16)

        own_blocks(mb, body)
        begin(n_all[mb])

    def gate(mb):
        arrived(n_all[mb])

        def body(j):
            at = cols(j, 256)
            gating = dot_nn(n2[mb_rows[mb], :], wg[:, at])
            up_part = dot_nn(n2[mb_rows[mb], :], wu[:, at])
            gt[mb_rows[mb], at] = gating
            up[mb_rows[mb], at] = up_part
            hd[mb_rows[mb], at] = (gating * jax.nn.sigmoid(gating) * up_part).astype(BF16)

        loop(7, body)

    def down(mb):
        sum_sent(0, mb)
        sum_over_z(1, mb, lambda at: dot_nn(hd[mb_rows[mb], :], wd[:, at]))

    def finish(mb):
        sum_arrived(1, mb)

        def body(at, mine):
            y_ref[at, :] = (mid[at, :] + summed(1, at, mine)).astype(BF16)

        own_blocks(mb, body)

        @pl.when(section == 0)
        def _():
            core_x[mb].start()

    def wait_x():
        @pl.when(section == 1)
        def _():
            for mb in range(2):
                core_x[mb].wait_recv()
                begin(x_all[mb])

    def free_cuts():
        for n in (1, 3, 4):
            for r in ORDER:
                z_copies[n, r].wait_send()

    def both(stage):
        stage(0)
        stage(1)

    def forward_1():
        need(0)
        take_input()
        need(1)
        wait_x()
        both(project)

    def forward_2():
        need(2)
        both(mix)

    def forward_3():
        both(middle)

    def forward_4():
        need(3)
        need(4)
        free_cuts()
        both(gate)

    def forward_5():
        need(5)
        both(down)

    segments = {5: forward_1, 7: forward_2, 9: forward_3, 13: forward_4}
    count = len(GATHER_UNITS)
    for step in range(count + 4):
        if step < count:
            stage_y(step)
        if 0 <= step - 2 < count:
            stage_p(step - 2)
        if step - 2 == count - 1:

            @pl.when(section == 0)
            def _():
                pl.semaphore_signal(go, inc=1, device_id=core, device_id_type=MESH)

        if 0 <= step - 4 < count:
            stage_q(step - 4)
        if step in segments:
            pl.when(section == 0)(segments[step])

    @pl.when(section == 1)
    def _():
        for segment in segments.values():
            segment()

    forward_5()
    both(finish)
    for copy in sent:
        if not any(copy is z_copies[n, r] for n in (1, 3, 4) for r in ORDER):
            copy.wait_send()

    ggain[...] = jnp.zeros((2, 1536), F32)

    def take_gradient(mb):
        @pl.when(section == 0)
        def _():
            core_g[mb].wait_recv()
            begin(e_all[mb])

    def back_hidden(mb):
        arrived(e_all[mb])

        def body(j):
            at = cols(j, 256)
            dh = dot_nt(ea[mb_rows[mb], :], wd[at, :])
            gating, up_part = gt[mb_rows[mb], at], up[mb_rows[mb], at]
            sg = jax.nn.sigmoid(gating)
            dg[mb_rows[mb], at] = (dh * up_part * sg * (1.0 + gating * (1.0 - sg))).astype(BF16)
            du[mb_rows[mb], at] = (dh * gating * sg).astype(BF16)

        loop(7, body)

    def back_ffn(mb):
        sum_sent(1, mb)
        sum_over_z(2, mb, lambda at: dot_nt(dg[mb_rows[mb], :], wg[at, :]) + dot_nt(du[mb_rows[mb], :], wu[at, :]))

    def back_middle(mb):
        sum_arrived(2, mb)

        def body(at, mine):
            dn2 = summed(2, at, mine)
            values = mid[at, :]
            scale = rms(values)
            weighted = dn2 * gains[1:2, :]
            mean_term = jnp.mean(weighted * values, axis=-1, keepdims=True)
            grad = ea[mine, :].astype(F32) + scale * weighted - values * (scale * scale * scale) * mean_term
            ggain[1:2, :] += jnp.sum(dn2 * values * scale, axis=0, keepdims=True)
            dmid[at, :] = grad
            fa[mine, :] = grad.astype(BF16)

        own_blocks(mb, body)
        begin(f_all[mb])

    def back_mix(mb):
        arrived(f_all[mb])
        dce[mb, 0:256, :] = dot_nt(fa[mb_rows[mb], :], wout[...])
        for zc in range(4):
            at, here = slice(mb * 256 + 64 * zc, mb * 256 + 64 * zc + 64), slice(64 * zc, 64 * zc + 64)
            dm = dce[mb, here, :]
            dp[at, 384:768] = (dm * cv[at, :]).astype(BF16)
            dce[mb, here, :] = dm * proj[1, at, :]

        @pl.when(has_before)
        def _():
            halo_before[mb].start()

    def back_conv(mb):
        @pl.when(has_after)
        def _():
            halo_before[mb].wait_recv()
            dce[mb, 256:264, :] = hb[mb]

        @pl.when(jnp.logical_not(has_after))
        def _():
            dce[mb, 256:264, :] = jnp.zeros((8, 384), F32)

        for zc in range(4):
            at, t0 = slice(mb * 256 + 64 * zc, mb * 256 + 64 * zc + 64), 64 * zc
            total = tap(0) * dce[mb, t0 : t0 + 64, :]
            for k in (1, 2):
                total = total + tap(k) * dce[mb, t0 + k : t0 + k + 64, :]
            dp[at, 0:384] = (total * proj[2, at, :]).astype(BF16)
            dp[at, 768:1152] = (total * proj[0, at, :]).astype(BF16)

    def back_in(mb):
        sum_sent(2, mb)
        sum_over_z(3, mb, lambda at: dot_nt(dp[mb_rows[mb], :], win[at, :]))

    def back_input(mb):
        sum_arrived(3, mb)

        def body(at, mine):
            dn = summed(3, at, mine)
            values = xa[mine, :].astype(F32)
            scale = rms(values)
            weighted = dn * gains[0:1, :]
            mean_term = jnp.mean(weighted * values, axis=-1, keepdims=True)
            grad = dmid[at, :] + scale * weighted - values * (scale * scale * scale) * mean_term
            ggain[0:1, :] += jnp.sum(dn * values * scale, axis=0, keepdims=True)
            gx_ref[at, :] = grad
            g0[at, :] = grad.astype(BF16)

        own_blocks(mb, body)

        @pl.when(section == 1)
        def _():
            core_g[mb].start()

    stores = [
        pltpu.make_async_copy(src, dst, store.at[n])
        for n, (src, dst) in enumerate(((win, gin_h), (wout, gout_h), (wg, gg_h), (wu, gu_h), (wd, gd_h)))
    ]

    def grad(n, width, left, right):
        target = (win, wout, wg, wu, wd)[n]

        def body(j):
            at = cols(j, width)
            target[at, :] = dot_tn(left[:, at], right[...]).astype(BF16)

        loop(target.shape[0] // width, body)
        stores[n].start()

    both(take_gradient)
    both(lambda mb: (back_hidden(mb), back_ffn(mb)))
    grad(4, 256, hd, ea)
    back_middle(0)
    grad(2, 256, n2, dg)
    back_middle(1)
    grad(3, 256, n2, du)
    both(back_mix)
    grad(1, 128, mx, fa)
    for k in range(3):
        total = jnp.zeros((1, 384), F32)
        for mb in range(2):
            for zc in range(4):
                t0 = 8 + 64 * zc - k
                products = dce[mb, 64 * zc : 64 * zc + 64, :] * ge[mb, t0 : t0 + 64, :]
                total = total + jnp.sum(products, axis=0, keepdims=True)
        gtap[k : k + 1, :] = total
    both(lambda mb: (back_conv(mb), back_in(mb)))
    grad(0, 256, xn, dp)
    both(back_input)

    gs_ref[...] = jnp.zeros((256, 128), F32)
    for q in range(8):
        at = pl.ds(pl.multiple_of(q * 32 + z * 8, 8), 8)
        gs_ref[at, 0:48] = gtap[:, 48 * q : 48 * q + 48]
    for f in range(32):
        gs_ref[8 * f + 3 : 8 * f + 5, 0:48] = ggain[0:2, 48 * f : 48 * f + 48]

    for mb in range(2):

        @pl.when(section == 1)
        def _():
            core_g[mb].wait_send()

        @pl.when(section == 0)
        def _():
            core_x[mb].wait_send()

        @pl.when(has_after)
        def _():
            halo_after[mb].wait_send()

        @pl.when(has_before)
        def _():
            halo_before[mb].wait_send()

        sum_sent(3, mb)
        for copies in (x_all, n_all, e_all, f_all):
            for copy in copies[mb]:
                copy.wait_send()
    for copy in stores:
        copy.wait()


def cut_conv(weight, out):
    for q in range(8):
        for zz in range(4):
            for part in range(3):
                first, to = part * 1536 + (4 * q + zz) * 48, part * 384 + q * 48
                out[zz * 48 : zz * 48 + 48, to : to + 48] = weight[:, first : first + 48]


def cut_ffn(weight, out):
    for zz in range(4):
        for q in range(8):
            first = (4 * q + zz) * 216
            out[zz * 48 : zz * 48 + 48, 224 * q : 224 * q + 216] = weight[:, first : first + 216]
            out[zz * 48 : zz * 48 + 48, 224 * q + 216 : 224 * q + 224] = jnp.zeros((48, 8), BF16)


def run_blocks(x, cot, small, w_in, w_out, w_gate, w_up, w_down):
    shape = jax.ShapeDtypeStruct
    dma = pltpu.SemaphoreType.DMA
    vm = pltpu.VMEM
    count = len(GATHER_UNITS)
    return pl.pallas_call(
        blocks_kernel,
        out_shape=(
            shape((128, 1536), BF16),
            shape((128, 1536), F32),
            shape((1536, 1152), BF16),
            shape((384, 1536), BF16),
            shape((1536, 1792), BF16),
            shape((1536, 1792), BF16),
            shape((1792, 1536), BF16),
            shape((256, 128), F32),
        ),
        in_specs=[VMEM] * 8,
        out_specs=[VMEM] * 2 + [ANY] * 5 + [VMEM],
        scratch_shapes=[
            vm((512, 1536), BF16), vm((512, 1536), BF16), vm((512, 1536), BF16), vm((512, 1536), BF16),
            vm((512, 1536), BF16), vm((512, 1536), BF16), vm((4, 3, 128, 1536), BF16),
            vm((3, 512, 384), F32), vm((2, 264, 384), F32), vm((2, 264, 384), F32), vm((512, 384), F32),
            vm((2, 8, 384), F32), vm((2, 8, 384), F32), vm((512, 384), BF16),
            vm((512, 1792), F32), vm((512, 1792), F32), vm((512, 1792), BF16), vm((512, 1792), BF16),
            vm((512, 1792), BF16), vm((128, 1536), F32), vm((128, 1536), F32), vm((512, 1152), BF16),
            vm((128, 1536), BF16),
            vm((1536, 1152), BF16), vm((384, 1536), BF16), vm((1536, 1792), BF16), vm((1536, 1792), BF16),
            vm((1792, 1536), BF16), vm((256, 128), F32), vm((8, 1536), F32), vm((8, 384), F32), vm((8, 384), F32),
            vm((2, 1536), F32),
            dma((5,)), dma((4, 2, 3)), dma((4, 2, 3)), dma((4, 2, 3, 3)), dma((4, 2, 3, 3)),
            dma((2, 2)), dma((2, 2)), dma((2, 2)), dma((2, 2)),
            dma((5, 3)), dma((5, 3)), dma((count, 3)), dma((count, 3)), dma((count, 4)), dma((count, 4)),
            dma((count, 4)), dma((count, 4)), pltpu.SemaphoreType.REGULAR,
        ],
        compiler_params=pltpu.CompilerParams(
            collective_id=1, has_side_effects=True, vmem_limit_bytes=63 * 2**20
        ),
        name="two_blocks",
    )(x, cot, small, w_in, w_out, w_gate, w_up, w_down)


def reduce_kernel(
    g_d, g_g, g_u, g_o, g_in, g_s,
    o_d, o_g, o_u, o_o, o_in, o_s,
    v_d, v_g, v_u, v_o, v_in, v_s,
    q1_g, q1_u, q1_o, q1_in, q1_s,
    p_d, p_g, p_u, p_o, p_in, p_s,
    y_d, y_g, y_u, y_o, y_in, y_s,
    f_d, f_g, f_u, f_o, f_in, f_s,
    t_d, t_g, t_u, t_o, t_in, t_s,
    e_g, e_u, e_in, e_s, l_d, l_g, l_u, l_in, b_s,
    load, q_send, q_recv, p_send, p_recv, y_send, y_recv, t_send, t_recv, z_send, z_recv, keep,
):
    section, xl, xh, y, z = place()
    partner, twin, zs, ys = plane_peers()
    grads = (g_d, g_g, g_u, g_o, g_in, g_s)
    held = (v_d, v_g, v_u, v_o, v_in, v_s)
    from_twin = (None, q1_g, q1_u, q1_o, q1_in, q1_s)
    from_partner = (p_d, p_g, p_u, p_o, p_in, p_s)
    from_y = (y_d, y_g, y_u, y_o, y_in, y_s)
    mine = (f_d, f_g, f_u, f_o, f_in, f_s)
    theirs = (t_d, t_g, t_u, t_o, t_in, t_s)
    ended = (None, e_g, e_u, None, e_in, e_s)
    outs = (l_d, l_g, l_u, o_o, l_in, b_s)
    loads = [pltpu.make_async_copy(grads[n], held[n], load.at[n]) for n in range(6)]
    for copy in loads:
        copy.start()
    barrier_all([partner, twin, *zs.values(), *ys.values()])
    near, far = xh * 4, (1 - xh) * 4
    me = near + y
    sent = []
    copies = {}

    def begin(key, copy):
        copy.start()
        copies[key] = copy
        sent.append(copy)

    def half(u, ref, first, h):
        n, c0, size = REDUCE_UNITS[u]
        if n == 3:
            return ref.at[pl.ds(first, 4), :, pl.ds(pl.multiple_of(h * 768, 128), 768)]
        return ref.at[pl.ds(first, 4), pl.ds(h * 2, 2), :, pl.ds(c0, size)]

    def arrived(u, ref):
        n, c0, size = REDUCE_UNITS[u]
        return ref if n == 3 else ref.at[:, :, :, pl.ds(c0, size)]

    def row_of(u, ref, *lead):
        n, c0, size = REDUCE_UNITS[u]
        if n == 0:
            return ref.at[*lead, pl.ds(c0, size)]
        if n == 3:
            return ref.at[*lead] if lead else ref
        return ref.at[*lead, :, :, pl.ds(c0, size)]

    def add(u, first, h, other):
        n, c0, size = REDUCE_UNITS[u]
        if n == 0:
            rows = size // 16

            def body(i):
                row, at = i // rows, pl.ds(pl.multiple_of(c0 + lax.rem(i, rows) * 16, 16), 16)
                v_d[first + row, at, :] = v_d[first + row, at, :] + other[row, at, :]

            loop(4 * rows, body)
        elif n == 3:
            at = pl.ds(pl.multiple_of(h * 768, 128), 768)

            def body(i):
                v_o[first + i, :, at] = v_o[first + i, :, at] + other[i]

            loop(4, body)
        else:
            ref, at = held[n], slice(c0, c0 + size)

            def body(i):
                a, b = first + i // 2, h * 2 + lax.rem(i, 2)
                ref[a, b, :, at] = ref[a, b, :, at] + other[i // 2, lax.rem(i, 2), :, at]

            loop(8, body)

    def stage_0(u):
        n = REDUCE_UNITS[u][0]
        if n not in ready:
            ready.add(n)
            loads[n].wait()
        if n:
            dst = arrived(u, from_twin[n])
            begin(("q", u), remote(half(u, held[n], far, 1 - xl), dst, q_send.at[u], q_recv.at[u], twin))
        else:
            begin_p(u, held[n].at[pl.ds(far, 4), pl.ds(*REDUCE_UNITS[u][1:])])

    def begin_p(u, src):
        n, c0, size = REDUCE_UNITS[u]
        dst = from_partner[n].at[:, pl.ds(c0, size)] if n == 0 else arrived(u, from_partner[n])
        begin(("p", u), remote(src, dst, p_send.at[u], p_recv.at[u], partner))

    def stage_1(u):
        n = REDUCE_UNITS[u][0]
        if n:
            copies["q", u].wait_recv()
            add(u, far, xl, from_twin[n])
            begin_p(u, half(u, held[n], far, xl))

    def stage_2(u):
        n = REDUCE_UNITS[u][0]
        copies["p", u].wait_recv()
        add(u, near, 1 - xl, from_partner[n])
        for r in ORDER:
            src, dst = row_of(u, held[n], near + lax.rem(y + r, 4)), row_of(u, from_y[n], r - 1)
            begin(("y", u, r), remote(src, dst, y_send.at[u, r - 1], y_recv.at[u, r - 1], ys[r]))

    def blocks(u):
        n, c0, size = REDUCE_UNITS[u]
        if n == 0:
            return size // 16, lambda i: (pl.ds(pl.multiple_of(c0 + i * 16, 16), 16), slice(None))
        if n == 3:
            return 3, lambda i: (pl.ds(pl.multiple_of(i * 16, 16), 16), slice(None))
        return 4, lambda i: (i, slice(None), slice(c0, c0 + size))

    def stage_3(u):
        n = REDUCE_UNITS[u][0]
        for r in ORDER:
            copies["y", u, r].wait_recv()
        number, at = blocks(u)

        def body(i):
            total = held[n][me, *at(i)].astype(F32)
            for r in range(3):
                total = total + from_y[n][r, *at(i)].astype(F32)
            mine[n][at(i)] = total.astype(mine[n].dtype)

        loop(number, body)
        begin(("t", u), remote(row_of(u, mine[n]), row_of(u, theirs[n]), t_send.at[u], t_recv.at[u], twin))

    def stage_4(u):
        n, c0, size = REDUCE_UNITS[u]
        copies["t", u].wait_recv()
        number, at = blocks(u)
        target = outs[n] if ended[n] is None else ended[n]

        def body(i):
            if ended[n] is None:
                target[at(i)] = mine[n][at(i)].astype(F32) + theirs[n][at(i)].astype(F32)
            else:
                target[at(i)] = mine[n][at(i)] + theirs[n][at(i)]

        loop(number, body)
        if ended[n] is not None:
            part = (slice(None), pl.ds(c0, size))
            for r in ORDER:
                src, dst = target.at[lax.rem(z + r, 4), *part], outs[n].at[z, *part]
                begin(("z", u, r), remote(src, dst, z_send.at[u, r - 1], z_recv.at[u, r - 1], zs[r]))
            copy = pltpu.make_async_copy(target.at[z, *part], outs[n].at[z, *part], keep.at[u])
            copy.start()
            copies["keep", u] = copy

    ready = set()
    count = len(REDUCE_UNITS)
    stages = (stage_0, stage_1, stage_2, stage_3, stage_4)
    for step in range(count + 16):
        for s, stage in enumerate(stages):
            if 0 <= step - 4 * s < count:
                stage(step - 4 * s)
    o_d[...] = l_d[0:216, :]

    def landed(n):
        for u in range(count):
            if REDUCE_UNITS[u][0] == n:
                copies["keep", u].wait()
                for r in ORDER:
                    copies["z", u, r].wait_recv()

    for n, out in ((1, o_g), (2, o_u)):
        landed(n)
        for zz in range(4):
            for q in range(8):
                first = (4 * q + zz) * 216
                out[:, first : first + 216] = outs[n][zz, :, 224 * q : 224 * q + 216].astype(F32)
    landed(4)
    for zz in range(4):
        for q in range(8):
            for part in range(3):
                first, at = part * 1536 + (4 * q + zz) * 48, part * 384 + q * 48
                o_in[:, first : first + 48] = l_in[zz, :, at : at + 48].astype(F32)
    landed(5)
    o_s[...] = b_s[0] + b_s[1] + b_s[2] + b_s[3]
    for copy in sent:
        copy.wait_send()


def reduce(g_d, g_g, g_u, g_o, g_in, g_s):
    shape = jax.ShapeDtypeStruct
    dma = pltpu.SemaphoreType.DMA
    vm = pltpu.VMEM
    count = len(REDUCE_UNITS)
    big = ((4, 48, 1792), (4, 48, 1792), (4, 48, 1152))
    return pl.pallas_call(
        reduce_kernel,
        out_shape=(
            shape((216, 1536), F32),
            shape((48, 6912), F32),
            shape((48, 6912), F32),
            shape((48, 1536), F32),
            shape((48, 4608), F32),
            shape((8, 128), F32),
        ),
        in_specs=[ANY] * 6,
        out_specs=[VMEM] * 6,
        scratch_shapes=[
            vm((8, 224, 1536), BF16), vm((8, 4, 48, 1792), BF16), vm((8, 4, 48, 1792), BF16),
            vm((8, 48, 1536), BF16), vm((8, 4, 48, 1152), BF16), vm((8, 4, 8, 128), F32),
            vm((4, 2, 48, 1792), BF16), vm((4, 2, 48, 1792), BF16), vm((4, 48, 768), BF16),
            vm((4, 2, 48, 1152), BF16), vm((4, 2, 8, 128), F32),
            vm((4, 224, 1536), BF16), vm((4, 2, 48, 1792), BF16), vm((4, 2, 48, 1792), BF16),
            vm((4, 48, 768), BF16), vm((4, 2, 48, 1152), BF16), vm((4, 2, 8, 128), F32),
            vm((3, 224, 1536), BF16), vm((3, 4, 48, 1792), BF16), vm((3, 4, 48, 1792), BF16),
            vm((3, 48, 1536), BF16), vm((3, 4, 48, 1152), BF16), vm((3, 4, 8, 128), F32),
            vm((224, 1536), BF16), vm(big[0], BF16), vm(big[1], BF16), vm((48, 1536), BF16), vm(big[2], BF16),
            vm((4, 8, 128), F32),
            vm((224, 1536), BF16), vm(big[0], BF16), vm(big[1], BF16), vm((48, 1536), BF16), vm(big[2], BF16),
            vm((4, 8, 128), F32),
            vm(big[0], BF16), vm(big[1], BF16), vm(big[2], BF16), vm((4, 8, 128), F32),
            vm((224, 1536), F32), vm(big[0], BF16), vm(big[1], BF16), vm(big[2], BF16), vm((4, 8, 128), F32),
            dma((6,)), dma((count,)), dma((count,)), dma((count,)), dma((count,)), dma((count, 3)), dma((count, 3)),
            dma((count,)), dma((count,)), dma((count, 3)), dma((count, 3)), dma((count,)),
        ],
        compiler_params=pltpu.CompilerParams(
            collective_id=2, has_side_effects=True, vmem_limit_bytes=63 * 2**20
        ),
        name="reduce_grads",
    )(g_d, g_g, g_u, g_o, g_in, g_s)


def local(inputs, cotangent, w_in, w_out, w_gate, w_up, w_down, kernel, gain_mix, gain_ffn):
    small = jnp.concatenate([kernel[0], gain_mix, gain_ffn], axis=0).astype(F32)
    small = jnp.pad(small, ((0, 3), (0, 80)))
    y, gx, g_in, g_o, g_g, g_u, g_d, g_s = run_blocks(
        inputs.reshape(128, 1536), cotangent.reshape(128, 1536), small, w_in[0], w_out[0], w_gate[0], w_up[0], w_down[0]
    )
    o_d, o_g, o_u, o_o, o_in, o_s = reduce(
        g_d.reshape(8, 224, 1536),
        g_g.reshape(8, 4, 48, 1792),
        g_u.reshape(8, 4, 48, 1792),
        g_o.reshape(8, 48, 1536),
        g_in.reshape(8, 4, 48, 1152),
        g_s.reshape(8, 4, 8, 128),
    )
    return (
        y.reshape(1, 2, 64, 1536),
        gx.reshape(1, 2, 64, 1536),
        o_in[None],
        o_o[None],
        o_g[None],
        o_u[None],
        o_d[None],
        o_s[None, 0:3, :48],
        o_s[3:4, :48],
        o_s[4:5, :48],
    )


def solution(mesh):
    names = ("section", "xl", "xh", "y", "z")
    fine = Mesh(mesh.devices.reshape(2, 2, 2, 4, 4), names)
    tokens, shard = ("xl", "xh", "y", "z"), ("xh", "y", "z")
    weight = P("section", shard, None)
    acts = P("section", None, tokens, None)
    return jax.shard_map(
        local,
        mesh=fine,
        in_specs=(
            P(None, tokens, None),
            P(None, tokens, None),
            weight,
            weight,
            weight,
            weight,
            weight,
            P("section", None, shard),
            P("section", shard),
            P("section", shard),
        ),
        out_specs=(
            acts,
            acts,
            weight,
            weight,
            weight,
            weight,
            weight,
            P("section", None, shard),
            P("section", shard),
            P("section", shard),
        ),
        check_vma=False,
    )
```

time: 505 us -> 444 us (0.88)
  local copies, waits for them, and re-layouts: 42.1 us -> 11.5 us
  Pallas kernels: 455 us -> 430 us
    pallas_call x3 -> x2, Pallas kernels: 455 us -> 430 us  [the longest x1 306 us: run_blocks(): pl.pallas_call(blocks_kernel, out_shape=(shape((128, 1536), BF16), shape(...]
    convert_element_type x7 -> x0, local copies, waits for them, and re-layouts: 15.5 us -> none  [the longest x3 8.28 us: local(): o_in.reshape(4, 48, 3, 8, 48).transpose(1, 2, 3, 0, 4).reshape(1, 48, 4608)]
    reshape x13 -> x0, local copies, waits for them, and re-layouts: 12.4 us -> none  [the longest x2 3.63 us: cut_ffn(): return tiles.transpose(2, 0, 1, 3).reshape(4, 48, 1792)]
    unnamed x22 -> x20, local copies, waits for them, and re-layouts: 2.94 us -> 9.55 us
    another operation x6 -> x0, local copies, waits for them, and re-layouts: 5.15 us -> none  [the longest x4 4.97 us: cut_ffn(): weight.reshape(48, 8, 4, 216)]
where the time goes in v3:
time: 444 us; the launch traced here: 443 us
  Pallas kernels  430 us (97%)
  local copies, waits for them, and re-layouts  11.5 us (3%)
    pallas_call x1, Pallas kernels, run_blocks(): pl.pallas_call(blocks_kernel, out_shape=(shape((128, 1536), BF16), shape(...  306 us
    pallas_call x1, Pallas kernels, reduce(): pl.pallas_call(reduce_kernel, out_shape=(shape((216, 1536), F32), shape((...  124 us
    unnamed x20, local copies, waits for them, and re-layouts  9.55 us

profile of v3, /device:TPU:2, one launch (start us, length us, event | category | flops | bytes accessed | tf_op | source)
XLA Modules:
  0.0 443.3 jit_solution(11187159555751232755)
XLA Ops:
  0.6 1.3 fusion.9.small
  2.0 306.1 %two_blocks.1 = (bf16[128,1536]{1,0:T(8,128)(2,1)}, f32[128,1536]{1,0:T(8,128)}, bf16[1536,1152]{1,0:T(8,128)(2,1)}, bf16[384,1536]{1,0:T(8,128)(2,1)}, bf16[153...) custom-call(bf16[128,1536]{1,0:T(8,128)(2,1)} %bitcast.37, ...), custom_call_target="tpu_custom_call" | custom-call | tf_op jit(solution)/shard_map/two_blocks/pallas_call | solution.py:656
  308.1 0.0 copy-start.4
  308.1 123.7 %reduce_grads.1 = (f32[216,1536]{1,0:T(8,128)}, f32[48,6912]{1,0:T(8,128)}, f32[48,6912]{1,0:T(8,128)}, f32[48,1536]{1,0:T(8,128)}, f32[48,4608]{1,0:T(8,128)}, /*index=5*/f32[8,128]{1,0:T(8,128)}) custom-call(bf16[8,224,1536]{2,1,0:T(8,128)(2,1)} %bitcast.25, bf16[8,4,48,1792]{3,2,1,0:T(8,128)(2,1)} %bitcast.23, bf16[8,4,48,1792]{3,2,1,0:T(8,128)(2,1)} %bitcast.24, ...), custom_call_target="tpu_custom_call" | custom-call | tf_op jit(solution)/shard_map/reduce_grads/pallas_call | solution.py:890
  431.8 0.0 copy-start.3
  431.8 1.3 fusion.10
  433.1 0.7 slice_bitcast_fusion
  433.8 0.6 copy.20
  434.3 1.8 copy.28
  436.1 0.0 copy-done.4
  436.1 0.0 copy-start.5
  436.1 0.9 copy.29
  437.0 0.0 copy-done.3
  437.0 0.0 copy-start.2
  437.0 0.9 copy.30
  437.9 0.0 copy-done.5
  437.9 0.7 copy.31
  438.6 0.0 copy-done.2
  438.7 0.0 copy-start.1
  438.7 1.1 copy.32
  439.7 0.7 copy-done.1
  440.5 0.0 copy-start
  440.5 1.1 copy.33
  441.5 0.7 copy-done
  442.3 1.1 copy.34
Async XLA Ops:
  308.1 128.0 %copy-start.4 = (f32[128,1536]{1,0:T(8,128)S(1)}, f32[128,1536]{1,0:T(8,128)}, u32[]{:S(2)}) copy-start(f32[128,1536]{1,0:T(8,128)} %get-tuple-element.25) | copy-start | bytes 2359300
  431.8 5.2 %copy-start.3 = (f32[48,4608]{1,0:T(8,128)S(1)}, f32[48,4608]{1,0:T(8,128)}, u32[]{:S(2)}) copy-start(f32[48,4608]{1,0:T(8,128)} %get-tuple-element.32) | copy-start | bytes 2654212
  436.1 1.8 copy-start.5
  437.0 1.7 copy-start.2
  438.7 1.8 copy-start.1
  440.5 1.8 copy-start

commit v4 on v3

--- a/solution.py
+++ b/solution.py
@@ -16,15 +16,40 @@
 ORDER = (1, 3, 2)
 
 GATHER_UNITS = (
-    (0, 0, 128), (1, 0, 1152), (2, 0, 1536),
+    (2, 0, 1536), (0, 0, 128), (1, 0, 640), (1, 640, 512),
     (3, 0, 640), (4, 0, 640), (3, 640, 640), (4, 640, 640), (3, 1280, 512), (4, 1280, 512),
     (5, 0, 80), (5, 80, 80), (5, 160, 64),
 )
+GATHER_LAGS = (3, 5)
+FORWARD_AT = ((8, 9, 12, 15), (11, 13, 15, 17))
+GO_AFTER = 15
 REDUCE_UNITS = (
-    (0, 0, 80), (0, 80, 80), (0, 160, 64),
-    (1, 0, 640), (1, 640, 640), (1, 1280, 512), (2, 0, 640), (2, 640, 640), (2, 1280, 512),
-    (3, 0, 1536), (4, 0, 640), (4, 640, 512), (5, 0, 128),
+    (0, 0, 32, 0),
+    (2, 0, 128, 2),
+    (0, 32, 48, 1),
+    (2, 128, 128, 2),
+    (4, 0, 256, 0),
+    (1, 0, 768, 0),
+    (2, 256, 640, 0),
+    (4, 256, 128, 0),
+    (4, 384, 128, 1),
+    (5, 0, 128, 0),
+    (4, 512, 256, 2),
+    (1, 768, 512, 0),
+    (1, 1280, 512, 0),
+    (2, 896, 128, 0),
+    (4, 768, 128, 2),
+    (4, 896, 256, 2),
+    (2, 1024, 640, 0),
+    (2, 1664, 128, 1),
+    (0, 80, 16, 2),
+    (3, 0, 1536, 0),
+    (0, 96, 48, 0),
+    (0, 144, 16, 2),
+    (0, 160, 32, 0),
+    (0, 192, 32, 0),
 )
+REDUCE_LAGS = (0, 21, 27, 35, 41)
 
 
 def place():
@@ -80,7 +105,7 @@
 def blocks_kernel(
     x_ref, cot_ref, small, w_in, w_out, w_gate, w_up, w_down,
     y_ref, gx_ref, gin_h, gout_h, gg_h, gu_h, gd_h, gs_ref,
-    xa, xn, n2, ea, fa, part, rr, proj, ge, dce, cv, ha, hb, mx, gt, up, hd, dg, du,
+    xa, xn, n2, ea, fa, part, rr, proj, ge, dce, cv, ha, hb, mx, by_gate, by_up, hd, dg, du,
     mid, dmid, dp, g0, win, wout, wg, wu, wd, sm, gains, taps, gtap, ggain,
     store, a_send, a_recv, s_send, s_recv, h_send, h_recv, c_send, c_recv,
     z_send, z_recv, y_send, y_recv, p_send, p_recv, q_send, q_recv, go,
@@ -117,6 +142,8 @@
     rows = (32, 192, 48, 192, 192, 224)
     cut_conv(w_in, dp)
     wout[pl.ds(pl.multiple_of(me * 48, 16), 48), :] = w_out[...]
+    first_d = pl.multiple_of(me * 224, 16)
+    wd[pl.ds(first_d, 224), :] = jnp.concatenate([w_down[...], jnp.zeros((8, 1536), BF16)], axis=0)
     pl.semaphore_wait(barrier, 10 - (group + 1) // 16 + (group + 15) // 16)
 
     def of_z(n, ref, first, zz):
@@ -190,8 +217,6 @@
     push_z(3)
     cut_ffn(w_up, dg)
     push_z(4)
-    first_d = pl.multiple_of(me * 224, 16)
-    wd[pl.ds(first_d, 224), :] = jnp.concatenate([w_down[...], jnp.zeros((8, 1536), BF16)], axis=0)
 
     def piece(u, q):
         n, first, size = GATHER_UNITS[u]
@@ -372,14 +397,16 @@
         arrived(n_all[mb])
 
         def body(j):
-            at = cols(j, 256)
+            at = cols(j, 896)
             gating = dot_nn(n2[mb_rows[mb], :], wg[:, at])
             up_part = dot_nn(n2[mb_rows[mb], :], wu[:, at])
-            gt[mb_rows[mb], at] = gating
-            up[mb_rows[mb], at] = up_part
-            hd[mb_rows[mb], at] = (gating * jax.nn.sigmoid(gating) * up_part).astype(BF16)
-
-        loop(7, body)
+            sg = jax.nn.sigmoid(gating)
+            silu = gating * sg
+            by_gate[mb_rows[mb], at] = up_part * sg * (1.0 + gating * (1.0 - sg))
+            by_up[mb_rows[mb], at] = silu
+            hd[mb_rows[mb], at] = (silu * up_part).astype(BF16)
+
+        loop(2, body)
 
     def down(mb):
         sum_sent(0, mb)
@@ -437,28 +464,27 @@
         need(5)
         both(down)
 
-    segments = {5: forward_1, 7: forward_2, 9: forward_3, 13: forward_4}
+    segments = (forward_1, forward_2, forward_3, forward_4)
     count = len(GATHER_UNITS)
-    for step in range(count + 4):
+    lag_p, lag_q = GATHER_LAGS
+    for step in range(count + lag_q):
         if step < count:
             stage_y(step)
-        if 0 <= step - 2 < count:
-            stage_p(step - 2)
-        if step - 2 == count - 1:
+        if 0 <= step - lag_p < count:
+            stage_p(step - lag_p)
+        if step == GO_AFTER:
 
             @pl.when(section == 0)
             def _():
                 pl.semaphore_signal(go, inc=1, device_id=core, device_id_type=MESH)
 
-        if 0 <= step - 4 < count:
-            stage_q(step - 4)
-        if step in segments:
-            pl.when(section == 0)(segments[step])
-
-    @pl.when(section == 1)
-    def _():
-        for segment in segments.values():
-            segment()
+        if 0 <= step - lag_q < count:
+            stage_q(step - lag_q)
+        for turn, segment in enumerate(segments):
+            if step == FORWARD_AT[0][turn]:
+                pl.when(section == 0)(segment)
+            if step == FORWARD_AT[1][turn]:
+                pl.when(section == 1)(segment)
 
     forward_5()
     both(finish)
@@ -478,14 +504,12 @@
         arrived(e_all[mb])
 
         def body(j):
-            at = cols(j, 256)
+            at = cols(j, 896)
             dh = dot_nt(ea[mb_rows[mb], :], wd[at, :])
-            gating, up_part = gt[mb_rows[mb], at], up[mb_rows[mb], at]
-            sg = jax.nn.sigmoid(gating)
-            dg[mb_rows[mb], at] = (dh * up_part * sg * (1.0 + gating * (1.0 - sg))).astype(BF16)
-            du[mb_rows[mb], at] = (dh * gating * sg).astype(BF16)
-
-        loop(7, body)
+            dg[mb_rows[mb], at] = (dh * by_gate[mb_rows[mb], at]).astype(BF16)
+            du[mb_rows[mb], at] = (dh * by_up[mb_rows[mb], at]).astype(BF16)
+
+        loop(2, body)
 
     def back_ffn(mb):
         sum_sent(1, mb)
@@ -580,13 +604,13 @@
 
     both(take_gradient)
     both(lambda mb: (back_hidden(mb), back_ffn(mb)))
-    grad(4, 256, hd, ea)
+    grad(4, 896, hd, ea)
     back_middle(0)
-    grad(2, 256, n2, dg)
+    grad(2, 768, n2, dg)
     back_middle(1)
-    grad(3, 256, n2, du)
+    grad(3, 768, n2, du)
     both(back_mix)
-    grad(1, 128, mx, fa)
+    grad(1, 384, mx, fa)
     for k in range(3):
         total = jnp.zeros((1, 384), F32)
         for mb in range(2):
@@ -596,7 +620,7 @@
                 total = total + jnp.sum(products, axis=0, keepdims=True)
         gtap[k : k + 1, :] = total
     both(lambda mb: (back_conv(mb), back_in(mb)))
-    grad(0, 256, xn, dp)
+    grad(0, 768, xn, dp)
     both(back_input)
 
     gs_ref[...] = jnp.zeros((256, 128), F32)
@@ -690,185 +714,206 @@
     )(x, cot, small, w_in, w_out, w_gate, w_up, w_down)
 
 
+def unit_shape(u):
+    n, first, size, mode = REDUCE_UNITS[u]
+    if n == 0:
+        return (size, 1536), (size, 768)
+    if n == 3:
+        return (48, 1536), (48, 768)
+    height = 8 if n == 5 else 48
+    return (4, height, size), (2, height, size)
+
+
+def unit_buffers(u):
+    n, first, size, mode = REDUCE_UNITS[u]
+    whole, part = unit_shape(u)
+    dtype = F32 if n == 5 else BF16
+    shapes = {
+        0: ((4, *part), (4, *part), (3, *whole)),
+        1: (None, (4, *whole), (3, *whole)),
+        2: (None, whole, (3, 2, *whole)),
+    }[mode]
+    shapes += (whole, whole if n in (1, 2, 4, 5) else None)
+    return [None if shape is None else pltpu.VMEM(shape, dtype) for shape in shapes]
+
+
 def reduce_kernel(
     g_d, g_g, g_u, g_o, g_in, g_s,
     o_d, o_g, o_u, o_o, o_in, o_s,
-    v_d, v_g, v_u, v_o, v_in, v_s,
-    q1_g, q1_u, q1_o, q1_in, q1_s,
-    p_d, p_g, p_u, p_o, p_in, p_s,
-    y_d, y_g, y_u, y_o, y_in, y_s,
-    f_d, f_g, f_u, f_o, f_in, f_s,
-    t_d, t_g, t_u, t_o, t_in, t_s,
-    e_g, e_u, e_in, e_s, l_d, l_g, l_u, l_in, b_s,
-    load, q_send, q_recv, p_send, p_recv, y_send, y_recv, t_send, t_recv, z_send, z_recv, keep,
+    v_d, v_g, v_u, v_o, v_in, v_s, l_d, l_g, l_u, l_in, l_s,
+    load, q_send, q_recv, p_send, p_recv, y_send, y_recv, t_send, t_recv, z_send, z_recv,
+    *buffers,
 ):
     section, xl, xh, y, z = place()
     partner, twin, zs, ys = plane_peers()
-    grads = (g_d, g_g, g_u, g_o, g_in, g_s)
     held = (v_d, v_g, v_u, v_o, v_in, v_s)
-    from_twin = (None, q1_g, q1_u, q1_o, q1_in, q1_s)
-    from_partner = (p_d, p_g, p_u, p_o, p_in, p_s)
-    from_y = (y_d, y_g, y_u, y_o, y_in, y_s)
-    mine = (f_d, f_g, f_u, f_o, f_in, f_s)
-    theirs = (t_d, t_g, t_u, t_o, t_in, t_s)
-    ended = (None, e_g, e_u, None, e_in, e_s)
-    outs = (l_d, l_g, l_u, o_o, l_in, b_s)
-    loads = [pltpu.make_async_copy(grads[n], held[n], load.at[n]) for n in range(6)]
+    landing = (l_d, l_g, l_u, o_o, l_in, l_s)
+    loads = [pltpu.make_async_copy(src, held[n], load.at[n]) for n, src in enumerate((g_d, g_g, g_u, g_o, g_in, g_s))]
     for copy in loads:
         copy.start()
     barrier_all([partner, twin, *zs.values(), *ys.values()])
-    near, far = xh * 4, (1 - xh) * 4
-    me = near + y
-    sent = []
-    copies = {}
+    count = len(REDUCE_UNITS)
+    left = list(buffers)
+    slots = [[None if shape is None else left.pop(0) for shape in unit_buffers(u)] for u in range(count)]
+    from_twin, from_partner, from_y, theirs, ended = zip(*slots)
+    near, far = xh, 1 - xh
+    sent, copies = [], {}
 
     def begin(key, copy):
         copy.start()
         copies[key] = copy
         sent.append(copy)
 
-    def half(u, ref, first, h):
-        n, c0, size = REDUCE_UNITS[u]
+    def tail(u, h=None):
+        n, first, size, mode = REDUCE_UNITS[u]
+        across = slice(None) if h is None else pl.ds(pl.multiple_of(h * 768, 128), 768)
+        if n == 0:
+            return pl.ds(first, size), across
         if n == 3:
-            return ref.at[pl.ds(first, 4), :, pl.ds(pl.multiple_of(h * 768, 128), 768)]
-        return ref.at[pl.ds(first, 4), pl.ds(h * 2, 2), :, pl.ds(c0, size)]
-
-    def arrived(u, ref):
-        n, c0, size = REDUCE_UNITS[u]
-        return ref if n == 3 else ref.at[:, :, :, pl.ds(c0, size)]
-
-    def row_of(u, ref, *lead):
-        n, c0, size = REDUCE_UNITS[u]
-        if n == 0:
-            return ref.at[*lead, pl.ds(c0, size)]
-        if n == 3:
-            return ref.at[*lead] if lead else ref
-        return ref.at[*lead, :, :, pl.ds(c0, size)]
-
-    def add(u, first, h, other):
-        n, c0, size = REDUCE_UNITS[u]
-        if n == 0:
-            rows = size // 16
-
-            def body(i):
-                row, at = i // rows, pl.ds(pl.multiple_of(c0 + lax.rem(i, rows) * 16, 16), 16)
-                v_d[first + row, at, :] = v_d[first + row, at, :] + other[row, at, :]
-
-            loop(4 * rows, body)
-        elif n == 3:
-            at = pl.ds(pl.multiple_of(h * 768, 128), 768)
-
-            def body(i):
-                v_o[first + i, :, at] = v_o[first + i, :, at] + other[i]
-
-            loop(4, body)
-        else:
-            ref, at = held[n], slice(c0, c0 + size)
-
-            def body(i):
-                a, b = first + i // 2, h * 2 + lax.rem(i, 2)
-                ref[a, b, :, at] = ref[a, b, :, at] + other[i // 2, lax.rem(i, 2), :, at]
-
-            loop(8, body)
+            return slice(None), across
+        return slice(None) if h is None else pl.ds(h * 2, 2), slice(None), pl.ds(first, size)
+
+    def blocks(u, h=None):
+        n, first, size, mode = REDUCE_UNITS[u]
+        if n in (0, 3):
+            across = slice(None) if h is None else pl.ds(pl.multiple_of(h * 768, 128), 768)
+            start = first if n == 0 else 0
+
+            def at(i):
+                return (pl.ds(pl.multiple_of(start + i * 16, 16), 16), across), (
+                    pl.ds(pl.multiple_of(i * 16, 16), 16),
+                    slice(None),
+                )
+
+            return (size if n == 0 else 48) // 16, at
+        shift = 0 if h is None else h * 2
+        return 4 if h is None else 2, lambda i: ((shift + i, slice(None), slice(first, first + size)), (i,))
+
+    def add_rows(u, side, h, other):
+        ref = held[REDUCE_UNITS[u][0]]
+        number, at = blocks(u, h)
+
+        def body(k):
+            row = k // number
+            here, there = at(lax.rem(k, number))
+            ref[side, row, *here] = ref[side, row, *here] + other[row, *there]
+
+        loop(4 * number, body)
+
+    def send_y(u, source):
+        for r in ORDER:
+            dst = from_y[u].at[r - 1]
+            begin(("y", u, r), remote(source(lax.rem(y + r, 4)), dst, y_send.at[u, r - 1], y_recv.at[u, r - 1], ys[r]))
+
+    def send_p(u, src):
+        begin(("p", u), remote(src, from_partner[u], p_send.at[u], p_recv.at[u], partner))
+
+    def send_twin(u):
+        src = held[REDUCE_UNITS[u][0]].at[near, y, *tail(u)]
+        begin(("t", u), remote(src, theirs[u], t_send.at[u], t_recv.at[u], twin))
+
+    def sum_y(u, sides):
+        for r in ORDER:
+            copies["y", u, r].wait_recv()
+        ref = held[REDUCE_UNITS[u][0]]
+        number, at = blocks(u)
+
+        def body(k):
+            side = near if len(sides) == 1 else k // number
+            here, there = at(lax.rem(k, number))
+            total = ref[side, y, *here].astype(F32)
+            for r in range(3):
+                got = from_y[u][r, *there] if len(sides) == 1 else from_y[u][r, side, *there]
+                total = total + got.astype(F32)
+            ref[side, y, *here] = total.astype(ref.dtype)
+
+        loop(len(sides) * number, body)
+
+    ready = set()
 
     def stage_0(u):
-        n = REDUCE_UNITS[u][0]
+        n, first, size, mode = REDUCE_UNITS[u]
         if n not in ready:
             ready.add(n)
             loads[n].wait()
-        if n:
-            dst = arrived(u, from_twin[n])
-            begin(("q", u), remote(half(u, held[n], far, 1 - xl), dst, q_send.at[u], q_recv.at[u], twin))
+        if mode == 0:
+            src = held[n].at[far, :, *tail(u, 1 - xl)]
+            begin(("q", u), remote(src, from_twin[u], q_send.at[u], q_recv.at[u], twin))
+        elif mode == 1:
+            send_p(u, held[n].at[far, :, *tail(u)])
         else:
-            begin_p(u, held[n].at[pl.ds(far, 4), pl.ds(*REDUCE_UNITS[u][1:])])
-
-    def begin_p(u, src):
-        n, c0, size = REDUCE_UNITS[u]
-        dst = from_partner[n].at[:, pl.ds(c0, size)] if n == 0 else arrived(u, from_partner[n])
-        begin(("p", u), remote(src, dst, p_send.at[u], p_recv.at[u], partner))
+            send_y(u, lambda row: held[n].at[:, row, *tail(u)])
 
     def stage_1(u):
-        n = REDUCE_UNITS[u][0]
-        if n:
+        n, first, size, mode = REDUCE_UNITS[u]
+        if mode == 0:
             copies["q", u].wait_recv()
-            add(u, far, xl, from_twin[n])
-            begin_p(u, half(u, held[n], far, xl))
+            add_rows(u, far, xl, from_twin[u])
+            send_p(u, held[n].at[far, :, *tail(u, xl)])
+        elif mode == 2:
+            sum_y(u, (0, 1))
+            send_p(u, held[n].at[far, y, *tail(u)])
 
     def stage_2(u):
-        n = REDUCE_UNITS[u][0]
+        n, first, size, mode = REDUCE_UNITS[u]
         copies["p", u].wait_recv()
-        add(u, near, 1 - xl, from_partner[n])
-        for r in ORDER:
-            src, dst = row_of(u, held[n], near + lax.rem(y + r, 4)), row_of(u, from_y[n], r - 1)
-            begin(("y", u, r), remote(src, dst, y_send.at[u, r - 1], y_recv.at[u, r - 1], ys[r]))
-
-    def blocks(u):
-        n, c0, size = REDUCE_UNITS[u]
-        if n == 0:
-            return size // 16, lambda i: (pl.ds(pl.multiple_of(c0 + i * 16, 16), 16), slice(None))
-        if n == 3:
-            return 3, lambda i: (pl.ds(pl.multiple_of(i * 16, 16), 16), slice(None))
-        return 4, lambda i: (i, slice(None), slice(c0, c0 + size))
+        if mode == 2:
+            number, at = blocks(u)
+
+            def body(i):
+                here, there = at(i)
+                held[n][near, y, *here] = held[n][near, y, *here] + from_partner[u][there]
+
+            loop(number, body)
+            send_twin(u)
+        else:
+            add_rows(u, near, 1 - xl if mode == 0 else None, from_partner[u])
+            send_y(u, lambda row: held[n].at[near, row, *tail(u)])
 
     def stage_3(u):
-        n = REDUCE_UNITS[u][0]
-        for r in ORDER:
-            copies["y", u, r].wait_recv()
-        number, at = blocks(u)
-
-        def body(i):
-            total = held[n][me, *at(i)].astype(F32)
-            for r in range(3):
-                total = total + from_y[n][r, *at(i)].astype(F32)
-            mine[n][at(i)] = total.astype(mine[n].dtype)
-
-        loop(number, body)
-        begin(("t", u), remote(row_of(u, mine[n]), row_of(u, theirs[n]), t_send.at[u], t_recv.at[u], twin))
+        if REDUCE_UNITS[u][3] != 2:
+            sum_y(u, (0,))
+            send_twin(u)
 
     def stage_4(u):
-        n, c0, size = REDUCE_UNITS[u]
+        n, first, size, mode = REDUCE_UNITS[u]
         copies["t", u].wait_recv()
         number, at = blocks(u)
-        target = outs[n] if ended[n] is None else ended[n]
 
         def body(i):
-            if ended[n] is None:
-                target[at(i)] = mine[n][at(i)].astype(F32) + theirs[n][at(i)].astype(F32)
+            here, there = at(i)
+            if n in (0, 3):
+                landing[n][here] = held[n][near, y, *here].astype(F32) + theirs[u][there].astype(F32)
             else:
-                target[at(i)] = mine[n][at(i)] + theirs[n][at(i)]
+                ended[u][there] = held[n][near, y, *here] + theirs[u][there]
 
         loop(number, body)
-        if ended[n] is not None:
-            part = (slice(None), pl.ds(c0, size))
+        if n not in (0, 3):
+            part = (slice(None), pl.ds(first, size))
             for r in ORDER:
-                src, dst = target.at[lax.rem(z + r, 4), *part], outs[n].at[z, *part]
+                src, dst = ended[u].at[lax.rem(z + r, 4)], landing[n].at[z, *part]
                 begin(("z", u, r), remote(src, dst, z_send.at[u, r - 1], z_recv.at[u, r - 1], zs[r]))
-            copy = pltpu.make_async_copy(target.at[z, *part], outs[n].at[z, *part], keep.at[u])
-            copy.start()
-            copies["keep", u] = copy
-
-    ready = set()
-    count = len(REDUCE_UNITS)
+            landing[n][z, :, first : first + size] = ended[u][z]
+
     stages = (stage_0, stage_1, stage_2, stage_3, stage_4)
-    for step in range(count + 16):
-        for s, stage in enumerate(stages):
-            if 0 <= step - 4 * s < count:
-                stage(step - 4 * s)
-    o_d[...] = l_d[0:216, :]
+    for step in range(count + REDUCE_LAGS[-1]):
+        for lag, stage in zip(REDUCE_LAGS, stages):
+            if 0 <= step - lag < count:
+                stage(step - lag)
 
     def landed(n):
         for u in range(count):
             if REDUCE_UNITS[u][0] == n:
-                copies["keep", u].wait()
                 for r in ORDER:
                     copies["z", u, r].wait_recv()
 
+    o_d[...] = l_d[0:216, :]
     for n, out in ((1, o_g), (2, o_u)):
         landed(n)
         for zz in range(4):
             for q in range(8):
                 first = (4 * q + zz) * 216
-                out[:, first : first + 216] = outs[n][zz, :, 224 * q : 224 * q + 216].astype(F32)
+                out[:, first : first + 216] = landing[n][zz, :, 224 * q : 224 * q + 216].astype(F32)
     landed(4)
     for zz in range(4):
         for q in range(8):
@@ -876,7 +921,7 @@
                 first, at = part * 1536 + (4 * q + zz) * 48, part * 384 + q * 48
                 o_in[:, first : first + 48] = l_in[zz, :, at : at + 48].astype(F32)
     landed(5)
-    o_s[...] = b_s[0] + b_s[1] + b_s[2] + b_s[3]
+    o_s[...] = l_s[0] + l_s[1] + l_s[2] + l_s[3]
     for copy in sent:
         copy.wait_send()
 
@@ -886,7 +931,6 @@
     dma = pltpu.SemaphoreType.DMA
     vm = pltpu.VMEM
     count = len(REDUCE_UNITS)
-    big = ((4, 48, 1792), (4, 48, 1792), (4, 48, 1152))
     return pl.pallas_call(
         reduce_kernel,
         out_shape=(
@@ -900,28 +944,26 @@
         in_specs=[ANY] * 6,
         out_specs=[VMEM] * 6,
         scratch_shapes=[
-            vm((8, 224, 1536), BF16), vm((8, 4, 48, 1792), BF16), vm((8, 4, 48, 1792), BF16),
-            vm((8, 48, 1536), BF16), vm((8, 4, 48, 1152), BF16), vm((8, 4, 8, 128), F32),
-            vm((4, 2, 48, 1792), BF16), vm((4, 2, 48, 1792), BF16), vm((4, 48, 768), BF16),
-            vm((4, 2, 48, 1152), BF16), vm((4, 2, 8, 128), F32),
-            vm((4, 224, 1536), BF16), vm((4, 2, 48, 1792), BF16), vm((4, 2, 48, 1792), BF16),
-            vm((4, 48, 768), BF16), vm((4, 2, 48, 1152), BF16), vm((4, 2, 8, 128), F32),
-            vm((3, 224, 1536), BF16), vm((3, 4, 48, 1792), BF16), vm((3, 4, 48, 1792), BF16),
-            vm((3, 48, 1536), BF16), vm((3, 4, 48, 1152), BF16), vm((3, 4, 8, 128), F32),
-            vm((224, 1536), BF16), vm(big[0], BF16), vm(big[1], BF16), vm((48, 1536), BF16), vm(big[2], BF16),
+            vm((2, 4, 224, 1536), BF16), vm((2, 4, 4, 48, 1792), BF16), vm((2, 4, 4, 48, 1792), BF16),
+            vm((2, 4, 48, 1536), BF16), vm((2, 4, 4, 48, 1152), BF16), vm((2, 4, 4, 8, 128), F32),
+            vm((224, 1536), F32), vm((4, 48, 1792), BF16), vm((4, 48, 1792), BF16), vm((4, 48, 1152), BF16),
             vm((4, 8, 128), F32),
-            vm((224, 1536), BF16), vm(big[0], BF16), vm(big[1], BF16), vm((48, 1536), BF16), vm(big[2], BF16),
-            vm((4, 8, 128), F32),
-            vm(big[0], BF16), vm(big[1], BF16), vm(big[2], BF16), vm((4, 8, 128), F32),
-            vm((224, 1536), F32), vm(big[0], BF16), vm(big[1], BF16), vm(big[2], BF16), vm((4, 8, 128), F32),
             dma((6,)), dma((count,)), dma((count,)), dma((count,)), dma((count,)), dma((count, 3)), dma((count, 3)),
-            dma((count,)), dma((count,)), dma((count, 3)), dma((count, 3)), dma((count,)),
+            dma((count,)), dma((count,)), dma((count, 3)), dma((count, 3)),
+            *(buffer for u in range(count) for buffer in unit_buffers(u) if buffer is not None),
         ],
         compiler_params=pltpu.CompilerParams(
             collective_id=2, has_side_effects=True, vmem_limit_bytes=63 * 2**20
         ),
         name="reduce_grads",
-    )(g_d, g_g, g_u, g_o, g_in, g_s)
+    )(
+        g_d.reshape(2, 4, 224, 1536),
+        g_g.reshape(2, 4, 4, 48, 1792),
+        g_u.reshape(2, 4, 4, 48, 1792),
+        g_o.reshape(2, 4, 48, 1536),
+        g_in.reshape(2, 4, 4, 48, 1152),
+        g_s.reshape(2, 4, 4, 8, 128),
+    )
 
 
 def local(inputs, cotangent, w_in, w_out, w_gate, w_up, w_down, kernel, gain_mix, gain_ffn):
@@ -930,14 +972,7 @@
     y, gx, g_in, g_o, g_g, g_u, g_d, g_s = run_blocks(
         inputs.reshape(128, 1536), cotangent.reshape(128, 1536), small, w_in[0], w_out[0], w_gate[0], w_up[0], w_down[0]
     )
-    o_d, o_g, o_u, o_o, o_in, o_s = reduce(
-        g_d.reshape(8, 224, 1536),
-        g_g.reshape(8, 4, 48, 1792),
-        g_u.reshape(8, 4, 48, 1792),
-        g_o.reshape(8, 48, 1536),
-        g_in.reshape(8, 4, 48, 1152),
-        g_s.reshape(8, 4, 8, 128),
-    )
+    o_d, o_g, o_u, o_o, o_in, o_s = reduce(g_d, g_g, g_u, g_o, g_in, g_s)
     return (
         y.reshape(1, 2, 64, 1536),
         gx.reshape(1, 2, 64, 1536),

time: 444 us -> 396 us (0.89)
  Pallas kernels: 430 us -> 382 us
    pallas_call x1, Pallas kernels: 306 us -> 270 us  [run_blocks(): pl.pallas_call(blocks_kernel, out_shape=(shape((128, 1536), BF16), shape(...]
    pallas_call x1, Pallas kernels: 124 us -> 112 us  [reduce(): pl.pallas_call(reduce_kernel, out_shape=(shape((216, 1536), F32), shape((...]
where the time goes in v4:
time: 396 us; the launch traced here: 395 us
  Pallas kernels  382 us (96%)
  local copies, waits for them, and re-layouts  11.5 us (3%)
    pallas_call x1, Pallas kernels, run_blocks(): pl.pallas_call(blocks_kernel, out_shape=(shape((128, 1536), BF16), shape(...  270 us
    pallas_call x1, Pallas kernels, reduce(): pl.pallas_call(reduce_kernel, out_shape=(shape((216, 1536), F32), shape((...  112 us
    unnamed x20, local copies, waits for them, and re-layouts  9.55 us

profile of v4, /device:TPU:2, one launch (start us, length us, event | category | flops | bytes accessed | tf_op | source)
XLA Modules:
  0.0 395.5 jit_solution(6828918026227612918)
XLA Ops:
  0.6 1.3 fusion.9.small
  2.0 270.0 %two_blocks.1 = (bf16[128,1536]{1,0:T(8,128)(2,1)}, f32[128,1536]{1,0:T(8,128)}, bf16[1536,1152]{1,0:T(8,128)(2,1)}, bf16[384,1536]{1,0:T(8,128)(2,1)}, bf16[153...) custom-call(bf16[128,1536]{1,0:T(8,128)(2,1)} %bitcast.37, ...), custom_call_target="tpu_custom_call" | custom-call | tf_op jit(solution)/shard_map/two_blocks/pallas_call | solution.py:680
  272.0 0.0 copy-start.4
  272.0 111.9 %reduce_grads.1 = (f32[216,1536]{1,0:T(8,128)}, f32[48,6912]{1,0:T(8,128)}, f32[48,6912]{1,0:T(8,128)}, f32[48,1536]{1,0:T(8,128)}, f32[48,4608]{1,0:T(8,128)}, /*index=5*/f32[8,128]{1,0:T(8,128)}) custom-call(bf16[2,4,224,1536]{3,2,1,0:T(8,128)(2,1)} %bitcast.25, bf16[2,4,4,48,1792]{4,3,2,1,0:T(8,128)(2,1)} %bitcast.23, ...), custom_call_target="tpu_custom_call" | custom-call | tf_op jit(solution)/shard_map/reduce_grads/pallas_call | solution.py:934
  383.9 0.0 copy-start.3
  383.9 1.3 fusion.10
  385.2 0.7 slice_bitcast_fusion
  385.9 0.6 copy.20
  386.5 1.8 copy.28
  388.2 0.0 copy-done.4
  388.2 0.0 copy-start.5
  388.2 0.9 copy.29
  389.1 0.0 copy-done.3
  389.1 0.0 copy-start.2
  389.1 0.9 copy.30
  390.0 0.0 copy-done.5
  390.0 0.7 copy.31
  390.8 0.0 copy-done.2
  390.8 0.0 copy-start.1
  390.8 1.1 copy.32
  391.9 0.7 copy-done.1
  392.6 0.0 copy-start
  392.6 1.1 copy.33
  393.7 0.7 copy-done
  394.4 1.1 copy.34
Async XLA Ops:
  272.0 116.2 %copy-start.4 = (f32[128,1536]{1,0:T(8,128)S(1)}, f32[128,1536]{1,0:T(8,128)}, u32[]{:S(2)}) copy-start(f32[128,1536]{1,0:T(8,128)} %get-tuple-element.25) | copy-start | bytes 2359300
  383.9 5.2 %copy-start.3 = (f32[48,4608]{1,0:T(8,128)S(1)}, f32[48,4608]{1,0:T(8,128)}, u32[]{:S(2)}) copy-start(f32[48,4608]{1,0:T(8,128)} %get-tuple-element.32) | copy-start | bytes 2654212
  388.2 1.8 copy-start.5
  389.1 1.7 copy-start.2
  390.8 1.8 copy-start.1
  392.6 1.8 copy-start

commit v5 on v4

--- a/solution.py
+++ b/solution.py
@@ -16,40 +16,43 @@
 ORDER = (1, 3, 2)
 
 GATHER_UNITS = (
-    (2, 0, 1536), (0, 0, 128), (1, 0, 640), (1, 640, 512),
-    (3, 0, 640), (4, 0, 640), (3, 640, 640), (4, 640, 640), (3, 1280, 512), (4, 1280, 512),
-    (5, 0, 80), (5, 80, 80), (5, 160, 64),
+    (2, 0, 1536),
+    (0, 0, 128),
+    (1, 0, 640),
+    (1, 640, 512),
+    (5, 0, 80),
+    (3, 0, 640),
+    (4, 0, 640),
+    (4, 640, 512),
+    (4, 1152, 640),
+    (3, 640, 640),
+    (3, 1280, 512),
+    (5, 80, 80),
+    (5, 160, 64),
 )
 GATHER_LAGS = (3, 5)
-FORWARD_AT = ((8, 9, 12, 15), (11, 13, 15, 17))
-GO_AFTER = 15
+FORWARD_AT = ((9, 9, 10, 10, 11, 12, 16, 16), (11, 12, 13, 14, 16, 17, 17, 17))
+GO_AFTER = 12
 REDUCE_UNITS = (
-    (0, 0, 32, 0),
-    (2, 0, 128, 2),
-    (0, 32, 48, 1),
-    (2, 128, 128, 2),
-    (4, 0, 256, 0),
-    (1, 0, 768, 0),
-    (2, 256, 640, 0),
-    (4, 256, 128, 0),
-    (4, 384, 128, 1),
-    (5, 0, 128, 0),
-    (4, 512, 256, 2),
-    (1, 768, 512, 0),
-    (1, 1280, 512, 0),
-    (2, 896, 128, 0),
-    (4, 768, 128, 2),
-    (4, 896, 256, 2),
-    (2, 1024, 640, 0),
-    (2, 1664, 128, 1),
-    (0, 80, 16, 2),
+    (1, 0, 768, 1),
+    (1, 768, 256, 2),
+    (4, 0, 1024, 0),
+    (2, 0, 1024, 2),
+    (0, 0, 16, 2),
+    (1, 1024, 128, 1),
+    (2, 1024, 512, 0),
+    (1, 1152, 256, 2),
+    (0, 16, 48, 0),
+    (4, 1024, 128, 0),
+    (5, 0, 128, 2),
+    (0, 64, 80, 0),
+    (0, 144, 16, 2),
+    (1, 1408, 384, 2),
+    (2, 1536, 256, 2),
+    (0, 160, 64, 0),
     (3, 0, 1536, 0),
-    (0, 96, 48, 0),
-    (0, 144, 16, 2),
-    (0, 160, 32, 0),
-    (0, 192, 32, 0),
 )
-REDUCE_LAGS = (0, 21, 27, 35, 41)
+REDUCE_LAGS = (0, 11, 16, 20, 24, 29)
 
 
 def place():
@@ -408,8 +411,17 @@
 
         loop(2, body)
 
+    def sent_before(mb, first, second):
+        @pl.when(section == 0)
+        def _():
+            sum_sent(first, mb)
+
+        @pl.when(section == 1)
+        def _():
+            sum_sent(second, mb)
+
     def down(mb):
-        sum_sent(0, mb)
+        sent_before(mb, 0, 3)
         sum_over_z(1, mb, lambda at: dot_nn(hd[mb_rows[mb], :], wd[:, at]))
 
     def finish(mb):
@@ -440,31 +452,27 @@
         stage(0)
         stage(1)
 
-    def forward_1():
+    def begin_forward():
         need(0)
         take_input()
         need(1)
         wait_x()
-        both(project)
-
-    def forward_2():
+        project(0)
+
+    def begin_mix():
         need(2)
-        both(mix)
-
-    def forward_3():
-        both(middle)
-
-    def forward_4():
+        mix(0)
+
+    def begin_gate():
         need(3)
         need(4)
         free_cuts()
-        both(gate)
-
-    def forward_5():
-        need(5)
-        both(down)
-
-    segments = (forward_1, forward_2, forward_3, forward_4)
+        gate(0)
+
+    segments = (
+        begin_forward, lambda: project(1), begin_mix, lambda: mix(1),
+        lambda: middle(0), lambda: middle(1), begin_gate, lambda: gate(1),
+    )
     count = len(GATHER_UNITS)
     lag_p, lag_q = GATHER_LAGS
     for step in range(count + lag_q):
@@ -486,11 +494,12 @@
             if step == FORWARD_AT[1][turn]:
                 pl.when(section == 1)(segment)
 
-    forward_5()
-    both(finish)
-    for copy in sent:
-        if not any(copy is z_copies[n, r] for n in (1, 3, 4) for r in ORDER):
-            copy.wait_send()
+    need(5)
+
+    @pl.when(section == 0)
+    def _():
+        both(down)
+        both(finish)
 
     ggain[...] = jnp.zeros((2, 1536), F32)
 
@@ -512,7 +521,7 @@
         loop(2, body)
 
     def back_ffn(mb):
-        sum_sent(1, mb)
+        sent_before(mb, 1, 0)
         sum_over_z(2, mb, lambda at: dot_nt(dg[mb_rows[mb], :], wg[at, :]) + dot_nt(du[mb_rows[mb], :], wu[at, :]))
 
     def back_middle(mb):
@@ -602,26 +611,38 @@
         loop(target.shape[0] // width, body)
         stores[n].start()
 
+    def grad_taps():
+        for k in range(3):
+            total = jnp.zeros((1, 384), F32)
+            for mb in range(2):
+                for zc in range(4):
+                    t0 = 8 + 64 * zc - k
+                    products = dce[mb, 64 * zc : 64 * zc + 64, :] * ge[mb, t0 : t0 + 64, :]
+                    total = total + jnp.sum(products, axis=0, keepdims=True)
+            gtap[k : k + 1, :] = total
+
     both(take_gradient)
     both(lambda mb: (back_hidden(mb), back_ffn(mb)))
-    grad(4, 896, hd, ea)
+    for copy in sent:
+        if not any(copy is z_copies[n, r] for n in (1, 3, 4) for r in ORDER):
+            copy.wait_send()
     back_middle(0)
     grad(2, 768, n2, dg)
     back_middle(1)
     grad(3, 768, n2, du)
     both(back_mix)
+    both(lambda mb: (back_conv(mb), back_in(mb)))
     grad(1, 384, mx, fa)
-    for k in range(3):
-        total = jnp.zeros((1, 384), F32)
-        for mb in range(2):
-            for zc in range(4):
-                t0 = 8 + 64 * zc - k
-                products = dce[mb, 64 * zc : 64 * zc + 64, :] * ge[mb, t0 : t0 + 64, :]
-                total = total + jnp.sum(products, axis=0, keepdims=True)
-        gtap[k : k + 1, :] = total
-    both(lambda mb: (back_conv(mb), back_in(mb)))
+    grad_taps()
+    for mb in range(2):
+        back_input(mb)
+        pl.when(section == 1)(functools.partial(down, mb))
+    grad(4, 896, hd, ea)
     grad(0, 768, xn, dp)
-    both(back_input)
+
+    @pl.when(section == 1)
+    def _():
+        both(finish)
 
     gs_ref[...] = jnp.zeros((256, 128), F32)
     for q in range(8):
@@ -648,7 +669,7 @@
         def _():
             halo_before[mb].wait_send()
 
-        sum_sent(3, mb)
+        sent_before(mb, 3, 1)
         for copies in (x_all, n_all, e_all, f_all):
             for copy in copies[mb]:
                 copy.wait_send()
@@ -729,9 +750,9 @@
     whole, part = unit_shape(u)
     dtype = F32 if n == 5 else BF16
     shapes = {
-        0: ((4, *part), (4, *part), (3, *whole)),
-        1: (None, (4, *whole), (3, *whole)),
-        2: (None, whole, (3, 2, *whole)),
+        0: ((4, *part), (4, *part), (2, *part), (2, *whole)),
+        1: (None, (4, *whole), (2, *part), (2, *whole)),
+        2: (None, whole, (2, 2, *part), (2, 2, *whole)),
     }[mode]
     shapes += (whole, whole if n in (1, 2, 4, 5) else None)
     return [None if shape is None else pltpu.VMEM(shape, dtype) for shape in shapes]
@@ -749,13 +770,14 @@
     held = (v_d, v_g, v_u, v_o, v_in, v_s)
     landing = (l_d, l_g, l_u, o_o, l_in, l_s)
     loads = [pltpu.make_async_copy(src, held[n], load.at[n]) for n, src in enumerate((g_d, g_g, g_u, g_o, g_in, g_s))]
-    for copy in loads:
-        copy.start()
+    first_use = list(dict.fromkeys(unit[0] for unit in REDUCE_UNITS))
+    for n in first_use[:2]:
+        loads[n].start()
     barrier_all([partner, twin, *zs.values(), *ys.values()])
     count = len(REDUCE_UNITS)
     left = list(buffers)
     slots = [[None if shape is None else left.pop(0) for shape in unit_buffers(u)] for u in range(count)]
-    from_twin, from_partner, from_y, theirs, ended = zip(*slots)
+    from_twin, from_partner, halves_y, from_y, theirs, ended = zip(*slots)
     near, far = xh, 1 - xh
     sent, copies = [], {}
 
@@ -800,10 +822,37 @@
 
         loop(4 * number, body)
 
-    def send_y(u, source):
-        for r in ORDER:
-            dst = from_y[u].at[r - 1]
-            begin(("y", u, r), remote(source(lax.rem(y + r, 4)), dst, y_send.at[u, r - 1], y_recv.at[u, r - 1], ys[r]))
+    def sides(u):
+        return (0, 1) if REDUCE_UNITS[u][3] == 2 else (near,)
+
+    def lead(u, row):
+        return (slice(None) if REDUCE_UNITS[u][3] == 2 else near, row)
+
+    def of_side(u, k, side):
+        return (k, side) if REDUCE_UNITS[u][3] == 2 else (k,)
+
+    def send_halves(u):
+        ref = held[REDUCE_UNITS[u][0]]
+        for k, r in enumerate((1, 3)):
+            src = ref.at[*lead(u, lax.rem(y + 2, 4)), *tail(u, k)]
+            begin(("half", u, k), remote(src, halves_y[u].at[k], y_send.at[u, k], y_recv.at[u, k], ys[r]))
+
+    def send_wholes(u):
+        ref = held[REDUCE_UNITS[u][0]]
+        for k, r in enumerate((1, 3)):
+            row = lax.rem(y + r, 4)
+            copies["half", u, k].wait_recv()
+            number, at = blocks(u, k)
+            for side in sides(u):
+
+                def body(i):
+                    here, there = at(i)
+                    got = halves_y[u][*of_side(u, k, side), *there]
+                    ref[side, row, *here] = ref[side, row, *here] + got
+
+                loop(number, body)
+            src = ref.at[*lead(u, row), *tail(u)]
+            begin(("y", u, k), remote(src, from_y[u].at[k], y_send.at[u, 2 + k], y_recv.at[u, 2 + k], ys[r]))
 
     def send_p(u, src):
         begin(("p", u), remote(src, from_partner[u], p_send.at[u], p_recv.at[u], partner))
@@ -812,22 +861,21 @@
         src = held[REDUCE_UNITS[u][0]].at[near, y, *tail(u)]
         begin(("t", u), remote(src, theirs[u], t_send.at[u], t_recv.at[u], twin))
 
-    def sum_y(u, sides):
-        for r in ORDER:
-            copies["y", u, r].wait_recv()
+    def sum_y(u):
+        for k in range(2):
+            copies["y", u, k].wait_recv()
         ref = held[REDUCE_UNITS[u][0]]
         number, at = blocks(u)
-
-        def body(k):
-            side = near if len(sides) == 1 else k // number
-            here, there = at(lax.rem(k, number))
-            total = ref[side, y, *here].astype(F32)
-            for r in range(3):
-                got = from_y[u][r, *there] if len(sides) == 1 else from_y[u][r, side, *there]
-                total = total + got.astype(F32)
-            ref[side, y, *here] = total.astype(ref.dtype)
-
-        loop(len(sides) * number, body)
+        for side in sides(u):
+
+            def body(i):
+                here, there = at(i)
+                total = ref[side, y, *here].astype(F32)
+                for k in range(2):
+                    total = total + from_y[u][*of_side(u, k, side), *there].astype(F32)
+                ref[side, y, *here] = total.astype(ref.dtype)
+
+            loop(number, body)
 
     ready = set()
 
@@ -836,13 +884,15 @@
         if n not in ready:
             ready.add(n)
             loads[n].wait()
+            for following in first_use[len(ready) + 1 : len(ready) + 2]:
+                loads[following].start()
         if mode == 0:
             src = held[n].at[far, :, *tail(u, 1 - xl)]
             begin(("q", u), remote(src, from_twin[u], q_send.at[u], q_recv.at[u], twin))
         elif mode == 1:
             send_p(u, held[n].at[far, :, *tail(u)])
         else:
-            send_y(u, lambda row: held[n].at[:, row, *tail(u)])
+            send_halves(u)
 
     def stage_1(u):
         n, first, size, mode = REDUCE_UNITS[u]
@@ -851,13 +901,22 @@
             add_rows(u, far, xl, from_twin[u])
             send_p(u, held[n].at[far, :, *tail(u, xl)])
         elif mode == 2:
-            sum_y(u, (0, 1))
-            send_p(u, held[n].at[far, y, *tail(u)])
+            send_wholes(u)
 
     def stage_2(u):
         n, first, size, mode = REDUCE_UNITS[u]
-        copies["p", u].wait_recv()
         if mode == 2:
+            sum_y(u)
+            send_p(u, held[n].at[far, y, *tail(u)])
+        else:
+            copies["p", u].wait_recv()
+            add_rows(u, near, 1 - xl if mode == 0 else None, from_partner[u])
+            send_halves(u)
+
+    def stage_3(u):
+        n, first, size, mode = REDUCE_UNITS[u]
+        if mode == 2:
+            copies["p", u].wait_recv()
             number, at = blocks(u)
 
             def body(i):
@@ -867,15 +926,14 @@
             loop(number, body)
             send_twin(u)
         else:
-            add_rows(u, near, 1 - xl if mode == 0 else None, from_partner[u])
-            send_y(u, lambda row: held[n].at[near, row, *tail(u)])
-
-    def stage_3(u):
+            send_wholes(u)
+
+    def stage_4(u):
         if REDUCE_UNITS[u][3] != 2:
-            sum_y(u, (0,))
+            sum_y(u)
             send_twin(u)
 
-    def stage_4(u):
+    def stage_5(u):
         n, first, size, mode = REDUCE_UNITS[u]
         copies["t", u].wait_recv()
         number, at = blocks(u)
@@ -895,7 +953,7 @@
                 begin(("z", u, r), remote(src, dst, z_send.at[u, r - 1], z_recv.at[u, r - 1], zs[r]))
             landing[n][z, :, first : first + size] = ended[u][z]
 
-    stages = (stage_0, stage_1, stage_2, stage_3, stage_4)
+    stages = (stage_0, stage_1, stage_2, stage_3, stage_4, stage_5)
     for step in range(count + REDUCE_LAGS[-1]):
         for lag, stage in zip(REDUCE_LAGS, stages):
             if 0 <= step - lag < count:
@@ -948,7 +1006,7 @@
             vm((2, 4, 48, 1536), BF16), vm((2, 4, 4, 48, 1152), BF16), vm((2, 4, 4, 8, 128), F32),
             vm((224, 1536), F32), vm((4, 48, 1792), BF16), vm((4, 48, 1792), BF16), vm((4, 48, 1152), BF16),
             vm((4, 8, 128), F32),
-            dma((6,)), dma((count,)), dma((count,)), dma((count,)), dma((count,)), dma((count, 3)), dma((count, 3)),
+            dma((6,)), dma((count,)), dma((count,)), dma((count,)), dma((count,)), dma((count, 4)), dma((count, 4)),
             dma((count,)), dma((count,)), dma((count, 3)), dma((count, 3)),
             *(buffer for u in range(count) for buffer in unit_buffers(u) if buffer is not None),
         ],

time: 396 us -> 369 us (0.932)
  Pallas kernels: 382 us -> 354 us
    pallas_call x1, Pallas kernels: 112 us -> 96.2 us  [reduce(): pl.pallas_call(reduce_kernel, out_shape=(shape((216, 1536), F32), shape((...]
    pallas_call x1, Pallas kernels: 270 us -> 258 us  [run_blocks(): pl.pallas_call(blocks_kernel, out_shape=(shape((128, 1536), BF16), shape(...]
where the time goes in v5:
time: 369 us; the launch traced here: 368 us
  Pallas kernels  354 us (96%)
  local copies, waits for them, and re-layouts  11.5 us (3%)
    pallas_call x1, Pallas kernels, run_blocks(): pl.pallas_call(blocks_kernel, out_shape=(shape((128, 1536), BF16), shape(...  258 us
    pallas_call x1, Pallas kernels, reduce(): pl.pallas_call(reduce_kernel, out_shape=(shape((216, 1536), F32), shape((...  96.2 us
    unnamed x20, local copies, waits for them, and re-layouts  9.55 us

profile of v5, /device:TPU:2, one launch (start us, length us, event | category | flops | bytes accessed | tf_op | source)
XLA Modules:
  0.0 367.6 jit_solution(9749371230386675)
XLA Ops:
  0.6 1.3 fusion.9.small
  2.0 257.8 %two_blocks.1 = (bf16[128,1536]{1,0:T(8,128)(2,1)}, f32[128,1536]{1,0:T(8,128)}, bf16[1536,1152]{1,0:T(8,128)(2,1)}, bf16[384,1536]{1,0:T(8,128)(2,1)}, bf16[153...) custom-call(bf16[128,1536]{1,0:T(8,128)(2,1)} %bitcast.37, ...), custom_call_target="tpu_custom_call" | custom-call | tf_op jit(solution)/shard_map/two_blocks/pallas_call | solution.py:701
  259.8 0.0 copy-start.4
  259.8 96.2 %reduce_grads.1 = (f32[216,1536]{1,0:T(8,128)}, f32[48,6912]{1,0:T(8,128)}, f32[48,6912]{1,0:T(8,128)}, f32[48,1536]{1,0:T(8,128)}, f32[48,4608]{1,0:T(8,128)}, /*index=5*/f32[8,128]{1,0:T(8,128)}) custom-call(bf16[2,4,224,1536]{3,2,1,0:T(8,128)(2,1)} %bitcast.25, bf16[2,4,4,48,1792]{4,3,2,1,0:T(8,128)(2,1)} %bitcast.23, ...), custom_call_target="tpu_custom_call" | custom-call | tf_op jit(solution)/shard_map/reduce_grads/pallas_call | solution.py:992
  356.0 0.0 copy-start.3
  356.0 1.3 fusion.10
  357.3 0.7 slice_bitcast_fusion
  358.0 0.6 copy.20
  358.6 1.8 copy.28
  360.3 0.0 copy-done.4
  360.3 0.0 copy-start.5
  360.3 0.9 copy.29
  361.2 0.0 copy-done.3
  361.2 0.0 copy-start.2
  361.2 0.9 copy.30
  362.1 0.0 copy-done.5
  362.1 0.7 copy.31
  362.8 0.0 copy-done.2
  362.9 0.0 copy-start.1
  362.9 1.1 copy.32
  363.9 0.7 copy-done.1
  364.7 0.0 copy-start
  364.7 1.1 copy.33
  365.8 0.7 copy-done
  366.5 1.1 copy.34
Async XLA Ops:
  259.8 100.6 %copy-start.4 = (f32[128,1536]{1,0:T(8,128)S(1)}, f32[128,1536]{1,0:T(8,128)}, u32[]{:S(2)}) copy-start(f32[128,1536]{1,0:T(8,128)} %get-tuple-element.25) | copy-start | bytes 2359300
  356.0 5.2 %copy-start.3 = (f32[48,4608]{1,0:T(8,128)S(1)}, f32[48,4608]{1,0:T(8,128)}, u32[]{:S(2)}) copy-start(f32[48,4608]{1,0:T(8,128)} %get-tuple-element.32) | copy-start | bytes 2654212
  360.3 1.8 copy-start.5
  361.2 1.7 copy-start.2
  362.9 1.8 copy-start.1
  364.7 1.8 copy-start

commit v6 on v5

--- a/solution.py
+++ b/solution.py
@@ -16,23 +16,22 @@
 ORDER = (1, 3, 2)
 
 GATHER_UNITS = (
-    (2, 0, 1536),
-    (0, 0, 128),
-    (1, 0, 640),
-    (1, 640, 512),
-    (5, 0, 80),
-    (3, 0, 640),
-    (4, 0, 640),
-    (4, 640, 512),
-    (4, 1152, 640),
-    (3, 640, 640),
-    (3, 1280, 512),
-    (5, 80, 80),
-    (5, 160, 64),
+    (0, 0, 128, 0),
+    (5, 0, 64, 0),
+    (5, 64, 32, 0),
+    (1, 0, 1152, 0),
+    (2, 0, 1536, 1),
+    (3, 0, 640, 0),
+    (4, 0, 384, 0),
+    (4, 384, 512, 0),
+    (4, 896, 768, 0),
+    (4, 1664, 128, 0),
+    (3, 640, 1152, 0),
+    (5, 96, 128, 1),
 )
-GATHER_LAGS = (3, 5)
-FORWARD_AT = ((9, 9, 10, 10, 11, 12, 16, 16), (11, 12, 13, 14, 16, 17, 17, 17))
-GO_AFTER = 12
+GATHER_LAGS = (1, 2, 4)
+FORWARD_AT = ((13, 14, 14, 15, 15, 15, 15, 15), (11, 12, 12, 14, 14, 15, 15, 15))
+GO_AFTER = 11
 REDUCE_UNITS = (
     (1, 0, 768, 1),
     (1, 768, 256, 2),
@@ -111,7 +110,7 @@
     xa, xn, n2, ea, fa, part, rr, proj, ge, dce, cv, ha, hb, mx, by_gate, by_up, hd, dg, du,
     mid, dmid, dp, g0, win, wout, wg, wu, wd, sm, gains, taps, gtap, ggain,
     store, a_send, a_recv, s_send, s_recv, h_send, h_recv, c_send, c_recv,
-    z_send, z_recv, y_send, y_recv, p_send, p_recv, q_send, q_recv, go,
+    z_send, z_recv, y_send, y_recv, f_send, f_recv, p_send, p_recv, q_send, q_recv, go,
 ):
     section, xl, xh, y, z = place()
     partner, twin, zs, ys = plane_peers()
@@ -222,7 +221,7 @@
     push_z(4)
 
     def piece(u, q):
-        n, first, size = GATHER_UNITS[u]
+        n, first, size, way = GATHER_UNITS[u]
         if n == 5:
             return wd.at[pl.ds(pl.multiple_of(q * 224 + first, 16), size)]
         if n == 2:
@@ -230,7 +229,7 @@
         return weights[n].at[pl.ds(rows_q(n, q), rows[n]), pl.ds(first, size)]
 
     def half(u, q, h):
-        n, first, size = GATHER_UNITS[u]
+        n, first, size, way = GATHER_UNITS[u]
         if n in (2, 5):
             left = pl.ds(pl.multiple_of(h * 768, 128), 768)
             if n == 5:
@@ -241,7 +240,36 @@
             pl.ds(pl.multiple_of(q * rows[n] + h * part_rows, 8 if n == 0 else 16), part_rows), pl.ds(first, size)
         ]
 
-    y_copies, p_copies, q_copies, started = {}, {}, {}, set()
+    y_copies, f_copies, p_copies, q_copies, started = {}, {}, {}, {}, set()
+
+    def go_on(table, key, copy):
+        copy.start()
+        table[key] = copy
+        sent.append(copy)
+
+    def push_y(u, far):
+        src = piece(u, (1 - xh if far else xh) * 4 + y)
+        for k, r in enumerate((1, 3)):
+            at = 2 * far + k
+            go_on(y_copies, (u, at), remote(src, src, y_send.at[u, at], y_recv.at[u, at], ys[r]))
+
+    def pass_y(u, far):
+        for k, r in enumerate((1, 3)):
+            at = 2 * far + k
+            y_copies[u, at].wait_recv()
+            src = half(u, (1 - xh if far else xh) * 4 + lax.rem(y + 4 - r, 4), k)
+            go_on(f_copies, (u, at), remote(src, src, f_send.at[u, at], f_recv.at[u, at], ys[r]))
+            if GATHER_UNITS[u][3] == 0:
+                push_p(u, r)
+
+    def push_p(u, r):
+        src = half(u, xh * 4 + lax.rem(y + 4 - r, 4), xl)
+        go_on(p_copies, (u, r), remote(src, src, p_send.at[u, r], p_recv.at[u, r], partner))
+
+    def pass_q(u, r):
+        p_copies[u, r].wait_recv()
+        src = half(u, (1 - xh) * 4 + lax.rem(y + 4 - r, 4), 1 - xl)
+        go_on(q_copies, (u, r), remote(src, src, q_send.at[u, r], q_recv.at[u, r], twin))
 
     def stage_y(u):
         n = GATHER_UNITS[u][0]
@@ -250,38 +278,36 @@
             if n not in (2, 5):
                 for r in ORDER:
                     z_copies[n, r].wait_recv()
-        for r in ORDER:
-            src = piece(u, me)
-            copy = remote(src, src, y_send.at[u, r - 1], y_recv.at[u, r - 1], ys[r])
-            copy.start()
-            y_copies[u, r] = copy
-            sent.append(copy)
         push_p(u, 0)
-
-    def push_p(u, r):
-        src = half(u, xh * 4 + lax.rem(y + 4 - r, 4), xl)
-        copy = remote(src, src, p_send.at[u, r], p_recv.at[u, r], partner)
-        copy.start()
-        p_copies[u, r] = copy
-        sent.append(copy)
+        push_y(u, 0)
 
     def stage_p(u):
-        for r in ORDER:
-            y_copies[u, r].wait_recv()
-            push_p(u, r)
+        if GATHER_UNITS[u][3]:
+            pass_q(u, 0)
+        pass_y(u, 0)
+
+    def stage_f(u):
+        if GATHER_UNITS[u][3]:
+            q_copies[u, 0].wait_recv()
+            push_y(u, 1)
+        else:
+            for k in range(2):
+                f_copies[u, k].wait_recv()
+            push_p(u, 2)
 
     def stage_q(u):
-        for r in (0, *ORDER):
-            p_copies[u, r].wait_recv()
-            src = half(u, (1 - xh) * 4 + lax.rem(y + 4 - r, 4), 1 - xl)
-            copy = remote(src, src, q_send.at[u, r], q_recv.at[u, r], twin)
-            copy.start()
-            q_copies[u, r] = copy
-            sent.append(copy)
+        if GATHER_UNITS[u][3]:
+            pass_y(u, 1)
+        else:
+            for r in (0, *ORDER):
+                pass_q(u, r)
 
     def need(n):
         for u, unit in enumerate(GATHER_UNITS):
-            if unit[0] == n:
+            if unit[0] == n and unit[3]:
+                for at in range(4):
+                    f_copies[u, at].wait_recv()
+            elif unit[0] == n:
                 for r in (0, *ORDER):
                     q_copies[u, r].wait_recv()
 
@@ -474,12 +500,14 @@
         lambda: middle(0), lambda: middle(1), begin_gate, lambda: gate(1),
     )
     count = len(GATHER_UNITS)
-    lag_p, lag_q = GATHER_LAGS
+    lag_p, lag_f, lag_q = GATHER_LAGS
     for step in range(count + lag_q):
         if step < count:
             stage_y(step)
         if 0 <= step - lag_p < count:
             stage_p(step - lag_p)
+        if 0 <= step - lag_f < count:
+            stage_f(step - lag_f)
         if step == GO_AFTER:
 
             @pl.when(section == 0)
@@ -725,8 +753,8 @@
             vm((2, 1536), F32),
             dma((5,)), dma((4, 2, 3)), dma((4, 2, 3)), dma((4, 2, 3, 3)), dma((4, 2, 3, 3)),
             dma((2, 2)), dma((2, 2)), dma((2, 2)), dma((2, 2)),
-            dma((5, 3)), dma((5, 3)), dma((count, 3)), dma((count, 3)), dma((count, 4)), dma((count, 4)),
-            dma((count, 4)), dma((count, 4)), pltpu.SemaphoreType.REGULAR,
+            dma((5, 3)), dma((5, 3)), dma((count, 4)), dma((count, 4)), dma((count, 4)), dma((count, 4)),
+            dma((count, 4)), dma((count, 4)), dma((count, 4)), dma((count, 4)), pltpu.SemaphoreType.REGULAR,
         ],
         compiler_params=pltpu.CompilerParams(
             collective_id=1, has_side_effects=True, vmem_limit_bytes=63 * 2**20

time: 369 us -> 365 us (0.989)
    pallas_call x1, Pallas kernels: 258 us -> 250 us  [run_blocks(): pl.pallas_call(blocks_kernel, out_shape=(shape((128, 1536), BF16), shape(...]
    pallas_call x1, Pallas kernels: 96.2 us -> 101 us  [reduce(): pl.pallas_call(reduce_kernel, out_shape=(shape((216, 1536), F32), shape((...]
where the time goes in v6:
time: 365 us
  Pallas kernels  351 us (96%)
  local copies, waits for them, and re-layouts  11.5 us (3%)
    pallas_call x1, Pallas kernels, run_blocks(): pl.pallas_call(blocks_kernel, out_shape=(shape((128, 1536), BF16), shape(...  250 us
    pallas_call x1, Pallas kernels, reduce(): pl.pallas_call(reduce_kernel, out_shape=(shape((216, 1536), F32), shape((...  101 us
    unnamed x20, local copies, waits for them, and re-layouts  9.55 us

profile of v6, /device:TPU:2, one launch (start us, length us, event | category | flops | bytes accessed | tf_op | source)
XLA Modules:
  0.0 364.6 jit_solution(15810831900249404630)
XLA Ops:
  0.6 1.3 fusion.9.small
  2.0 250.1 %two_blocks.1 = (bf16[128,1536]{1,0:T(8,128)(2,1)}, f32[128,1536]{1,0:T(8,128)}, bf16[1536,1152]{1,0:T(8,128)(2,1)}, bf16[384,1536]{1,0:T(8,128)(2,1)}, bf16[153...) custom-call(bf16[128,1536]{1,0:T(8,128)(2,1)} %bitcast.37, ...), custom_call_target="tpu_custom_call" | custom-call | tf_op jit(solution)/shard_map/two_blocks/pallas_call | solution.py:729
  252.0 0.0 copy-start.4
  252.0 101.0 %reduce_grads.1 = (f32[216,1536]{1,0:T(8,128)}, f32[48,6912]{1,0:T(8,128)}, f32[48,6912]{1,0:T(8,128)}, f32[48,1536]{1,0:T(8,128)}, f32[48,4608]{1,0:T(8,128)}, /*index=5*/f32[8,128]{1,0:T(8,128)}) custom-call(bf16[2,4,224,1536]{3,2,1,0:T(8,128)(2,1)} %bitcast.25, bf16[2,4,4,48,1792]{4,3,2,1,0:T(8,128)(2,1)} %bitcast.23, ...), custom_call_target="tpu_custom_call" | custom-call | tf_op jit(solution)/shard_map/reduce_grads/pallas_call | solution.py:1020
  353.1 0.0 copy-start.3
  353.1 1.3 fusion.10
  354.4 0.7 slice_bitcast_fusion
  355.0 0.6 copy.20
  355.6 1.8 copy.28
  357.4 0.0 copy-done.4
  357.4 0.0 copy-start.5
  357.4 0.9 copy.29
  358.3 0.0 copy-done.3
  358.3 0.0 copy-start.2
  358.3 0.9 copy.30
  359.2 0.0 copy-done.5
  359.2 0.7 copy.31
  359.9 0.0 copy-done.2
  359.9 0.0 copy-start.1
  359.9 1.1 copy.32
  361.0 0.7 copy-done.1
  361.7 0.0 copy-start
  361.7 1.1 copy.33
  362.8 0.7 copy-done
  363.5 1.1 copy.34
Async XLA Ops:
  252.0 105.3 %copy-start.4 = (f32[128,1536]{1,0:T(8,128)S(1)}, f32[128,1536]{1,0:T(8,128)}, u32[]{:S(2)}) copy-start(f32[128,1536]{1,0:T(8,128)} %get-tuple-element.25) | copy-start | bytes 2359300
  353.1 5.2 %copy-start.3 = (f32[48,4608]{1,0:T(8,128)S(1)}, f32[48,4608]{1,0:T(8,128)}, u32[]{:S(2)}) copy-start(f32[48,4608]{1,0:T(8,128)} %get-tuple-element.32) | copy-start | bytes 2654212
  357.4 1.8 copy-start.5
  358.3 1.7 copy-start.2
  359.9 1.8 copy-start.1
  361.7 1.8 copy-start

commit v7 on v6

--- a/solution.py
+++ b/solution.py
@@ -209,16 +209,16 @@
             xa[own_rows(mb), :] = x_ref[mb * 64 : mb * 64 + 64, :]
             begin(x_all[mb])
 
+    cut_ffn(w_gate, hd)
+    push_z(3)
+    cut_ffn(w_up, dg)
+    push_z(4)
+
     @pl.when(section == 1)
     def _():
         for mb in range(2):
             ea[own_rows(mb), :] = cot_ref[mb * 64 : mb * 64 + 64, :]
             begin(e_all[mb])
-
-    cut_ffn(w_gate, hd)
-    push_z(3)
-    cut_ffn(w_up, dg)
-    push_z(4)
 
     def piece(u, q):
         n, first, size, way = GATHER_UNITS[u]

time: 365 us -> 365 us (level)
  no operation moved by 1% of the time
where the time goes in v7:
time: 365 us
  Pallas kernels  351 us (96%)
  local copies, waits for them, and re-layouts  11.5 us (3%)
    pallas_call x1, Pallas kernels, run_blocks(): pl.pallas_call(blocks_kernel, out_shape=(shape((128, 1536), BF16), shape(...  250 us
    pallas_call x1, Pallas kernels, reduce(): pl.pallas_call(reduce_kernel, out_shape=(shape((216, 1536), F32), shape((...  101 us
    unnamed x20, local copies, waits for them, and re-layouts  9.55 us

profile of v7, /device:TPU:2, one launch (start us, length us, event | category | flops | bytes accessed | tf_op | source)
XLA Modules:
  0.0 364.6 jit_solution(13859178314992420133)
XLA Ops:
  0.6 1.3 fusion.9.small
  2.0 250.1 %two_blocks.1 = (bf16[128,1536]{1,0:T(8,128)(2,1)}, f32[128,1536]{1,0:T(8,128)}, bf16[1536,1152]{1,0:T(8,128)(2,1)}, bf16[384,1536]{1,0:T(8,128)(2,1)}, bf16[153...) custom-call(bf16[128,1536]{1,0:T(8,128)(2,1)} %bitcast.37, ...), custom_call_target="tpu_custom_call" | custom-call | tf_op jit(solution)/shard_map/two_blocks/pallas_call | solution.py:729
  252.0 0.0 copy-start.4
  252.0 101.0 %reduce_grads.1 = (f32[216,1536]{1,0:T(8,128)}, f32[48,6912]{1,0:T(8,128)}, f32[48,6912]{1,0:T(8,128)}, f32[48,1536]{1,0:T(8,128)}, f32[48,4608]{1,0:T(8,128)}, /*index=5*/f32[8,128]{1,0:T(8,128)}) custom-call(bf16[2,4,224,1536]{3,2,1,0:T(8,128)(2,1)} %bitcast.25, bf16[2,4,4,48,1792]{4,3,2,1,0:T(8,128)(2,1)} %bitcast.23, ...), custom_call_target="tpu_custom_call" | custom-call | tf_op jit(solution)/shard_map/reduce_grads/pallas_call | solution.py:1020
  353.1 0.0 copy-start.3
  353.1 1.3 fusion.10
  354.4 0.7 slice_bitcast_fusion
  355.0 0.6 copy.20
  355.6 1.8 copy.28
  357.4 0.0 copy-done.4
  357.4 0.0 copy-start.5
  357.4 0.9 copy.29
  358.3 0.0 copy-done.3
  358.3 0.0 copy-start.2
  358.3 0.9 copy.30
  359.2 0.0 copy-done.5
  359.2 0.7 copy.31
  359.9 0.0 copy-done.2
  359.9 0.0 copy-start.1
  359.9 1.1 copy.32
  361.0 0.7 copy-done.1
  361.7 0.0 copy-start
  361.7 1.1 copy.33
  362.8 0.7 copy-done
  363.5 1.1 copy.34
Async XLA Ops:
  252.0 105.3 %copy-start.4 = (f32[128,1536]{1,0:T(8,128)S(1)}, f32[128,1536]{1,0:T(8,128)}, u32[]{:S(2)}) copy-start(f32[128,1536]{1,0:T(8,128)} %get-tuple-element.25) | copy-start | bytes 2359300
  353.1 5.2 %copy-start.3 = (f32[48,4608]{1,0:T(8,128)S(1)}, f32[48,4608]{1,0:T(8,128)}, u32[]{:S(2)}) copy-start(f32[48,4608]{1,0:T(8,128)} %get-tuple-element.32) | copy-start | bytes 2654212
  357.4 1.8 copy-start.5
  358.3 1.7 copy-start.2
  359.9 1.8 copy-start.1
  361.7 1.8 copy-start
